TPU v7x, 768 devices: a whole 4x8x12 slice. The times are simulated.
768 devices in a mesh: replica: 48 (over y_hi, z), node: 4 (over x), local: 4 (over y_lo, core).
Axes of the slice: x: 4, y: 8 (y_hi: 4, y_lo: 2; y = y_hi * 2 + y_lo), z: 12, core: 2. Of those that a mesh axis runs over, the one named last changes fastest.
Arguments:
- token_grads: bfloat16 [24576, 3840], P(('replica', 'local'), 'node'), may hold values from -6 to 6
- routes: int32 [24576, 2], P(('replica', 'local')), may hold values from 0 to 3, all different within a row; in each aligned block of 128 rows (0 to 127, 128 to 255, ...) at most 72 rows name the same one
- gates: bfloat16 [24576, 2], P(('replica', 'local')), may hold values from 0.19921875 to 1
- expert_inputs: bfloat16 [48, 4, 4, 72, 3840], P('replica', 'local', None, None, 'node'), may hold values from -6 to 6
- gate_pre: bfloat16 [48, 4, 4, 72, 1024], P('replica', 'local'), may hold values from -8 to 8
- up_pre: bfloat16 [48, 4, 4, 72, 1024], P('replica', 'local'), may hold values from -6 to 6
- w_gate: bfloat16 [4, 3840, 1024], P('local', 'node'), may hold values from -0.09375 to 0.09375
- w_up: bfloat16 [4, 3840, 1024], P('local', 'node'), may hold values from -0.09375 to 0.09375
- w_down: bfloat16 [4, 1024, 3840], P('local', None, 'node'), may hold values from -0.1875 to 0.1875
Outputs:
- input_grads: bfloat16 [24576, 3840], P(('replica', 'local'), 'node')
- gate_grads: bfloat16 [24576, 2], P(('replica', 'local'))
- gate_weight_grads: float32 [4, 4, 7680, 128], P('local', 'node', 'replica')
- up_weight_grads: float32 [4, 4, 7680, 128], P('local', 'node', 'replica')
Inputs may be any that keep to these rules, and one draw needn't show every extreme that they name: `routes`: each token names 2 different experts. Among the tokens of one device no expert is named more than 72 times, a bound that some block reaches.
All inputs are finite; a program needn't handle non-finite values.
Results may differ from a plain program's by a relative error of at most 0.022.
Values may be sent and summed in bfloat16 or wider, within the bound.
No kernel may reach another device: no remote copies, remote signals or barrier semaphores. Data moves between devices by JAX's collectives and lax.ppermute only.
A program may use at most 64 MiB of HBM per device.

v0:
```python
import jax
import jax.numpy as jnp
from jax import lax
from jax.sharding import PartitionSpec as P


def local(token_grads, routes, gates, expert_inputs, gate_pre, up_pre, w_gate, w_up, w_down):
    tok_count, top_count = routes.shape
    n_local = lax.axis_size("local")
    n_node = lax.axis_size("node")
    n_copies = lax.axis_size("replica")
    capacity = expert_inputs.shape[3]
    feat_part = token_grads.shape[1]
    hidden = gate_pre.shape[4]
    quarter = hidden // n_node
    slots = n_local * capacity
    per_feature = hidden // 128
    picks = routes.reshape(-1)
    onehot = (picks[:, None] == jnp.arange(n_local, dtype=jnp.int32)[None, :]).astype(jnp.int32)
    before = jnp.cumsum(onehot, axis=0) - onehot
    slot_of = jnp.sum(before * onehot, axis=1)
    target = picks * capacity + slot_of
    placing = (target[None, :] == jnp.arange(slots, dtype=jnp.int32)[:, None]).astype(jnp.bfloat16)
    spread = jnp.repeat(token_grads, top_count, axis=0)
    outgoing = jnp.dot(placing, spread, preferred_element_type=jnp.float32).astype(jnp.bfloat16)
    out_gates = jnp.dot(placing, gates.reshape(-1), preferred_element_type=jnp.float32).astype(
        jnp.bfloat16
    )
    arrived, arrived_gates = (
        lax.all_to_all(
            outgoing.reshape(n_local, capacity, feat_part),
            "local",
            split_axis=0,
            concat_axis=0,
            tiled=True,
        ),
        lax.all_to_all(
            out_gates.reshape(n_local, capacity), "local", split_axis=0, concat_axis=0, tiled=True
        ),
    )
    dy_rows = arrived.reshape(slots, feat_part)
    gate_rows = arrived_gates.reshape(slots, 1).astype(jnp.float32)
    down_part = w_down[0]
    raw_part = lax.dot_general(
        dy_rows, down_part, (((1,), (1,)), ((), ())), preferred_element_type=jnp.float32
    )
    gpre = gate_pre[0, 0].reshape(slots, hidden).astype(jnp.float32)
    upre = up_pre[0, 0].reshape(slots, hidden).astype(jnp.float32)
    sig = jax.nn.sigmoid(gpre)
    act = gpre * sig
    slope = sig * (1.0 + gpre * (1.0 - sig))
    dgate_part = jnp.sum(raw_part * act * upre, axis=1)
    dgate_cols = jnp.broadcast_to(dgate_part[:, None], (slots, n_node))
    raw_share, dgate_share = (
        lax.psum_scatter(
            raw_part.astype(jnp.bfloat16), "node", scatter_dimension=1, tiled=True
        ).astype(jnp.float32),
        lax.psum_scatter(
            dgate_cols.astype(jnp.bfloat16), "node", scatter_dimension=1, tiled=True
        ).astype(jnp.float32),
    )
    begin = lax.axis_index("node") * quarter
    act_share = lax.dynamic_slice_in_dim(act, begin, quarter, 1)
    up_share = lax.dynamic_slice_in_dim(upre, begin, quarter, 1)
    slope_share = lax.dynamic_slice_in_dim(slope, begin, quarter, 1)
    scaled = raw_share * gate_rows
    gate_share = (scaled * up_share * slope_share).astype(jnp.bfloat16)
    up_delta_share = (scaled * act_share).astype(jnp.bfloat16)
    gate_delta, up_delta = (
        lax.all_gather(gate_share, "node", axis=1, tiled=True),
        lax.all_gather(up_delta_share, "node", axis=1, tiled=True),
    )
    dgate = dgate_share[:, 0]
    slot_input = lax.dot_general(
        gate_delta, w_gate[0], (((1,), (1,)), ((), ())), preferred_element_type=jnp.float32
    ) + lax.dot_general(
        up_delta, w_up[0], (((1,), (1,)), ((), ())), preferred_element_type=jnp.float32
    )
    slot_input = slot_input.astype(jnp.bfloat16)
    back_rows, back_gate = (
        lax.all_to_all(
            slot_input.reshape(n_local, capacity, feat_part),
            "local",
            split_axis=0,
            concat_axis=0,
            tiled=True,
        ),
        lax.all_to_all(
            dgate.astype(jnp.bfloat16).reshape(n_local, capacity),
            "local",
            split_axis=0,
            concat_axis=0,
            tiled=True,
        ),
    )
    combining = placing.reshape(slots, tok_count, top_count).sum(axis=2)
    input_grads = lax.dot_general(
        combining,
        back_rows.reshape(slots, feat_part),
        (((0,), (0,)), ((), ())),
        preferred_element_type=jnp.float32,
    ).astype(jnp.bfloat16)
    gate_grads = (
        lax.dot_general(
            placing,
            back_gate.reshape(slots),
            (((0,), (0,)), ((), ())),
            preferred_element_type=jnp.float32,
        )
        .astype(jnp.bfloat16)
        .reshape(tok_count, top_count)
    )
    x_rows = expert_inputs[0, 0].reshape(slots, feat_part)
    share_rows = feat_part * per_feature // n_copies

    def feature_term(count, deltas):
        term = lax.dot_general(
            x_rows, deltas, (((0,), (0,)), ((), ())), preferred_element_type=jnp.float32
        )
        return term.reshape(count, 128)

    gate_sum = lax.psum_scatter(
        feature_term(lax.axis_size("replica") * share_rows, gate_delta),
        "replica",
        scatter_dimension=0,
        tiled=True,
    )
    up_sum = lax.psum_scatter(
        feature_term(lax.axis_size("replica") * share_rows, up_delta),
        "replica",
        scatter_dimension=0,
        tiled=True,
    )
    gate_weight_grads = (gate_sum / n_copies).reshape(1, 1, share_rows, 128)
    up_weight_grads = (up_sum / n_copies).reshape(1, 1, share_rows, 128)
    return (input_grads, gate_grads, gate_weight_grads, up_weight_grads)


def solution(mesh):
    placed = (
        P(("replica", "local"), "node"),
        P(("replica", "local"), None),
        P(("replica", "local"), None),
        P("replica", "local", None, None, "node"),
        P("replica", "local", None, None, None),
        P("replica", "local", None, None, None),
        P("local", "node", None),
        P("local", "node", None),
        P("local", None, "node"),
    )
    return jax.shard_map(
        local,
        mesh=mesh,
        in_specs=placed,
        out_specs=(
            P(("replica", "local"), "node"),
            P(("replica", "local"), None),
            P("local", "node", "replica", None),
            P("local", "node", "replica", None),
        ),
        check_vma=False,
    )
```

profile of v0, /device:TPU:6, one launch (start us, length us, event | category | flops | bytes accessed | tf_op | source)
XLA Modules:
  0.0 967.4 jit_solution(10894059825687185062)
XLA Ops:
  7.2 0.9 copy.60
  8.4 1.2 reduce-window.6
  10.1 1.1 copy.65
  11.8 1.1 convolution_convert_fusion
  13.0 4.2 all-to-all-start
  17.2 1.4 add_divide_fusion
  18.6 8.2 all-to-all-done
  26.7 3.5 multiply_reduce_fusion
  30.7 0.7 all_to_all.21
  31.4 3.2 all-to-all-start.1
  34.7 2.9 bitcast_convert_fusion
  38.4 27.8 %reduce-scatter.4.cloned.1.call-done = bf16[288,256]{1,0:T(8,128)(2,1)} async-done(((bf16[288,1024]{1,0:T(8,128)(2,1)}), bf16[288,256]{1,0:T(8,128)(2,1)}) %reduce-scatter.4.cloned.1.call-update) | async-done | bytes 147472 | tf_op jit(solution)/shard_map/reduce_scatter | solution.py:55
  66.2 1.4 fusion.15
  67.6 13.3 %all_gather.6 = bf16[288,1024]{1,0:T(8,128)(2,1)S(1)} all-gather(bf16[288,256]{1,0:T(8,128)(2,1)S(1)} %get-tuple-element.27), channel_id=1, replica_groups=mesh['replica'=48,'node'=4,'local'=4] {'node'}, dimensions={1}, use_global_device_ids=true | all-gather | bytes 737280 | tf_op jit(solution)/shard_map/all_gather | solution.py:70
  80.8 3.1 convolution_bitcast_fusion.1
  84.0 4.8 reshape.125
  88.9 12.9 %all_gather.7 = bf16[288,1024]{1,0:T(8,128)(2,1)S(1)} all-gather(bf16[288,256]{1,0:T(8,128)(2,1)S(1)} %get-tuple-element.28), channel_id=1, replica_groups=mesh['replica'=48,'node'=4,'local'=4] {'node'}, dimensions={1}, use_global_device_ids=true | all-gather | bytes 737280 | tf_op jit(solution)/shard_map/all_gather | solution.py:71
  101.8 4.3 convolution_bitcast_fusion
  106.1 4.8 reshape.127
  110.9 1.3 dynamic-slice
  112.2 7.5 all-reduce
  119.7 0.7 dynamic-slice_reduce_fusion
  121.0 3.2 all-to-all-start.3
  124.3 2.5 fusion
  126.8 1.7 fusion.9
  128.5 3.6 all-to-all-start.2
  133.4 8.2 all-to-all-done.2
  141.6 1.1 convolution_convert_fusion.1
  142.7 380.5 %reduce-scatter.6.cloned.1.call-done = f32[160,128]{1,0:T(8,128)} async-done(((f32[7680,128]{1,0:T(8,128)}), f32[160,128]{1,0:T(8,128)}) %reduce-scatter.6.cloned.1.call-update) | async-done | bytes 81936 | tf_op jit(solution)/shard_map/reduce_scatter | solution.py:122
  523.3 1.5 multiply_bitcast_fusion.1
  524.8 434.5 %reduce-scatter.8.cloned.1.call-done = f32[160,128]{1,0:T(8,128)} async-done(((f32[7680,128]{1,0:T(8,128)}), f32[160,128]{1,0:T(8,128)}) %reduce-scatter.8.cloned.1.call-update) | async-done | bytes 81936 | tf_op jit(solution)/shard_map/reduce_scatter | solution.py:128
  959.3 1.5 multiply_bitcast_fusion
  (48 shorter events, 4.8 us)
Async XLA Ops:
  7.2 19.6 %copy-start = (bf16[1,1024,960]{1,2,0:T(8,128)(2,1)S(1)}, bf16[1,1024,960]{1,2,0:T(8,128)(2,1)}, u32[]{:S(2)}) copy-start(bf16[1,1024,960]{1,2,0:T(8,128)(2,1)} %param.17) | copy-start | bytes 5898244
  13.0 13.8 %all-to-all-start = ((bf16[4,72,960]{2,1,0:T(8,128)(2,1)}), bf16[4,72,960]{2,1,0:T(8,128)(2,1)}, u32[]{:S(2)}, u32[]{:S(2)}) async-start(bf16[4,72,960]{2,1,0:T(8,128)(2,1)} %bitcast.2), calls=%async_computation | async-start | bytes 1179648 | tf_op jit(solution)/shard_map/all_to_all | solution.py:30
  17.1 49.1 %reduce-scatter.4.cloned.1.call-start = ((), (), s32[]{:S(2)}) async-start(), calls=%async_computation.7 | async-start | bytes 737280 | tf_op jit(solution)/shard_map/reduce_scatter | solution.py:55
  26.7 3.5 copy-start.3
  31.4 6.9 all-to-all-start.1
  34.6 488.6 %reduce-scatter.6.cloned.1.call-start = ((), (), s32[]{:S(2)}) async-start(), calls=%async_computation.8 | async-start | bytes 4014080 | tf_op jit(solution)/shard_map/reduce_scatter | solution.py:122
  66.2 14.7 %copy-start.1 = (bf16[1,1,4,72,960]{4,3,2,1,0:T(8,128)(2,1)S(1)}, bf16[1,1,4,72,960]{4,3,2,1,0:T(8,128)(2,1)}, u32[]{:S(2)}) copy-start(bf16[1,1,4,72,960]{4,3,2,1,0:T(8,128)(2,1)} %param.12) | copy-start | bytes 1658884
  88.8 870.5 %reduce-scatter.8.cloned.1.call-start = ((), (), s32[]{:S(2)}) async-start(), calls=%async_computation.9 | async-start | bytes 4014080 | tf_op jit(solution)/shard_map/reduce_scatter | solution.py:128
  121.0 7.4 all-to-all-start.3
  124.3 2.5 copy-start.4
  128.5 3.8 copy-start.2
  128.5 13.1 %all-to-all-start.2 = ((bf16[4,72,960]{2,1,0:T(8,128)(2,1)}), bf16[4,72,960]{2,1,0:T(8,128)(2,1)S(1)}, u32[]{:S(2)}, u32[]{:S(2)}) async-start(bf16[4,72,960]{2,1,0:T(8,128)(2,1)} %bitcast.10), calls=%async_computation.3 | async-start | bytes 1179648 | tf_op jit(solution)/shard_map/all_to_all | solution.py:81
Sparse Core Ops, SparseCore 0:
  30.4 35.7 reduce-scatter.3
  88.9 434.2 reduce-scatter.5
  529.1 430.1 reduce-scatter.7
where the time goes:
time: 968 us; the launch traced here: 967 us
  waiting for transfers between devices  860 us (89%)
  blocking collectives  33.7 us (3%)
  matrix products  17.7 us (2%)
  local copies, waits for them, and re-layouts  17.6 us (2%)
  starting transfers between devices  14.3 us (1%)
  between operations  13.9 us (1%)
  other arithmetic  10.2 us (1%)
    reduce_scatter x1, waiting for transfers between devices, local(): lax.psum_scatter(feature_term(lax.axis_size('replica') * share_rows, up_d...  435 us
    reduce_scatter x1, waiting for transfers between devices, local(): lax.psum_scatter(feature_term(lax.axis_size('replica') * share_rows, gate...  381 us
    reduce_scatter x1, waiting for transfers between devices, local(): lax.psum_scatter(raw_part.astype(jnp.bfloat16), 'node', scatter_dimension...  27.8 us
  transfers between devices with their start and end apart: 7, of which 6 were waited for; matrix products, arithmetic and copies ran while one was open for 3% of the time, Pallas kernels for 0%

commit v1 on v0

v1 whole, which is shorter than its diff:
```python
import functools

import jax
import jax.numpy as jnp
from jax import lax
from jax.experimental import pallas as pl
from jax.experimental.pallas import tpu as pltpu
from jax.sharding import Mesh
from jax.sharding import PartitionSpec as P

BF = jnp.bfloat16
F32 = jnp.float32
MIB = 1 << 20


def picks_of(routes, n_local, capacity):
    tokens, top = routes.shape
    lanes = lax.broadcasted_iota(jnp.int32, (tokens, 128), 1)
    named = [(lanes == routes[:, k : k + 1]) for k in range(top)]
    total = sum(jnp.where(n, 1.0, 0.0) for n in named).astype(BF)
    rows = lax.broadcasted_iota(jnp.int32, (tokens, tokens), 0)
    cols = lax.broadcasted_iota(jnp.int32, (tokens, tokens), 1)
    earlier = jnp.where(cols < rows, 1.0, 0.0).astype(BF)
    before = jnp.dot(earlier, total, preferred_element_type=F32)
    slots = lax.broadcasted_iota(jnp.int32, (tokens, n_local * capacity), 1)
    masks = []
    for k in range(top):
        slot = jnp.sum(jnp.where(named[k], before, 0.0), axis=1, keepdims=True)
        masks.append(slots == routes[:, k : k + 1] * capacity + slot.astype(jnp.int32))
    return masks


def dispatch_kernel(n_local, capacity, routes_ref, gates_ref, rows_ref, out_ref):
    masks = picks_of(routes_ref[...], n_local, capacity)
    gates = gates_ref[...].astype(F32)
    scaled = sum(
        jnp.where(m, gates[:, k : k + 1], 0.0) for k, m in enumerate(masks)
    ).astype(BF)
    out = lax.dot_general(
        scaled, rows_ref[...], (((0,), (0,)), ((), ())), preferred_element_type=F32
    ).astype(BF)
    for e in range(n_local):
        out_ref[e] = out[e * capacity : (e + 1) * capacity]


def raw_kernel(rows_ref, down_ref, out_ref):
    out_ref[0] = lax.dot_general(
        rows_ref[...], down_ref[...], (((1,), (1,)), ((), ())), preferred_element_type=F32
    ).astype(BF)


def sum_kernel(parts_ref, out_ref):
    total = parts_ref[0].astype(F32)
    for i in range(1, parts_ref.shape[0]):
        total = total + parts_ref[i].astype(F32)
    out_ref[...] = total.astype(BF)


def delta_kernel(raw_ref, gate_ref, up_ref, x_ref, grad_ref, delta_ref, dgate_ref):
    step = pl.program_id(0)
    raw = raw_ref[0].astype(F32)
    g = gate_ref[...].astype(F32)
    u = up_ref[...].astype(F32)
    sig = 1.0 / (1.0 + jnp.exp(-g))
    act = g * sig
    up_delta = raw * act
    gate_delta = raw * u * sig * (1.0 + g * (1.0 - sig))
    both = jnp.concatenate([gate_delta.astype(BF), up_delta.astype(BF)], axis=1)
    delta_ref[0] = both
    grad_ref[...] = jnp.dot(x_ref[...], both, preferred_element_type=F32).astype(BF)

    @pl.when(step == 0)
    def _():
        dgate_ref[...] = jnp.zeros_like(dgate_ref)

    dgate_ref[...] += jnp.broadcast_to(
        jnp.sum(up_delta * u, axis=1, keepdims=True), dgate_ref.shape
    )


def input_kernel(feat, delta_ref, wg_ref, wu_ref, dgate_ref, out_ref, total):
    step = pl.program_id(0)
    quarter = wg_ref.shape[1]
    dims = (((1,), (1,)), ((), ()))
    term = lax.dot_general(
        delta_ref[0, :, :quarter], wg_ref[...], dims, preferred_element_type=F32
    ) + lax.dot_general(delta_ref[0, :, quarter:], wu_ref[...], dims, preferred_element_type=F32)

    @pl.when(step == 0)
    def _():
        total[...] = term

    @pl.when(step > 0)
    def _():
        total[...] += term

    @pl.when(step == pl.num_programs(0) - 1)
    def _():
        rest = out_ref.shape[1] - feat
        out_ref[:, :feat] = total[...].astype(BF)
        out_ref[:, feat:] = dgate_ref[:, :rest].astype(BF)


def combine_kernel(n_local, capacity, routes_ref, gates_ref, back_ref, rows_ref, grads_ref):
    masks = [jnp.where(m, 1.0, 0.0).astype(BF) for m in picks_of(routes_ref[...], n_local, capacity)]
    feat = rows_ref.shape[1]
    back = back_ref[...]
    rows_ref[...] = jnp.dot(
        sum(masks[1:], masks[0]), back[:, :feat], preferred_element_type=F32
    ).astype(BF)
    tail = back[:, back.shape[1] - 128 :]
    gates = gates_ref[...].astype(F32)
    for k, m in enumerate(masks):
        own = jnp.dot(m, tail, preferred_element_type=F32)[:, 127:128]
        grads_ref[:, k : k + 1] = (own / gates[:, k : k + 1]).astype(BF)


def params(mib=32, **more):
    return pltpu.CompilerParams(vmem_limit_bytes=mib * MIB, **more)


def local(token_grads, routes, gates, expert_inputs, gate_pre, up_pre, w_gate, w_up, w_down):
    tokens, top = routes.shape
    n_local = lax.axis_size("local")
    n_node = lax.axis_size("node")
    n_z = lax.axis_size("z")
    n_y = lax.axis_size("y")
    n_copies = n_y * n_z
    capacity = expert_inputs.shape[3]
    feat = token_grads.shape[1]
    hidden = gate_pre.shape[4]
    quarter = hidden // n_node
    slots = n_local * capacity
    own = feat // n_copies
    wide = -(-(feat + 1) // 128) * 128

    outgoing = pl.pallas_call(
        functools.partial(dispatch_kernel, n_local, capacity),
        out_shape=jax.ShapeDtypeStruct((n_local, capacity, feat), BF),
        compiler_params=params(),
        name="dispatch",
    )(routes, gates, token_grads)
    arrived = lax.all_to_all(outgoing, "local", split_axis=0, concat_axis=0, tiled=True)

    raw_parts = pl.pallas_call(
        raw_kernel,
        grid=(n_node,),
        in_specs=[
            pl.BlockSpec((slots, feat), lambda i: (0, 0)),
            pl.BlockSpec((quarter, feat), lambda i: (i, 0)),
        ],
        out_specs=pl.BlockSpec((1, slots, quarter), lambda i: (i, 0, 0)),
        out_shape=jax.ShapeDtypeStruct((n_node, slots, quarter), BF),
        compiler_params=params(),
        name="raw",
    )(arrived.reshape(slots, feat), w_down[0])
    raw_shares = lax.all_to_all(raw_parts, "node", split_axis=0, concat_axis=0, tiled=True)
    raw_share = pl.pallas_call(
        sum_kernel,
        out_shape=jax.ShapeDtypeStruct((slots, quarter), BF),
        compiler_params=params(),
        name="share",
    )(raw_shares)
    raw = lax.all_gather(raw_share, "node", axis=0, tiled=False)

    x_rows = (
        expert_inputs[0, 0]
        .reshape(slots, n_y, n_z, own)
        .transpose(2, 1, 3, 0)
        .reshape(feat, slots)
    )
    grad, delta, dgate = pl.pallas_call(
        delta_kernel,
        grid=(n_node,),
        in_specs=[
            pl.BlockSpec((1, slots, quarter), lambda i: (i, 0, 0)),
            pl.BlockSpec((slots, quarter), lambda i: (0, i)),
            pl.BlockSpec((slots, quarter), lambda i: (0, i)),
            pl.BlockSpec((feat, slots), lambda i: (0, 0)),
        ],
        out_specs=[
            pl.BlockSpec((feat, 2 * quarter), lambda i: (0, i)),
            pl.BlockSpec((1, slots, 2 * quarter), lambda i: (i, 0, 0)),
            pl.BlockSpec((slots, 128), lambda i: (0, 0)),
        ],
        out_shape=[
            jax.ShapeDtypeStruct((feat, 2 * hidden), BF),
            jax.ShapeDtypeStruct((n_node, slots, 2 * quarter), BF),
            jax.ShapeDtypeStruct((slots, 128), F32),
        ],
        compiler_params=params(),
        name="delta",
    )(raw, gate_pre.reshape(slots, hidden), up_pre.reshape(slots, hidden), x_rows)

    z_sum = lax.psum_scatter(grad, "z", scatter_dimension=0, tiled=True)

    slot_input = pl.pallas_call(
        functools.partial(input_kernel, feat),
        grid=(n_node,),
        in_specs=[
            pl.BlockSpec((1, slots, 2 * quarter), lambda i: (i, 0, 0)),
            pl.BlockSpec((feat, quarter), lambda i: (0, i)),
            pl.BlockSpec((feat, quarter), lambda i: (0, i)),
            pl.BlockSpec((slots, 128), lambda i: (0, 0)),
        ],
        out_specs=pl.BlockSpec((slots, wide), lambda i: (0, 0)),
        out_shape=jax.ShapeDtypeStruct((slots, wide), BF),
        scratch_shapes=[pltpu.VMEM((slots, feat), F32)],
        compiler_params=params(),
        name="slot_input",
    )(delta, w_gate[0], w_up[0], dgate)
    back = lax.all_to_all(
        slot_input.reshape(n_local, capacity, wide), "local", split_axis=0, concat_axis=0, tiled=True
    )
    input_grads, gate_grads = pl.pallas_call(
        functools.partial(combine_kernel, n_local, capacity),
        out_shape=[
            jax.ShapeDtypeStruct((tokens, feat), BF),
            jax.ShapeDtypeStruct((tokens, top), BF),
        ],
        compiler_params=params(),
        name="combine",
    )(routes, gates, back.reshape(slots, wide))

    y_parts = lax.all_to_all(
        z_sum.reshape(n_y, own, 2 * hidden), "y", split_axis=0, concat_axis=0, tiled=True
    )
    total = jnp.sum(y_parts.astype(F32), axis=0) / n_copies
    total = total.reshape(own, n_node, 2, quarter)
    rows = own * hidden // 128
    gate_weight_grads = total[:, :, 0].reshape(1, 1, rows, 128)
    up_weight_grads = total[:, :, 1].reshape(1, 1, rows, 128)
    return (input_grads, gate_grads, gate_weight_grads, up_weight_grads)


def solution(mesh):
    n_y = 4
    shape = mesh.devices.shape
    cut = Mesh(
        mesh.devices.reshape(n_y, shape[0] // n_y, shape[1], shape[2]), ("y", "z", "node", "local")
    )
    replica = ("y", "z")
    placed = (
        P((*replica, "local"), "node"),
        P((*replica, "local"), None),
        P((*replica, "local"), None),
        P(replica, "local", None, None, "node"),
        P(replica, "local", None, None, None),
        P(replica, "local", None, None, None),
        P("local", "node", None),
        P("local", "node", None),
        P("local", None, "node"),
    )
    return jax.shard_map(
        local,
        mesh=cut,
        in_specs=placed,
        out_specs=(
            P((*replica, "local"), "node"),
            P((*replica, "local"), None),
            P("local", "node", replica, None),
            P("local", "node", replica, None),
        ),
        check_vma=False,
    )
```

time: 968 us -> 161 us (0.17)
  waiting for transfers between devices: 860 us -> 72.8 us
  blocking collectives: 33.7 us -> 13.5 us
  matrix products: 17.7 us -> 0 us
  Pallas kernels: 0 us -> 12.9 us
  starting transfers between devices: 14.3 us -> 26.6 us
  other arithmetic: 10.2 us -> 0.08 us
    reduce_scatter x3 -> x1, waiting for transfers between devices: 843 us -> 54.6 us  [local(): z_sum = lax.psum_scatter(grad, 'z', scatter_dimension=0, tiled=True)]
    dot_general x9 -> x0, matrix products: 17.7 us -> none  [the longest x2 7.42 us: feature_term(): lax.dot_general(x_rows, deltas, (((0,), (0,)), ((), ())), preferred_eleme...]
    pallas_call x0 -> x6, Pallas kernels: none -> 12.9 us  [the longest x1 4.15 us: local(): pl.pallas_call(delta_kernel, grid=(n_node,), in_specs=[pl.BlockSpec((1, s...]
    all_gather x2 -> x1, blocking collectives: 26.2 us -> 13.5 us  [local(): raw = lax.all_gather(raw_share, 'node', axis=0, tiled=False)]
    all_to_all x4, starting transfers between devices: 14.2 us -> 26.6 us  [the longest x1 12.9 us: local(): lax.all_to_all(raw_parts, 'node', split_axis=0, concat_axis=0, tiled=True)]
  transfers between devices with their start and end apart: 7 -> 5, of which waited for: 6 -> 4; matrix products, arithmetic and copies ran while one was open for 3% -> 7% of each run, Pallas kernels for 0% -> 3%
where the time goes in v1:
time: 161 us; the launch traced here: 160 us
  waiting for transfers between devices  72.8 us (45%)
  starting transfers between devices  26.6 us (17%)
  local copies, waits for them, and re-layouts  20 us (12%)
  between operations  14.1 us (9%)
  blocking collectives  13.5 us (8%)
  Pallas kernels  12.9 us (8%)
    reduce_scatter x1, waiting for transfers between devices, local(): z_sum = lax.psum_scatter(grad, 'z', scatter_dimension=0, tiled=True)  54.6 us
    unnamed x19, local copies, waits for them, and re-layouts  14 us
    all_gather x1, blocking collectives, local(): raw = lax.all_gather(raw_share, 'node', axis=0, tiled=False)  13.5 us
    all_to_all x1, starting transfers between devices, local(): lax.all_to_all(raw_parts, 'node', split_axis=0, concat_axis=0, tiled=True)  12.9 us
    all_to_all x1, waiting for transfers between devices, local(): lax.all_to_all(z_sum.reshape(n_y, own, 2 * hidden), 'y', split_axis=0, co...  7.71 us
    all_to_all x1, starting transfers between devices, local(): lax.all_to_all(z_sum.reshape(n_y, own, 2 * hidden), 'y', split_axis=0, co...  6.69 us
    all_to_all x1, waiting for transfers between devices, local(): lax.all_to_all(outgoing, 'local', split_axis=0, concat_axis=0, tiled=True)  6.67 us
    pallas_call x1, Pallas kernels, local(): pl.pallas_call(delta_kernel, grid=(n_node,), in_specs=[pl.BlockSpec((1, s...  4.15 us
  transfers between devices with their start and end apart: 5, of which 4 were waited for; matrix products, arithmetic and copies ran while one was open for 7% of the time, Pallas kernels for 3%

profile of v1, /device:TPU:6, one launch (start us, length us, event | category | flops | bytes accessed | tf_op | source)
XLA Modules:
  0.0 160.0 jit_solution(12083099738726380695)
XLA Ops:
  7.2 0.8 copy.29.gates_ref
  7.9 0.8 copy.28.routes_ref
  8.7 1.1 copy.24.rows_ref
  9.8 1.6 dispatch.1
  11.4 3.5 %all-to-all-start = ((bf16[4,72,960]{2,1,0:T(8,128)(2,1)}), bf16[4,72,960]{2,1,0:T(8,128)(2,1)S(1)}, u32[]{:S(2)}, u32[]{:S(2)}) async-start(bf16[4,72,960]{2,1,0:T(8,128)(2,1)} %dispatch.1), calls=%async_computation | async-start | bytes 1179648 | tf_op jit(solution)/shard_map/all_to_all | solution.py:143
  14.9 2.8 %copy.25 = bf16[1,1024,960]{2,1,0:T(8,128)(2,1)S(1)} copy(bf16[1,1024,960]{1,2,0:T(8,128)(2,1)} %param.17) | data formatting | bytes 3932160 | tf_op args[8]
  17.7 6.7 %all-to-all-done = bf16[4,72,960]{2,1,0:T(8,128)(2,1)S(1)} async-done(((bf16[4,72,960]{2,1,0:T(8,128)(2,1)}), bf16[4,72,960]{2,1,0:T(8,128)(2,1)S(1)}, u32[]{:S(2)}, u32[]{:S(2)}) %all-to-all-start) | async-done | bytes 552992 | tf_op jit(solution)/shard_map/all_to_all | solution.py:143
  24.4 2.4 %raw.1 = bf16[4,288,256]{2,1,0:T(8,128)(2,1)} custom-call(bf16[288,960]{1,0:T(8,128)(2,1)S(1)} %bitcast.15, bf16[1024,960]{1,0:T(8,128)(2,1)S(1)} %bitcast.14), custom_call_target="tpu_custom_call" | custom-call | tf_op jit(solution)/shard_map/raw/pallas_call | solution.py:145
  26.8 12.9 %all-to-all-start.1 = ((bf16[4,288,256]{2,1,0:T(8,128)(2,1)}), bf16[4,288,256]{2,1,0:T(8,128)(2,1)S(1)}, u32[]{:S(2)}, u32[]{:S(2)}) async-start(bf16[4,288,256]{2,1,0:T(8,128)(2,1)} %raw.1), calls=%async_computation.1 | async-start | bytes 1179648 | tf_op jit(solution)/shard_map/all_to_all | solution.py:157
  39.7 1.0 copy.26
  40.8 0.8 reshape_squeeze.9
  41.6 1.0 copy.27
  42.6 1.5 reshape.36.x_ref
  44.2 3.8 %all-to-all-done.1.parts_ref = bf16[4,288,256]{2,1,0:T(8,128)(2,1)S(1)} async-done(((bf16[4,288,256]{2,1,0:T(8,128)(2,1)}), bf16[4,288,256]{2,1,0:T(8,128)(2,1)S(1)}, u32[]{:S(2)}, u32[]{:S(2)}) %all-to-all-start.1) | async-done | bytes 589856 | tf_op jit(solution)/shard_map/all_to_all | solution.py:157
  47.9 0.1 share.1
  48.0 13.5 %all-gather = bf16[1152,256]{1,0:T(8,128)(2,1)S(1)} all-gather(bf16[288,256]{1,0:T(8,128)(2,1)S(1)} %share.1), channel_id=2, replica_groups=mesh['y'=4,'z'=12,'node'=4,'local'=4] {'node'}, dimensions={0}, use_global_device_ids=true | all-gather | bytes 737280 | tf_op jit(solution)/shard_map/all_gather | solution.py:164
  61.6 1.1 copy-done.4
  62.6 4.1 %delta.1 = (bf16[960,2048]{1,0:T(8,128)(2,1)S(1)}, bf16[4,288,512]{2,1,0:T(8,128)(2,1)S(1)}, f32[288,128]{1,0:T(8,128)S(1)}) custom-call(bf16[4,288,256]{2,1,0:T(8,128)(2,1)S(1)} %bitcast.16, bf16[288,1024]{1,0:T(8,128)(2,1)S(1)} %bitcast.20, bf16[288,1024]{1,0:T(8,128)(2,1)S(1)} %bitcast.21, bf16[960,288]{1,0:T(8,128)(2,1)S(1)} %reshape.36.x_ref), custom_call_target="tpu_custom_call" | custom-call | tf_op jit(solution)/shard_map/delta/pallas_call | solution.py:172
  66.8 1.8 %copy-done = bf16[960,2048]{1,0:T(8,128)(2,1)} copy-done((bf16[960,2048]{1,0:T(8,128)(2,1)}, bf16[960,2048]{1,0:T(8,128)(2,1)S(1)}, u32[]{:S(2)}) %copy-start) | copy-done | bytes 3932184
  68.7 1.5 copy-done.1
  70.2 1.5 copy-done.2
  71.7 3.9 %slot_input.1 = bf16[288,1024]{1,0:T(8,128)(2,1)} custom-call(bf16[4,288,512]{2,1,0:T(8,128)(2,1)S(1)} %get-tuple-element.9.delta_ref, bf16[960,1024]{1,0:T(8,128)(2,1)S(1)} %bitcast.18, bf16[960,1024]{1,0:T(8,128)(2,1)S(1)} %bitcast.19, f32[288,128]{1,0:T(8,128)S(1)} %get-tuple-element.10.dgate_ref), custom_call_target="tpu_custom_call" | custom-call | tf_op jit(solution)/shard_map/slot_input/pallas_call | solution.py:197
  75.6 3.5 %all-to-all-start.2 = ((bf16[4,72,1024]{2,1,0:T(8,128)(2,1)}), bf16[4,72,1024]{2,1,0:T(8,128)(2,1)S(1)}, u32[]{:S(2)}, u32[]{:S(2)}) async-start(bf16[4,72,1024]{2,1,0:T(8,128)(2,1)} %bitcast.8), calls=%async_computation.2 | async-start | bytes 1179648 | tf_op jit(solution)/shard_map/all_to_all | solution.py:212
  79.1 54.6 %reduce-scatter.2.cloned.1.call-done = bf16[80,2048]{1,0:T(8,128)(2,1)} async-done(((bf16[960,2048]{1,0:T(8,128)(2,1)}), bf16[80,2048]{1,0:T(8,128)(2,1)}) %reduce-scatter.2.cloned.1.call-update) | async-done | bytes 327696 | tf_op jit(solution)/shard_map/reduce_scatter | solution.py:195
  133.7 1.8 %reshape.39 = bf16[4,20,2048]{2,1,0:T(8,128)(2,1)} reshape(bf16[80,2048]{1,0:T(8,128)(2,1)} %reduce-scatter.2.cloned.1.call-done) | data formatting | bytes 655360 | tf_op jit(solution)/shard_map/reshape | solution.py:226
  135.5 6.7 %all-to-all-start.3 = ((bf16[4,20,2048]{2,1,0:T(8,128)(2,1)}), bf16[4,20,2048]{2,1,0:T(8,128)(2,1)S(1)}, u32[]{:S(2)}, u32[]{:S(2)}) async-start(bf16[4,20,2048]{2,1,0:T(8,128)(2,1)} %reshape.39), calls=%async_computation.4 | async-start | bytes 786432 | tf_op jit(solution)/shard_map/all_to_all | solution.py:225
  142.2 0.8 combine.1
  143.0 0.8 copy.30
  143.8 0.6 copy.31
  144.4 7.7 %all-to-all-done.3 = bf16[4,20,2048]{2,1,0:T(8,128)(2,1)S(1)} async-done(((bf16[4,20,2048]{2,1,0:T(8,128)(2,1)}), bf16[4,20,2048]{2,1,0:T(8,128)(2,1)S(1)}, u32[]{:S(2)}, u32[]{:S(2)}) %all-to-all-start.3) | async-done | bytes 327712 | tf_op jit(solution)/shard_map/all_to_all | solution.py:225
  152.2 0.1 div.10
  152.4 0.8 fusion
  (13 shorter events, 0.1 us)
Async XLA Ops:
  11.4 13.0 %all-to-all-start = ((bf16[4,72,960]{2,1,0:T(8,128)(2,1)}), bf16[4,72,960]{2,1,0:T(8,128)(2,1)S(1)}, u32[]{:S(2)}, u32[]{:S(2)}) async-start(bf16[4,72,960]{2,1,0:T(8,128)(2,1)} %dispatch.1), calls=%async_computation | async-start | bytes 1179648 | tf_op jit(solution)/shard_map/all_to_all | solution.py:143
  24.4 15.3 %copy-start.5 = (bf16[1,1,4,72,960]{4,3,2,1,0:T(8,128)(2,1)S(1)}, bf16[1,1,4,72,960]{4,3,2,1,0:T(8,128)(2,1)}, u32[]{:S(2)}) copy-start(bf16[1,1,4,72,960]{4,3,2,1,0:T(8,128)(2,1)} %param.12) | copy-start | bytes 1658884
  26.8 21.1 %all-to-all-start.1 = ((bf16[4,288,256]{2,1,0:T(8,128)(2,1)}), bf16[4,288,256]{2,1,0:T(8,128)(2,1)S(1)}, u32[]{:S(2)}, u32[]{:S(2)}) async-start(bf16[4,288,256]{2,1,0:T(8,128)(2,1)} %raw.1), calls=%async_computation.1 | async-start | bytes 1179648 | tf_op jit(solution)/shard_map/all_to_all | solution.py:157
  39.7 93.9 %reduce-scatter.2.cloned.1.call-start = ((), (), s32[]{:S(2)}) async-start(), calls=%async_computation.5 | async-start | bytes 4259840 | tf_op jit(solution)/shard_map/reduce_scatter | solution.py:195
  42.6 18.9 %copy-start.3 = (bf16[1,1,4,72,1024]{4,3,2,1,0:T(8,128)(2,1)S(1)}, bf16[1,1,4,72,1024]{4,3,2,1,0:T(8,128)(2,1)}, u32[]{:S(2)}) copy-start(bf16[1,1,4,72,1024]{4,3,2,1,0:T(8,128)(2,1)} %param.13) | copy-start | bytes 1769476
  61.5 1.1 copy-start.4
  66.8 1.9 %copy-start = (bf16[960,2048]{1,0:T(8,128)(2,1)}, bf16[960,2048]{1,0:T(8,128)(2,1)S(1)}, u32[]{:S(2)}) copy-start(bf16[960,2048]{1,0:T(8,128)(2,1)S(1)} %get-tuple-element.13) | copy-start | bytes 11796484
  68.6 1.5 copy-start.1
  70.2 1.5 copy-start.2
  75.6 59.9 %all-to-all-start.2 = ((bf16[4,72,1024]{2,1,0:T(8,128)(2,1)}), bf16[4,72,1024]{2,1,0:T(8,128)(2,1)S(1)}, u32[]{:S(2)}, u32[]{:S(2)}) async-start(bf16[4,72,1024]{2,1,0:T(8,128)(2,1)} %bitcast.8), calls=%async_computation.2 | async-start | bytes 1179648 | tf_op jit(solution)/shard_map/all_to_all | solution.py:212
  135.5 16.7 %all-to-all-start.3 = ((bf16[4,20,2048]{2,1,0:T(8,128)(2,1)}), bf16[4,20,2048]{2,1,0:T(8,128)(2,1)S(1)}, u32[]{:S(2)}, u32[]{:S(2)}) async-start(bf16[4,20,2048]{2,1,0:T(8,128)(2,1)} %reshape.39), calls=%async_computation.4 | async-start | bytes 786432 | tf_op jit(solution)/shard_map/all_to_all | solution.py:225
Sparse Core Ops, SparseCore 0:
  68.8 64.8 reduce-scatter.1

commit v2 on v1

v2 whole, which is shorter than its diff:
```python
import functools

import jax
import jax.numpy as jnp
from jax import lax
from jax.experimental import pallas as pl
from jax.experimental.pallas import tpu as pltpu
from jax.sharding import Mesh
from jax.sharding import PartitionSpec as P

BF = jnp.bfloat16
F32 = jnp.float32
MIB = 1 << 20


CUT = (4, 3, 4)


def picks_of(routes, n_local, capacity, turn=None):
    tokens, top = routes.shape
    lanes = lax.broadcasted_iota(jnp.int32, (tokens, 128), 1)
    named = [(lanes == routes[:, k : k + 1]) for k in range(top)]
    total = sum(jnp.where(n, 1.0, 0.0) for n in named).astype(BF)
    rows = lax.broadcasted_iota(jnp.int32, (tokens, tokens), 0)
    cols = lax.broadcasted_iota(jnp.int32, (tokens, tokens), 1)
    earlier = jnp.where(cols < rows, 1.0, 0.0).astype(BF)
    before = jnp.dot(earlier, total, preferred_element_type=F32)
    slots = lax.broadcasted_iota(jnp.int32, (tokens, n_local * capacity), 1)
    block = routes if turn is None else jnp.bitwise_xor(routes, turn)
    masks = []
    for k in range(top):
        slot = jnp.sum(jnp.where(named[k], before, 0.0), axis=1, keepdims=True)
        masks.append(slots == block[:, k : k + 1] * capacity + slot.astype(jnp.int32))
    return masks


def dispatch_kernel(n_local, capacity, routes_ref, gates_ref, rows_ref, out_ref):
    masks = picks_of(routes_ref[...].T, n_local, capacity)
    gates = gates_ref[...].astype(F32).T
    scaled = sum(jnp.where(m, gates[:, k : k + 1], 0.0) for k, m in enumerate(masks)).astype(BF)
    out = lax.dot_general(
        scaled, rows_ref[...], (((0,), (1,)), ((), ())), preferred_element_type=F32
    ).astype(BF)
    for e in range(n_local):
        out_ref[e] = out[e * capacity : (e + 1) * capacity]


def raw_kernel(rows_ref, down_ref, out_ref):
    out_ref[0] = jnp.dot(rows_ref[...], down_ref[...], preferred_element_type=F32).astype(BF)


def sum_kernel(parts_ref, out_ref):
    total = parts_ref[0].astype(F32)
    for i in range(1, parts_ref.shape[0]):
        total = total + parts_ref[i].astype(F32)
    out_ref[...] = total.astype(BF)


def factors(g, u):
    sig = 1.0 / (1.0 + jnp.exp(-g))
    return u * sig * (1.0 + g * (1.0 - sig)), g * sig


def early_kernel(own, n_zl, place_ref, x_ref, gate_ref, up_ref, slab_ref, fact_ref):
    zl, node = place_ref[0], place_ref[1]
    feat = x_ref.shape[1]
    part = feat // n_zl
    quarter = fact_ref.shape[1] // 2
    at = lax.broadcasted_iota(jnp.int32, (part, 1), 0)
    group = jnp.floor((at.astype(F32) + 0.5) * (1.0 / own)).astype(jnp.int32)
    cols = lax.broadcasted_iota(jnp.int32, (part, feat), 1)
    x = x_ref[...]
    for k in range(n_zl):
        to = jnp.bitwise_and(zl + k, n_zl - 1)
        wanted = (group * n_zl + to) * own + (at - group * own)
        chosen = jnp.where(cols == wanted, 1.0, 0.0).astype(BF)
        slab_ref[k] = lax.dot_general(
            chosen, x, (((1,), (1,)), ((), ())), preferred_element_type=F32
        ).astype(BF)
    here = pl.ds(pl.multiple_of(node * quarter, quarter), quarter)
    for_gate, for_up = factors(gate_ref[:, here].astype(F32), up_ref[:, here].astype(F32))
    fact_ref[:, :quarter] = for_gate.astype(BF)
    fact_ref[:, quarter:] = for_up.astype(BF)


def grads_kernel(own, place_ref, raw_ref, fact_ref, *rest):
    x_refs, (out_ref, keep_ref, delta) = rest[:-3], rest[-3:]
    zl, node = place_ref[0], place_ref[1]
    n_zl, slots, quarter = raw_ref.shape
    for k in range(n_zl):
        copy = jnp.bitwise_and(zl + n_zl - k, n_zl - 1)
        raw = raw_ref[copy].astype(F32)
        fact = fact_ref[copy].astype(F32)
        if k == 0:
            keep_ref[...] = raw_ref[copy]
        rows = slice(k * slots, (k + 1) * slots)
        delta[rows, :quarter] = (raw * fact[:, :quarter]).astype(BF)
        delta[rows, quarter:] = (raw * fact[:, quarter:]).astype(BF)
    d = delta[...]
    n_node = len(x_refs)
    for k in range(n_node):
        block = jnp.bitwise_and(node + n_node - k, n_node - 1)
        res = jnp.dot(x_refs[k][...], d, preferred_element_type=F32)
        for i in range(out_ref.shape[0]):
            piece = res[i * own : (i + 1) * own]
            tall = jnp.concatenate(
                [piece[:, c * 128 : (c + 1) * 128] for c in range(piece.shape[1] // 128)], axis=0
            )
            out_ref[i, block] = tall.astype(BF)


def input_kernel(capacity, place_ref, raw_ref, gate_ref, up_ref, wg_ref, wu_ref, out_ref, total, side):
    step = pl.program_id(0)
    raw = raw_ref[0].astype(F32)
    u = up_ref[...].astype(F32)
    for_gate, for_up = factors(gate_ref[...].astype(F32), u)
    up_delta = raw * for_up
    dims = (((1,), (1,)), ((), ()))
    term = lax.dot_general(
        (raw * for_gate).astype(BF), wg_ref[...], dims, preferred_element_type=F32
    ) + lax.dot_general(up_delta.astype(BF), wu_ref[...], dims, preferred_element_type=F32)
    dgate = jnp.broadcast_to(jnp.sum(up_delta * u, axis=1, keepdims=True), side.shape)

    @pl.when(step == 0)
    def _():
        total[...] = term
        side[...] = dgate

    @pl.when(step > 0)
    def _():
        total[...] += term
        side[...] += dgate

    @pl.when(step == pl.num_programs(0) - 1)
    def _():
        feat = total.shape[1]
        rest = out_ref.shape[2] - feat
        for k in range(out_ref.shape[0]):
            to = jnp.bitwise_xor(place_ref[2], k)
            rows = pl.ds(pl.multiple_of(to * capacity, 8), capacity)
            out_ref[k, :, :feat] = total[rows, :].astype(BF)
            out_ref[k, :, feat:] = side[rows, :rest].astype(BF)


def combine_kernel(n_local, capacity, place_ref, routes_ref, gates_ref, *rest):
    back_refs, (rows_ref, grads_ref) = rest[:-2], rest[-2:]
    masks = [
        jnp.where(m, 1.0, 0.0).astype(BF)
        for m in picks_of(routes_ref[...].T, n_local, capacity, place_ref[2])
    ]
    feat = rows_ref.shape[0]
    back = jnp.concatenate([r[...] for r in back_refs], axis=0)
    rows_ref[...] = lax.dot_general(
        back[:, :feat], sum(masks[1:], masks[0]), (((0,), (1,)), ((), ())), preferred_element_type=F32
    ).astype(BF)
    tail = back[:, back.shape[1] - 128 :]
    gates = gates_ref[...].astype(F32)
    for k, m in enumerate(masks):
        sums = lax.dot_general(
            tail, m, (((0,), (1,)), ((), ())), preferred_element_type=F32
        )[127:128]
        grads_ref[k : k + 1, :] = (sums / gates[k : k + 1, :]).astype(BF)


def final_kernel(n_copies, own, parts_ref, gate_ref, up_ref):
    copies, n_node = parts_ref.shape[0], parts_ref.shape[1]
    for x in range(n_node):
        total = parts_ref[0, x].astype(F32)
        for i in range(1, copies):
            total = total + parts_ref[i, x].astype(F32)
        total = total * (1.0 / n_copies)
        per = total.shape[0] // own // 2
        for c in range(2 * per):
            out = gate_ref if c < per else up_ref
            out[:, x * per + c % per, :] = total[c * own : (c + 1) * own]


def params(mib=32, **more):
    return pltpu.CompilerParams(vmem_limit_bytes=mib * MIB, **more)


def ring(x, axis, step):
    n = lax.axis_size(axis)
    return lax.ppermute(x, axis, [(i, (i + step) % n) for i in range(n)])


SMEM = pl.BlockSpec(memory_space=pltpu.SMEM)
VMEM = pl.BlockSpec(memory_space=pltpu.VMEM)


def local(token_grads, routes, gates, expert_inputs, gate_pre, up_pre, w_gate, w_up, w_down):
    tokens, top = routes.shape
    n_local = lax.axis_size("local")
    n_node = lax.axis_size("node")
    n_zl, n_zh, n_y = lax.axis_size("zl"), lax.axis_size("zh"), lax.axis_size("y")
    n_copies = n_y * n_zh * n_zl
    capacity = expert_inputs.shape[3]
    feat = token_grads.shape[1]
    hidden = gate_pre.shape[4]
    quarter = hidden // n_node
    slots = n_local * capacity
    own = feat // n_copies
    part = feat // n_zl
    wide = -(-(feat + 1) // 128) * 128
    place = jnp.stack([lax.axis_index(a) for a in ("zl", "node", "local")]).astype(jnp.int32)
    gate_rows = gate_pre.reshape(slots, hidden)
    up_rows = up_pre.reshape(slots, hidden)
    x_rows = expert_inputs.reshape(slots, feat)

    outgoing = pl.pallas_call(
        functools.partial(dispatch_kernel, n_local, capacity),
        out_shape=jax.ShapeDtypeStruct((n_local, capacity, feat), BF),
        compiler_params=params(),
        name="dispatch",
    )(routes.T, gates.T, token_grads.T)
    arrived = lax.all_to_all(outgoing, "local", split_axis=0, concat_axis=0, tiled=True)

    x_rows, _ = lax.optimization_barrier((x_rows, outgoing))
    slabs, facts = pl.pallas_call(
        functools.partial(early_kernel, own, n_zl),
        in_specs=[SMEM, VMEM, VMEM, VMEM],
        out_shape=[
            jax.ShapeDtypeStruct((n_zl, part, slots), BF),
            jax.ShapeDtypeStruct((slots, 2 * quarter), BF),
        ],
        compiler_params=params(),
        name="early",
    )(place, x_rows, gate_rows, up_rows)
    all_facts = lax.all_gather(facts, "zl", axis=0, tiled=False)
    copies_x = [slabs[0]] + [ring(slabs[k], "zl", k) for k in range(1, n_zl)]

    raw_parts = pl.pallas_call(
        raw_kernel,
        grid=(n_node,),
        in_specs=[
            pl.BlockSpec((slots, feat), lambda i: (0, 0)),
            pl.BlockSpec((feat, quarter), lambda i: (0, i)),
        ],
        out_specs=pl.BlockSpec((1, slots, quarter), lambda i: (i, 0, 0)),
        out_shape=jax.ShapeDtypeStruct((n_node, slots, quarter), BF),
        compiler_params=params(),
        name="raw",
    )(arrived.reshape(slots, feat), w_down[0].T)
    raw_shares = lax.all_to_all(raw_parts, "node", split_axis=0, concat_axis=0, tiled=True)

    *copies_x, _ = lax.optimization_barrier((*copies_x, raw_parts))
    own_x = jnp.concatenate(copies_x, axis=1)
    node_x = [own_x] + [ring(own_x, "node", k) for k in range(1, n_node)]

    raw_share = pl.pallas_call(
        sum_kernel,
        out_shape=jax.ShapeDtypeStruct((slots, quarter), BF),
        compiler_params=params(),
        name="share",
    )(raw_shares)
    raw_copies = lax.all_gather(raw_share, "zl", axis=0, tiled=False)

    tall = own * 2 * quarter // 128
    grads, kept = pl.pallas_call(
        functools.partial(grads_kernel, own),
        in_specs=[SMEM] + [VMEM] * (2 + n_node),
        out_shape=[
            jax.ShapeDtypeStruct((n_y * n_zh, n_node, tall, 128), BF),
            jax.ShapeDtypeStruct((slots, quarter), BF),
        ],
        scratch_shapes=[pltpu.VMEM((n_zl * slots, 2 * quarter), BF)],
        compiler_params=params(),
        name="grads",
    )(place, raw_copies, all_facts, *node_x)
    parts = lax.all_to_all(
        grads.reshape(n_y * n_zh * n_node, tall, 128),
        ("y", "zh", "node"),
        split_axis=0,
        concat_axis=0,
        tiled=True,
    )

    raw = lax.all_gather(kept, "node", axis=0, tiled=False)
    slot_input = pl.pallas_call(
        functools.partial(input_kernel, capacity),
        grid=(n_node,),
        in_specs=[
            SMEM,
            pl.BlockSpec((1, slots, quarter), lambda i: (i, 0, 0)),
            pl.BlockSpec((slots, quarter), lambda i: (0, i)),
            pl.BlockSpec((slots, quarter), lambda i: (0, i)),
            pl.BlockSpec((feat, quarter), lambda i: (0, i)),
            pl.BlockSpec((feat, quarter), lambda i: (0, i)),
        ],
        out_specs=pl.BlockSpec((n_local, capacity, wide), lambda i: (0, 0, 0)),
        out_shape=jax.ShapeDtypeStruct((n_local, capacity, wide), BF),
        scratch_shapes=[pltpu.VMEM((slots, feat), F32), pltpu.VMEM((slots, 128), F32)],
        compiler_params=params(),
        name="slot_input",
    )(place, raw, gate_rows, up_rows, w_gate[0], w_up[0])
    back = [slot_input[0]] + [
        lax.ppermute(slot_input[k], "local", [(i, i ^ k) for i in range(n_local)])
        for k in range(1, n_local)
    ]
    input_grads, gate_grads = pl.pallas_call(
        functools.partial(combine_kernel, n_local, capacity),
        in_specs=[SMEM] + [VMEM] * (2 + n_local),
        out_shape=[
            jax.ShapeDtypeStruct((feat, tokens), BF),
            jax.ShapeDtypeStruct((top, tokens), BF),
        ],
        compiler_params=params(),
        name="combine",
    )(place, routes.T, gates.T, *back)

    gate_sum, up_sum = pl.pallas_call(
        functools.partial(final_kernel, n_copies, own),
        out_shape=[jax.ShapeDtypeStruct((own, hidden // 128, 128), F32)] * 2,
        compiler_params=params(),
        name="final",
    )(parts.reshape(n_y * n_zh, n_node, tall, 128))
    rows = own * hidden // 128
    return (
        input_grads.T,
        gate_grads.T,
        gate_sum.reshape(1, 1, rows, 128),
        up_sum.reshape(1, 1, rows, 128),
    )


def solution(mesh):
    shape = mesh.devices.shape
    cut = Mesh(mesh.devices.reshape(*CUT, shape[1], shape[2]), ("y", "zh", "zl", "node", "local"))
    replica = ("y", "zh", "zl")
    placed = (
        P((*replica, "local"), "node"),
        P((*replica, "local"), None),
        P((*replica, "local"), None),
        P(replica, "local", None, None, "node"),
        P(replica, "local", None, None, None),
        P(replica, "local", None, None, None),
        P("local", "node", None),
        P("local", "node", None),
        P("local", None, "node"),
    )
    return jax.shard_map(
        local,
        mesh=cut,
        in_specs=placed,
        out_specs=(
            P((*replica, "local"), "node"),
            P((*replica, "local"), None),
            P("local", "node", replica, None),
            P("local", "node", replica, None),
        ),
        check_vma=False,
    )
```

time: 161 us -> 173 us (1.075)
  waiting for transfers between devices: 72.8 us -> 22.7 us
  starting transfers between devices: 26.6 us -> 69.5 us
  blocking collectives: 13.5 us -> 37 us
  local copies, waits for them, and re-layouts: 20 us -> 11.2 us
  Pallas kernels: 12.9 us -> 16.7 us
    reduce_scatter x1 -> x0, waiting for transfers between devices: 54.6 us -> none  [local(): z_sum = lax.psum_scatter(grad, 'z', scatter_dimension=0, tiled=True)]
    ppermute x0 -> x9, starting transfers between devices: none -> 36.6 us  [the longest x6 28.9 us: ring(): return lax.ppermute(x, axis, [(i, (i + step) % n) for i in range(n)])]
    all_gather x1 -> x2, blocking collectives: 13.5 us -> 37 us  [the longest x1 22.9 us: local(): raw_copies = lax.all_gather(raw_share, 'zl', axis=0, tiled=False)]
    all_to_all x2 -> x1, starting transfers between devices: 10.2 us -> 20.1 us  [local(): lax.all_to_all(grads.reshape(n_y * n_zh * n_node, tall, 128), ('y', 'zh',...]
    ppermute x0 -> x9, waiting for transfers between devices: none -> 9.07 us  [the longest x3 5.43 us: local(): lax.ppermute(slot_input[k], 'local', [(i, i ^ k) for i in range(n_local)])]
    all_to_all x1, waiting for transfers between devices: 6.67 us -> 0.01 us  [local(): lax.all_to_all(outgoing, 'local', split_axis=0, concat_axis=0, tiled=True)]
    all_to_all x2 -> x1, waiting for transfers between devices: 7.71 us -> 13.5 us  [local(): lax.all_to_all(grads.reshape(n_y * n_zh * n_node, tall, 128), ('y', 'zh',...]
    unnamed x19 -> x28, local copies, waits for them, and re-layouts: 14 us -> 9.84 us
  transfers between devices with their start and end apart: 5 -> 13, of which waited for: 4 -> 4; matrix products, arithmetic and copies ran while one was open for 7% -> 1% of each run, Pallas kernels for 3% -> 5%
where the time goes in v2:
time: 173 us; the launch traced here: 171 us
  starting transfers between devices  69.5 us (40%)
  blocking collectives  37 us (21%)
  waiting for transfers between devices  22.7 us (13%)
  Pallas kernels  16.7 us (10%)
  between operations  14.2 us (8%)
  local copies, waits for them, and re-layouts  11.2 us (6%)
    ppermute x6, starting transfers between devices, ring(): return lax.ppermute(x, axis, [(i, (i + step) % n) for i in range(n)])  28.9 us
    all_gather x1, blocking collectives, local(): raw_copies = lax.all_gather(raw_share, 'zl', axis=0, tiled=False)  22.9 us
    all_to_all x1, starting transfers between devices, local(): lax.all_to_all(grads.reshape(n_y * n_zh * n_node, tall, 128), ('y', 'zh',...  20.1 us
    all_gather x1, blocking collectives, local(): raw = lax.all_gather(kept, 'node', axis=0, tiled=False)  14.1 us
    all_to_all x1, waiting for transfers between devices, local(): lax.all_to_all(grads.reshape(n_y * n_zh * n_node, tall, 128), ('y', 'zh',...  13.5 us
    unnamed x28, local copies, waits for them, and re-layouts  9.84 us
    all_to_all x1, starting transfers between devices, local(): lax.all_to_all(raw_parts, 'node', split_axis=0, concat_axis=0, tiled=True)  9.3 us
    ppermute x3, starting transfers between devices, local(): lax.ppermute(slot_input[k], 'local', [(i, i ^ k) for i in range(n_local)])  7.7 us
  transfers between devices with their start and end apart: 13, of which 4 were waited for; matrix products, arithmetic and copies ran while one was open for 1% of the time, Pallas kernels for 5%

profile of v2, /device:TPU:6, one launch (start us, length us, event | category | flops | bytes accessed | tf_op | source)
XLA Modules:
  0.0 171.3 jit_solution(4228111139325545104)
XLA Ops:
  7.2 0.9 copy-done.9
  9.5 1.7 dispatch.1
  11.3 1.1 copy-done
  12.3 1.1 copy-done.2
  13.4 1.1 copy-done.8
  14.5 2.6 %early.1 = (bf16[4,240,288]{2,1,0:T(8,128)(2,1)S(1)}, bf16[288,512]{1,0:T(8,128)(2,1)}) custom-call(s32[3]{0:T(128)S(1)} %pad_add_fusion.place_ref, bf16[288,960]{1,0:T(8,128)(2,1)S(1)} %bitcast.52, bf16[288,1024]{1,0:T(8,128)(2,1)S(1)} %bitcast.42, bf16[288,1024]{1,0:T(8,128)(2,1)S(1)} %bitcast.44), custom_call_target="tpu_custom_call" | custom-call | tf_op jit(solution)/shard_map/early/pallas_call | solution.py:219
  17.1 3.5 %all-to-all-start = ((bf16[4,72,960]{2,1,0:T(8,128)(2,1)}), bf16[4,72,960]{2,1,0:T(8,128)(2,1)S(1)}, u32[]{:S(2)}, u32[]{:S(2)}) async-start(bf16[4,72,960]{2,1,0:T(8,128)(2,1)} %dispatch.1), calls=%async_computation | async-start | bytes 1179648 | tf_op jit(solution)/shard_map/all_to_all | solution.py:216
  21.4 7.9 %collective-permute-start.2 = (bf16[240,288]{1,0:T(8,128)(2,1)}, bf16[240,288]{1,0:T(8,128)(2,1)S(1)}, u32[]{:S(2)}, u32[]{:S(2)}) collective-permute-start(bf16[240,288]{1,0:T(8,128)(2,1)} %get-tuple-element.30), channel_id=1, source_target_pairs={{0,48},{16,0},{32,16},{48,32},{1,49},{17,1},{33,17},{49,33},{2,50}... | collective-permute-start | bytes 414728 | tf_op jit(solution)/shard_map/ppermute | solution.py:184
  29.3 1.9 %collective-permute-start.1 = (bf16[240,288]{1,0:T(8,128)(2,1)}, bf16[240,288]{1,0:T(8,128)(2,1)S(1)}, u32[]{:S(2)}, u32[]{:S(2)}) collective-permute-start(bf16[240,288]{1,0:T(8,128)(2,1)} %get-tuple-element.31), channel_id=1, source_target_pairs={{0,32},{16,48},{32,0},{48,16},{1,33},{17,49},{33,1},{49,17},{2,34}... | collective-permute-start | bytes 414728 | tf_op jit(solution)/shard_map/ppermute | solution.py:184
  31.2 2.5 %collective-permute-start = (bf16[240,288]{1,0:T(8,128)(2,1)}, bf16[240,288]{1,0:T(8,128)(2,1)S(1)}, u32[]{:S(2)}, u32[]{:S(2)}) collective-permute-start(bf16[240,288]{1,0:T(8,128)(2,1)} %get-tuple-element.32), channel_id=1, source_target_pairs={{0,16},{16,32},{32,48},{48,0},{1,17},{17,33},{33,49},{49,1},{2,18}... | collective-permute-start | bytes 414728 | tf_op jit(solution)/shard_map/ppermute | solution.py:184
  33.7 2.5 %raw.1 = bf16[4,288,256]{2,1,0:T(8,128)(2,1)} custom-call(bf16[288,960]{1,0:T(8,128)(2,1)S(1)} %bitcast.46, bf16[960,1024]{1,0:T(8,128)(2,1)S(1)} %bitcast.48), custom_call_target="tpu_custom_call" | custom-call | tf_op jit(solution)/shard_map/raw/pallas_call | solution.py:232
  36.3 9.3 %all-to-all-start.1 = ((bf16[4,288,256]{2,1,0:T(8,128)(2,1)}), bf16[4,288,256]{2,1,0:T(8,128)(2,1)S(1)}, u32[]{:S(2)}, u32[]{:S(2)}) async-start(bf16[4,288,256]{2,1,0:T(8,128)(2,1)} %raw.1), calls=%async_computation.1 | async-start | bytes 1179648 | tf_op jit(solution)/shard_map/all_to_all | solution.py:244
  45.6 3.6 %collective-permute-done.1 = bf16[240,288]{1,0:T(8,128)(2,1)S(1)} collective-permute-done((bf16[240,288]{1,0:T(8,128)(2,1)}, bf16[240,288]{1,0:T(8,128)(2,1)S(1)}, u32[]{:S(2)}, u32[]{:S(2)}) %collective-permute-start.1) | collective-permute-done | bytes 138272 | tf_op jit(solution)/shard_map/ppermute | solution.py:184
  49.7 2.7 %collective-permute-start.5 = (bf16[240,1152]{1,0:T(8,128)(2,1)S(1)}, bf16[240,1152]{1,0:T(8,128)(2,1)S(1)}, u32[]{:S(2)}, u32[]{:S(2)}) collective-permute-start(bf16[240,1152]{1,0:T(8,128)(2,1)S(1)} %concatenate.3.rest_0_), channel_id=1, source_target_pairs={{0,12},{4,0},{8,4},{12,8},{1,13},{5,1},{9,5},{13,9},{2,14},{6,2},{... | collective-permute-start | bytes 1658888 | tf_op jit(solution)/shard_map/ppermute | solution.py:184
  52.5 12.0 %collective-permute-start.4 = (bf16[240,1152]{1,0:T(8,128)(2,1)S(1)}, bf16[240,1152]{1,0:T(8,128)(2,1)S(1)}, u32[]{:S(2)}, u32[]{:S(2)}) collective-permute-start(bf16[240,1152]{1,0:T(8,128)(2,1)S(1)} %concatenate.3.rest_0_), channel_id=1, source_target_pairs={{0,8},{4,12},{8,0},{12,4},{1,9},{5,13},{9,1},{13,5},{2,10},{6,14},... | collective-permute-start | bytes 1658888 | tf_op jit(solution)/shard_map/ppermute | solution.py:184
  64.4 1.9 %collective-permute-start.3 = (bf16[240,1152]{1,0:T(8,128)(2,1)S(1)}, bf16[240,1152]{1,0:T(8,128)(2,1)S(1)}, u32[]{:S(2)}, u32[]{:S(2)}) collective-permute-start(bf16[240,1152]{1,0:T(8,128)(2,1)S(1)} %concatenate.3.rest_0_), channel_id=1, source_target_pairs={{0,4},{4,8},{8,12},{12,0},{1,5},{5,9},{9,13},{13,1},{2,6},{6,10},{... | collective-permute-start | bytes 1658888 | tf_op jit(solution)/shard_map/ppermute | solution.py:184
  66.4 22.9 %all-gather = bf16[1152,256]{1,0:T(8,128)(2,1)S(1)} all-gather(bf16[288,256]{1,0:T(8,128)(2,1)S(1)} %share.1), channel_id=2, replica_groups=mesh['y'=4,'zh'=3,'zl'=4,'node'=4,'local'=4] {'zl'}, dimensions={0}, use_global_device_ids=true | all-gather | bytes 737280 | tf_op jit(solution)/shard_map/all_gather | solution.py:256
  89.4 1.3 copy-done.7
  90.6 3.0 %grads.1 = (bf16[12,4,80,128]{3,2,1,0:T(8,128)(2,1)}, bf16[288,256]{1,0:T(8,128)(2,1)S(1)}) custom-call(s32[3]{0:T(128)S(1)} %pad_add_fusion.place_ref, bf16[4,288,256]{2,1,0:T(8,128)(2,1)S(1)} %bitcast.47, bf16[4,288,512]{2,1,0:T(8,128)(2,1)S(1)} %bitcast.51, bf16[240,1152]{1,0:T(8,128)(2,1)S(1)} %concatenate.3.rest_0_, ...), custom_call_target="tpu_custom_call" | custom-call | tf_op jit(solution)/shard_map/grads/pallas_call | solution.py:259
  93.6 20.1 %all-to-all-start.2 = ((bf16[48,80,128]{2,1,0:T(8,128)(2,1)}), bf16[48,80,128]{2,1,0:T(8,128)(2,1)S(1)}, u32[]{:S(2)}, u32[]{:S(2)}) async-start(bf16[48,80,128]{2,1,0:T(8,128)(2,1)} %bitcast.27), calls=%async_computation.2 | async-start | bytes 1966080 | tf_op jit(solution)/shard_map/all_to_all | solution.py:270
  113.7 14.1 %all-gather.2 = bf16[1152,256]{1,0:T(8,128)(2,1)S(1)} all-gather(bf16[288,256]{1,0:T(8,128)(2,1)S(1)} %get-tuple-element.24), channel_id=4, replica_groups=mesh['y'=4,'zh'=3,'zl'=4,'node'=4,'local'=4] {'node'}, dimensions={0}, use_global_device_ids=true | all-gather | bytes 737280 | tf_op jit(solution)/shard_map/all_gather | solution.py:278
  127.8 1.5 copy-done.5
  129.4 1.5 copy-done.6
  130.9 3.8 %slot_input.1 = bf16[4,72,1024]{2,1,0:T(8,128)(2,1)S(1)} custom-call(s32[3]{0:T(128)S(1)} %pad_add_fusion.place_ref, bf16[4,288,256]{2,1,0:T(8,128)(2,1)S(1)} %bitcast.41, bf16[288,1024]{1,0:T(8,128)(2,1)S(1)} %bitcast.43, bf16[288,1024]{1,0:T(8,128)(2,1)S(1)} %bitcast.45, bf16[960,1024]{1,0:T(8,128)(2,1)S(1)} %bitcast.49, bf16[960,1024]{1,0:T(8,128)(2,1)S(1)} %bitcast.50), custom_call_target="tpu_custom_call" | custom-call | tf_op jit(solution)/shard_map/slot_input/pallas_call | solution.py:279
  134.7 1.9 %collective-permute-start.8 = (bf16[72,1024]{1,0:T(8,128)(2,1)S(1)}, bf16[72,1024]{1,0:T(8,128)(2,1)S(1)}, u32[]{:S(2)}, u32[]{:S(2)}) collective-permute-start(bf16[72,1024]{1,0:T(8,128)(2,1)S(1)} %get-tuple-element.34), channel_id=1, source_target_pairs={{0,3},{1,2},{2,1},{3,0},{4,7},{5,6},{6,5},{7,4},{8,11},{9,10},{10,... | collective-permute-start | bytes 442376 | tf_op jit(solution)/shard_map/ppermute | solution.py:297
  136.6 3.8 %collective-permute-start.7 = (bf16[72,1024]{1,0:T(8,128)(2,1)S(1)}, bf16[72,1024]{1,0:T(8,128)(2,1)S(1)}, u32[]{:S(2)}, u32[]{:S(2)}) collective-permute-start(bf16[72,1024]{1,0:T(8,128)(2,1)S(1)} %get-tuple-element.35), channel_id=1, source_target_pairs={{0,2},{1,3},{2,0},{3,1},{4,6},{5,7},{6,4},{7,5},{8,10},{9,11},{10,... | collective-permute-start | bytes 442376 | tf_op jit(solution)/shard_map/ppermute | solution.py:297
  140.4 2.0 %collective-permute-start.6 = (bf16[72,1024]{1,0:T(8,128)(2,1)S(1)}, bf16[72,1024]{1,0:T(8,128)(2,1)S(1)}, u32[]{:S(2)}, u32[]{:S(2)}) collective-permute-start(bf16[72,1024]{1,0:T(8,128)(2,1)S(1)} %get-tuple-element.36), channel_id=1, source_target_pairs={{0,1},{1,0},{2,3},{3,2},{4,5},{5,4},{6,7},{7,6},{8,9},{9,8},{10,11... | collective-permute-start | bytes 442376 | tf_op jit(solution)/shard_map/ppermute | solution.py:297
  142.4 1.7 collective-permute-done.8.rest_3_
  144.1 3.7 %collective-permute-done.7.rest_2_ = bf16[72,1024]{1,0:T(8,128)(2,1)S(1)} collective-permute-done((bf16[72,1024]{1,0:T(8,128)(2,1)S(1)}, bf16[72,1024]{1,0:T(8,128)(2,1)S(1)}, u32[]{:S(2)}, u32[]{:S(2)}) %collective-permute-start.7) | collective-permute-done | bytes 147488 | tf_op jit(solution)/shard_map/ppermute | solution.py:297
  147.9 2.2 %combine.1 = (bf16[960,128]{1,0:T(8,128)(2,1)}, bf16[2,128]{1,0:T(2,128)(2,1)}) custom-call(s32[3]{0:T(128)S(1)} %pad_add_fusion.place_ref, s32[2,128]{1,0:T(2,128)S(1)} %bitcast.55, bf16[2,128]{1,0:T(2,128)(2,1)S(1)} %bitcast.57, bf16[72,1024]{1,0:T(8,128)(2,1)S(1)} %get-tuple-element.37.rest_0_, bf16[72,1024]{1,0:T(8,128)(2,1)S(1)} %collective-permute-done.6.rest_1_, ...), custom_call_target="tpu_custom_call" | custom-call | tf_op jit(solution)/shard_map/combine/pallas_call | solution.py:300
  150.1 13.5 %all-to-all-done.2 = bf16[48,80,128]{2,1,0:T(8,128)(2,1)S(1)} async-done(((bf16[48,80,128]{2,1,0:T(8,128)(2,1)}), bf16[48,80,128]{2,1,0:T(8,128)(2,1)S(1)}, u32[]{:S(2)}, u32[]{:S(2)}) %all-to-all-start.2) | async-done | bytes 983072 | tf_op jit(solution)/shard_map/all_to_all | solution.py:270
  163.6 0.8 final.1
  (37 shorter events, 3.0 us)
Async XLA Ops:
  7.2 82.2 %all-gather.5.cloned.1.call-start = ((), (), s32[]{:S(2)}) async-start(), calls=%async_computation.3 | async-start | bytes 1474560 | tf_op jit(solution)/shard_map/all_gather | solution.py:229
  7.2 0.9 copy-start.9
  8.2 0.7 copy-start.10
  8.8 0.7 copy-start.12
  11.3 1.1 copy-start
  12.3 1.1 copy-start.2
  13.4 1.1 copy-start.8
  14.5 19.3 %copy-start.4 = (bf16[1,1024,960]{1,2,0:T(8,128)(2,1)S(1)}, bf16[1,1024,960]{1,2,0:T(8,128)(2,1)}, u32[]{:S(2)}) copy-start(bf16[1,1024,960]{1,2,0:T(8,128)(2,1)} %param.17) | copy-start | bytes 5898244
  17.1 16.6 %all-to-all-start = ((bf16[4,72,960]{2,1,0:T(8,128)(2,1)}), bf16[4,72,960]{2,1,0:T(8,128)(2,1)S(1)}, u32[]{:S(2)}, u32[]{:S(2)}) async-start(bf16[4,72,960]{2,1,0:T(8,128)(2,1)} %dispatch.1), calls=%async_computation | async-start | bytes 1179648 | tf_op jit(solution)/shard_map/all_to_all | solution.py:216
  21.4 24.2 %collective-permute-start.2 = (bf16[240,288]{1,0:T(8,128)(2,1)}, bf16[240,288]{1,0:T(8,128)(2,1)S(1)}, u32[]{:S(2)}, u32[]{:S(2)}) collective-permute-start(bf16[240,288]{1,0:T(8,128)(2,1)} %get-tuple-element.30), channel_id=1, source_target_pairs={{0,48},{16,0},{32,16},{48,32},{1,49},{17,1},{33,17},{49,33},{2,50}... | collective-permute-start | bytes 414728 | tf_op jit(solution)/shard_map/ppermute | solution.py:184
  29.3 19.9 %collective-permute-start.1 = (bf16[240,288]{1,0:T(8,128)(2,1)}, bf16[240,288]{1,0:T(8,128)(2,1)S(1)}, u32[]{:S(2)}, u32[]{:S(2)}) collective-permute-start(bf16[240,288]{1,0:T(8,128)(2,1)} %get-tuple-element.31), channel_id=1, source_target_pairs={{0,32},{16,48},{32,0},{48,16},{1,33},{17,49},{33,1},{49,17},{2,34}... | collective-permute-start | bytes 414728 | tf_op jit(solution)/shard_map/ppermute | solution.py:184
  31.2 18.0 %collective-permute-start = (bf16[240,288]{1,0:T(8,128)(2,1)}, bf16[240,288]{1,0:T(8,128)(2,1)S(1)}, u32[]{:S(2)}, u32[]{:S(2)}) collective-permute-start(bf16[240,288]{1,0:T(8,128)(2,1)} %get-tuple-element.32), channel_id=1, source_target_pairs={{0,16},{16,32},{32,48},{48,0},{1,17},{17,33},{33,49},{49,1},{2,18}... | collective-permute-start | bytes 414728 | tf_op jit(solution)/shard_map/ppermute | solution.py:184
  36.3 30.1 %all-to-all-start.1 = ((bf16[4,288,256]{2,1,0:T(8,128)(2,1)}), bf16[4,288,256]{2,1,0:T(8,128)(2,1)S(1)}, u32[]{:S(2)}, u32[]{:S(2)}) async-start(bf16[4,288,256]{2,1,0:T(8,128)(2,1)} %raw.1), calls=%async_computation.1 | async-start | bytes 1179648 | tf_op jit(solution)/shard_map/all_to_all | solution.py:244
  49.7 39.6 %collective-permute-start.5 = (bf16[240,1152]{1,0:T(8,128)(2,1)S(1)}, bf16[240,1152]{1,0:T(8,128)(2,1)S(1)}, u32[]{:S(2)}, u32[]{:S(2)}) collective-permute-start(bf16[240,1152]{1,0:T(8,128)(2,1)S(1)} %concatenate.3.rest_0_), channel_id=1, source_target_pairs={{0,12},{4,0},{8,4},{12,8},{1,13},{5,1},{9,5},{13,9},{2,14},{6,2},{... | collective-permute-start | bytes 1658888 | tf_op jit(solution)/shard_map/ppermute | solution.py:184
  52.5 36.9 %collective-permute-start.4 = (bf16[240,1152]{1,0:T(8,128)(2,1)S(1)}, bf16[240,1152]{1,0:T(8,128)(2,1)S(1)}, u32[]{:S(2)}, u32[]{:S(2)}) collective-permute-start(bf16[240,1152]{1,0:T(8,128)(2,1)S(1)} %concatenate.3.rest_0_), channel_id=1, source_target_pairs={{0,8},{4,12},{8,0},{12,4},{1,9},{5,13},{9,1},{13,5},{2,10},{6,14},... | collective-permute-start | bytes 1658888 | tf_op jit(solution)/shard_map/ppermute | solution.py:184
  64.4 24.9 %collective-permute-start.3 = (bf16[240,1152]{1,0:T(8,128)(2,1)S(1)}, bf16[240,1152]{1,0:T(8,128)(2,1)S(1)}, u32[]{:S(2)}, u32[]{:S(2)}) collective-permute-start(bf16[240,1152]{1,0:T(8,128)(2,1)S(1)} %concatenate.3.rest_0_), channel_id=1, source_target_pairs={{0,4},{4,8},{8,12},{12,0},{1,5},{5,9},{9,13},{13,1},{2,6},{6,10},{... | collective-permute-start | bytes 1658888 | tf_op jit(solution)/shard_map/ppermute | solution.py:184
  89.4 1.3 copy-start.7
  93.6 34.2 %copy-start.1 = (bf16[1,1,4,72,1024]{4,3,2,1,0:T(8,128)(2,1)S(1)}, bf16[1,1,4,72,1024]{4,3,2,1,0:T(8,128)(2,1)}, u32[]{:S(2)}) copy-start(bf16[1,1,4,72,1024]{4,3,2,1,0:T(8,128)(2,1)} %param.13) | copy-start | bytes 1769476
  93.6 34.2 %copy-start.3 = (bf16[1,1,4,72,1024]{4,3,2,1,0:T(8,128)(2,1)S(1)}, bf16[1,1,4,72,1024]{4,3,2,1,0:T(8,128)(2,1)}, u32[]{:S(2)}) copy-start(bf16[1,1,4,72,1024]{4,3,2,1,0:T(8,128)(2,1)} %param.14) | copy-start | bytes 1769476
  93.6 70.0 %all-to-all-start.2 = ((bf16[48,80,128]{2,1,0:T(8,128)(2,1)}), bf16[48,80,128]{2,1,0:T(8,128)(2,1)S(1)}, u32[]{:S(2)}, u32[]{:S(2)}) async-start(bf16[48,80,128]{2,1,0:T(8,128)(2,1)} %bitcast.27), calls=%async_computation.2 | async-start | bytes 1966080 | tf_op jit(solution)/shard_map/all_to_all | solution.py:270
  127.8 1.5 copy-start.5
  129.4 1.5 copy-start.6
  130.9 17.0 %copy-start.11 = (s32[128,2]{0,1:T(2,128)S(1)}, s32[128,2]{0,1:T(2,128)}, u32[]{:S(2)}) copy-start(s32[128,2]{0,1:T(2,128)} %param.10) | copy-start | bytes 3076
  130.9 17.0 %copy-start.13 = (bf16[128,2]{0,1:T(2,128)(2,1)S(1)}, bf16[128,2]{0,1:T(2,128)(2,1)}, u32[]{:S(2)}) copy-start(bf16[128,2]{0,1:T(2,128)(2,1)} %param.11) | copy-start | bytes 1540
  134.7 9.4 %collective-permute-start.8 = (bf16[72,1024]{1,0:T(8,128)(2,1)S(1)}, bf16[72,1024]{1,0:T(8,128)(2,1)S(1)}, u32[]{:S(2)}, u32[]{:S(2)}) collective-permute-start(bf16[72,1024]{1,0:T(8,128)(2,1)S(1)} %get-tuple-element.34), channel_id=1, source_target_pairs={{0,3},{1,2},{2,1},{3,0},{4,7},{5,6},{6,5},{7,4},{8,11},{9,10},{10,... | collective-permute-start | bytes 442376 | tf_op jit(solution)/shard_map/ppermute | solution.py:297
  136.6 11.2 %collective-permute-start.7 = (bf16[72,1024]{1,0:T(8,128)(2,1)S(1)}, bf16[72,1024]{1,0:T(8,128)(2,1)S(1)}, u32[]{:S(2)}, u32[]{:S(2)}) collective-permute-start(bf16[72,1024]{1,0:T(8,128)(2,1)S(1)} %get-tuple-element.35), channel_id=1, source_target_pairs={{0,2},{1,3},{2,0},{3,1},{4,6},{5,7},{6,4},{7,5},{8,10},{9,11},{10,... | collective-permute-start | bytes 442376 | tf_op jit(solution)/shard_map/ppermute | solution.py:297
  140.4 7.5 %collective-permute-start.6 = (bf16[72,1024]{1,0:T(8,128)(2,1)S(1)}, bf16[72,1024]{1,0:T(8,128)(2,1)S(1)}, u32[]{:S(2)}, u32[]{:S(2)}) collective-permute-start(bf16[72,1024]{1,0:T(8,128)(2,1)S(1)} %get-tuple-element.36), channel_id=1, source_target_pairs={{0,1},{1,0},{2,3},{3,2},{4,5},{5,4},{6,7},{7,6},{8,9},{9,8},{10,11... | collective-permute-start | bytes 442376 | tf_op jit(solution)/shard_map/ppermute | solution.py:297
Sparse Core Ops, SparseCore 0:
  17.2 48.6 all-gather.4

commit v3 on v2

--- a/solution.py
+++ b/solution.py
@@ -49,64 +49,64 @@
     out_ref[0] = jnp.dot(rows_ref[...], down_ref[...], preferred_element_type=F32).astype(BF)
 
 
+def factors(g, u):
+    sig = 1.0 / (1.0 + jnp.exp(-g))
+    return u * sig * (1.0 + g * (1.0 - sig)), g * sig
+
+
+def early_kernel(n_y, place_ref, x_ref, out_ref):
+    y = place_ref[0]
+    feat = x_ref.shape[1]
+    part = feat // n_y
+    at = lax.broadcasted_iota(jnp.int32, (part, feat), 1) - lax.broadcasted_iota(
+        jnp.int32, (part, feat), 0
+    )
+    x = x_ref[...]
+    for k in range(n_y):
+        first = jnp.bitwise_and(y + k, n_y - 1) * part
+        chosen = jnp.where(at == first, 1.0, 0.0).astype(BF)
+        out_ref[k] = lax.dot_general(
+            chosen, x, (((1,), (1,)), ((), ())), preferred_element_type=F32
+        ).astype(BF)
+
+
+def share_kernel(place_ref, parts_ref, gate_ref, up_ref, raw_ref, delta_ref):
+    quarter = raw_ref.shape[1]
+    raw = parts_ref[0].astype(F32)
+    for i in range(1, parts_ref.shape[0]):
+        raw = raw + parts_ref[i].astype(F32)
+    raw_ref[...] = raw.astype(BF)
+    here = pl.ds(pl.multiple_of(place_ref[1] * quarter, quarter), quarter)
+    for_gate, for_up = factors(gate_ref[:, here].astype(F32), up_ref[:, here].astype(F32))
+    gate_delta = (raw * for_gate).astype(BF)
+    up_delta = (raw * for_up).astype(BF)
+    for k in range(delta_ref.shape[0]):
+        delta_ref[k, :, :quarter] = gate_delta
+        delta_ref[k, :, quarter:] = up_delta
+
+
+def grads_kernel(own, place_ref, delta_ref, x_ref, out_ref, ordered):
+    n_y, slots, _ = delta_ref.shape
+    for k in range(n_y):
+        copy = jnp.bitwise_and(place_ref[0] + n_y - k, n_y - 1)
+        ordered[k * slots : (k + 1) * slots] = delta_ref[copy]
+    d = ordered[...]
+    n_zl, n_zh, n_node = out_ref.shape[:3]
+    for b in range(n_node):
+        res = jnp.dot(x_ref[b], d, preferred_element_type=F32)
+        for i in range(n_zh * n_zl):
+            piece = res[i * own : (i + 1) * own]
+            tall = jnp.concatenate(
+                [piece[:, c * 128 : (c + 1) * 128] for c in range(piece.shape[1] // 128)], axis=0
+            )
+            out_ref[i % n_zl, i // n_zl, b] = tall.astype(BF)
+
+
 def sum_kernel(parts_ref, out_ref):
     total = parts_ref[0].astype(F32)
     for i in range(1, parts_ref.shape[0]):
         total = total + parts_ref[i].astype(F32)
     out_ref[...] = total.astype(BF)
-
-
-def factors(g, u):
-    sig = 1.0 / (1.0 + jnp.exp(-g))
-    return u * sig * (1.0 + g * (1.0 - sig)), g * sig
-
-
-def early_kernel(own, n_zl, place_ref, x_ref, gate_ref, up_ref, slab_ref, fact_ref):
-    zl, node = place_ref[0], place_ref[1]
-    feat = x_ref.shape[1]
-    part = feat // n_zl
-    quarter = fact_ref.shape[1] // 2
-    at = lax.broadcasted_iota(jnp.int32, (part, 1), 0)
-    group = jnp.floor((at.astype(F32) + 0.5) * (1.0 / own)).astype(jnp.int32)
-    cols = lax.broadcasted_iota(jnp.int32, (part, feat), 1)
-    x = x_ref[...]
-    for k in range(n_zl):
-        to = jnp.bitwise_and(zl + k, n_zl - 1)
-        wanted = (group * n_zl + to) * own + (at - group * own)
-        chosen = jnp.where(cols == wanted, 1.0, 0.0).astype(BF)
-        slab_ref[k] = lax.dot_general(
-            chosen, x, (((1,), (1,)), ((), ())), preferred_element_type=F32
-        ).astype(BF)
-    here = pl.ds(pl.multiple_of(node * quarter, quarter), quarter)
-    for_gate, for_up = factors(gate_ref[:, here].astype(F32), up_ref[:, here].astype(F32))
-    fact_ref[:, :quarter] = for_gate.astype(BF)
-    fact_ref[:, quarter:] = for_up.astype(BF)
-
-
-def grads_kernel(own, place_ref, raw_ref, fact_ref, *rest):
-    x_refs, (out_ref, keep_ref, delta) = rest[:-3], rest[-3:]
-    zl, node = place_ref[0], place_ref[1]
-    n_zl, slots, quarter = raw_ref.shape
-    for k in range(n_zl):
-        copy = jnp.bitwise_and(zl + n_zl - k, n_zl - 1)
-        raw = raw_ref[copy].astype(F32)
-        fact = fact_ref[copy].astype(F32)
-        if k == 0:
-            keep_ref[...] = raw_ref[copy]
-        rows = slice(k * slots, (k + 1) * slots)
-        delta[rows, :quarter] = (raw * fact[:, :quarter]).astype(BF)
-        delta[rows, quarter:] = (raw * fact[:, quarter:]).astype(BF)
-    d = delta[...]
-    n_node = len(x_refs)
-    for k in range(n_node):
-        block = jnp.bitwise_and(node + n_node - k, n_node - 1)
-        res = jnp.dot(x_refs[k][...], d, preferred_element_type=F32)
-        for i in range(out_ref.shape[0]):
-            piece = res[i * own : (i + 1) * own]
-            tall = jnp.concatenate(
-                [piece[:, c * 128 : (c + 1) * 128] for c in range(piece.shape[1] // 128)], axis=0
-            )
-            out_ref[i, block] = tall.astype(BF)
 
 
 def input_kernel(capacity, place_ref, raw_ref, gate_ref, up_ref, wg_ref, wu_ref, out_ref, total, side):
@@ -200,9 +200,9 @@
     quarter = hidden // n_node
     slots = n_local * capacity
     own = feat // n_copies
-    part = feat // n_zl
+    part = feat // n_y
     wide = -(-(feat + 1) // 128) * 128
-    place = jnp.stack([lax.axis_index(a) for a in ("zl", "node", "local")]).astype(jnp.int32)
+    place = jnp.stack([lax.axis_index(a) for a in ("y", "node", "local")]).astype(jnp.int32)
     gate_rows = gate_pre.reshape(slots, hidden)
     up_rows = up_pre.reshape(slots, hidden)
     x_rows = expert_inputs.reshape(slots, feat)
@@ -216,18 +216,14 @@
     arrived = lax.all_to_all(outgoing, "local", split_axis=0, concat_axis=0, tiled=True)
 
     x_rows, _ = lax.optimization_barrier((x_rows, outgoing))
-    slabs, facts = pl.pallas_call(
-        functools.partial(early_kernel, own, n_zl),
-        in_specs=[SMEM, VMEM, VMEM, VMEM],
-        out_shape=[
-            jax.ShapeDtypeStruct((n_zl, part, slots), BF),
-            jax.ShapeDtypeStruct((slots, 2 * quarter), BF),
-        ],
+    slabs = pl.pallas_call(
+        functools.partial(early_kernel, n_y),
+        in_specs=[SMEM, VMEM],
+        out_shape=jax.ShapeDtypeStruct((n_y, part, slots), BF),
         compiler_params=params(),
         name="early",
-    )(place, x_rows, gate_rows, up_rows)
-    all_facts = lax.all_gather(facts, "zl", axis=0, tiled=False)
-    copies_x = [slabs[0]] + [ring(slabs[k], "zl", k) for k in range(1, n_zl)]
+    )(place, x_rows)
+    copies_x = [slabs[0]] + [ring(slabs[k], "y", k) for k in range(1, n_y)]
 
     raw_parts = pl.pallas_call(
         raw_kernel,
@@ -243,39 +239,22 @@
     )(arrived.reshape(slots, feat), w_down[0].T)
     raw_shares = lax.all_to_all(raw_parts, "node", split_axis=0, concat_axis=0, tiled=True)
 
-    *copies_x, _ = lax.optimization_barrier((*copies_x, raw_parts))
-    own_x = jnp.concatenate(copies_x, axis=1)
-    node_x = [own_x] + [ring(own_x, "node", k) for k in range(1, n_node)]
-
-    raw_share = pl.pallas_call(
-        sum_kernel,
-        out_shape=jax.ShapeDtypeStruct((slots, quarter), BF),
+    *copies_x, raw_shares = lax.optimization_barrier((*copies_x, raw_shares))
+    node_x = lax.all_gather(jnp.concatenate(copies_x, axis=1), "node", axis=0, tiled=False)
+
+    raw_share, deltas = pl.pallas_call(
+        share_kernel,
+        in_specs=[SMEM, VMEM, VMEM, VMEM],
+        out_shape=[
+            jax.ShapeDtypeStruct((slots, quarter), BF),
+            jax.ShapeDtypeStruct((n_y, slots, 2 * quarter), BF),
+        ],
         compiler_params=params(),
         name="share",
-    )(raw_shares)
-    raw_copies = lax.all_gather(raw_share, "zl", axis=0, tiled=False)
-
-    tall = own * 2 * quarter // 128
-    grads, kept = pl.pallas_call(
-        functools.partial(grads_kernel, own),
-        in_specs=[SMEM] + [VMEM] * (2 + n_node),
-        out_shape=[
-            jax.ShapeDtypeStruct((n_y * n_zh, n_node, tall, 128), BF),
-            jax.ShapeDtypeStruct((slots, quarter), BF),
-        ],
-        scratch_shapes=[pltpu.VMEM((n_zl * slots, 2 * quarter), BF)],
-        compiler_params=params(),
-        name="grads",
-    )(place, raw_copies, all_facts, *node_x)
-    parts = lax.all_to_all(
-        grads.reshape(n_y * n_zh * n_node, tall, 128),
-        ("y", "zh", "node"),
-        split_axis=0,
-        concat_axis=0,
-        tiled=True,
-    )
-
-    raw = lax.all_gather(kept, "node", axis=0, tiled=False)
+    )(place, raw_shares, gate_rows, up_rows)
+    all_deltas = lax.all_to_all(deltas, "y", split_axis=0, concat_axis=0, tiled=True)
+
+    raw = lax.all_gather(raw_share, "node", axis=0, tiled=False)
     slot_input = pl.pallas_call(
         functools.partial(input_kernel, capacity),
         grid=(n_node,),
@@ -293,6 +272,18 @@
         compiler_params=params(),
         name="slot_input",
     )(place, raw, gate_rows, up_rows, w_gate[0], w_up[0])
+    all_deltas, slot_input = lax.optimization_barrier((all_deltas, slot_input))
+
+    tall = own * 2 * quarter // 128
+    grads = pl.pallas_call(
+        functools.partial(grads_kernel, own),
+        in_specs=[SMEM, VMEM, VMEM],
+        out_shape=jax.ShapeDtypeStruct((n_zl, n_zh, n_node, tall, 128), BF),
+        scratch_shapes=[pltpu.VMEM((n_y * slots, 2 * quarter), BF)],
+        compiler_params=params(),
+        name="grads",
+    )(place, all_deltas, node_x)
+    near = lax.all_to_all(grads, "zl", split_axis=0, concat_axis=0, tiled=True)
     back = [slot_input[0]] + [
         lax.ppermute(slot_input[k], "local", [(i, i ^ k) for i in range(n_local)])
         for k in range(1, n_local)
@@ -308,12 +299,27 @@
         name="combine",
     )(place, routes.T, gates.T, *back)
 
+    near, input_grads, gate_grads = lax.optimization_barrier((near, input_grads, gate_grads))
+    near_sum = pl.pallas_call(
+        sum_kernel,
+        out_shape=jax.ShapeDtypeStruct((n_zh, n_node, tall, 128), BF),
+        compiler_params=params(),
+        name="near_sum",
+    )(near)
+    parts = lax.all_to_all(
+        near_sum.reshape(n_zh * n_node, tall, 128),
+        ("zh", "node"),
+        split_axis=0,
+        concat_axis=0,
+        tiled=True,
+    )
+
     gate_sum, up_sum = pl.pallas_call(
         functools.partial(final_kernel, n_copies, own),
         out_shape=[jax.ShapeDtypeStruct((own, hidden // 128, 128), F32)] * 2,
         compiler_params=params(),
         name="final",
-    )(parts.reshape(n_y * n_zh, n_node, tall, 128))
+    )(parts.reshape(n_zh, n_node, tall, 128))
     rows = own * hidden // 128
     return (
         input_grads.T,

time: 173 us -> 171 us (0.988)
  waiting for transfers between devices: 22.7 us -> 50.8 us
  starting transfers between devices: 69.5 us -> 42.6 us
  local copies, waits for them, and re-layouts: 11.2 us -> 8.46 us
    all_gather x2 -> x1, blocking collectives: 37 us -> 13.4 us  [local(): raw = lax.all_gather(raw_share, 'node', axis=0, tiled=False)]
    all_to_all x0 -> x1, blocking collectives: none -> 22.7 us  [local(): lax.all_to_all(near_sum.reshape(n_zh * n_node, tall, 128), ('zh', 'node')...]
    ppermute x6 -> x3, starting transfers between devices: 28.9 us -> 10 us  [ring(): return lax.ppermute(x, axis, [(i, (i + step) % n) for i in range(n)])]
    ppermute x6 -> x3, waiting for transfers between devices: 3.64 us -> 15.7 us  [ring(): return lax.ppermute(x, axis, [(i, (i + step) % n) for i in range(n)])]
    all_to_all x1 -> x2, starting transfers between devices: 20.1 us -> 8.65 us  [the longest x1 5.12 us: local(): near = lax.all_to_all(grads, 'zl', split_axis=0, concat_axis=0, tiled=True)]
    all_to_all x1, waiting for transfers between devices: 0.01 us -> 9.51 us  [local(): lax.all_to_all(outgoing, 'local', split_axis=0, concat_axis=0, tiled=True)]
    all_to_all x1 -> x2, waiting for transfers between devices: 13.5 us -> 17.9 us  [the longest x1 9.02 us: local(): near = lax.all_to_all(grads, 'zl', split_axis=0, concat_axis=0, tiled=True)]
    all_to_all x1, starting transfers between devices: 9.3 us -> 12.9 us  [local(): lax.all_to_all(raw_parts, 'node', split_axis=0, concat_axis=0, tiled=True)]
  transfers between devices with their start and end apart: 13 -> 11, of which waited for: 4 -> 8; matrix products, arithmetic and copies ran while one was open for 1% -> 0% of each run, Pallas kernels for 5% -> 6%
where the time goes in v3:
time: 171 us; the launch traced here: 170 us
  waiting for transfers between devices  50.8 us (30%)
  starting transfers between devices  42.6 us (25%)
  blocking collectives  36.1 us (21%)
  Pallas kernels  17.5 us (10%)
  between operations  14.2 us (8%)
  local copies, waits for them, and re-layouts  8.46 us (5%)
    all_to_all x1, blocking collectives, local(): lax.all_to_all(near_sum.reshape(n_zh * n_node, tall, 128), ('zh', 'node')...  22.7 us
    ppermute x3, waiting for transfers between devices, ring(): return lax.ppermute(x, axis, [(i, (i + step) % n) for i in range(n)])  15.7 us
    all_gather x1, blocking collectives, local(): raw = lax.all_gather(raw_share, 'node', axis=0, tiled=False)  13.4 us
    all_to_all x1, starting transfers between devices, local(): lax.all_to_all(raw_parts, 'node', split_axis=0, concat_axis=0, tiled=True)  12.9 us
    ppermute x3, starting transfers between devices, ring(): return lax.ppermute(x, axis, [(i, (i + step) % n) for i in range(n)])  10 us
    all_to_all x1, waiting for transfers between devices, local(): lax.all_to_all(outgoing, 'local', split_axis=0, concat_axis=0, tiled=True)  9.51 us
    all_to_all x1, waiting for transfers between devices, local(): near = lax.all_to_all(grads, 'zl', split_axis=0, concat_axis=0, tiled=True)  9.02 us
    all_to_all x1, waiting for transfers between devices, local(): lax.all_to_all(deltas, 'y', split_axis=0, concat_axis=0, tiled=True)  8.84 us
  transfers between devices with their start and end apart: 11, of which 8 were waited for; matrix products, arithmetic and copies ran while one was open for 0% of the time, Pallas kernels for 6%

profile of v3, /device:TPU:6, one launch (start us, length us, event | category | flops | bytes accessed | tf_op | source)
XLA Modules:
  0.0 169.8 jit_solution(1585289853932390077)
XLA Ops:
  7.2 1.1 copy-done.7
  9.6 1.7 dispatch.1
  11.3 3.5 %all-to-all-start = ((bf16[4,72,960]{2,1,0:T(8,128)(2,1)}), bf16[4,72,960]{2,1,0:T(8,128)(2,1)S(1)}, u32[]{:S(2)}, u32[]{:S(2)}) async-start(bf16[4,72,960]{2,1,0:T(8,128)(2,1)} %dispatch.1), calls=%async_computation | async-start | bytes 1179648 | tf_op jit(solution)/shard_map/all_to_all | solution.py:216
  14.8 9.5 %all-to-all-done = bf16[4,72,960]{2,1,0:T(8,128)(2,1)S(1)} async-done(((bf16[4,72,960]{2,1,0:T(8,128)(2,1)}), bf16[4,72,960]{2,1,0:T(8,128)(2,1)S(1)}, u32[]{:S(2)}, u32[]{:S(2)}) %all-to-all-start) | async-done | bytes 552992 | tf_op jit(solution)/shard_map/all_to_all | solution.py:216
  24.3 2.5 %raw.1 = bf16[4,288,256]{2,1,0:T(8,128)(2,1)} custom-call(bf16[288,960]{1,0:T(8,128)(2,1)S(1)} %bitcast.44, bf16[960,1024]{1,0:T(8,128)(2,1)S(1)} %bitcast.46), custom_call_target="tpu_custom_call" | custom-call | tf_op jit(solution)/shard_map/raw/pallas_call | solution.py:228
  26.8 12.9 %all-to-all-start.1 = ((bf16[4,288,256]{2,1,0:T(8,128)(2,1)}), bf16[4,288,256]{2,1,0:T(8,128)(2,1)S(1)}, u32[]{:S(2)}, u32[]{:S(2)}) async-start(bf16[4,288,256]{2,1,0:T(8,128)(2,1)} %raw.1), calls=%async_computation.1 | async-start | bytes 1179648 | tf_op jit(solution)/shard_map/all_to_all | solution.py:240
  39.8 1.7 %early.1 = bf16[4,240,288]{2,1,0:T(8,128)(2,1)S(1)} custom-call(s32[3]{0:T(128)S(1)} %pad_add_fusion.place_ref, bf16[288,960]{1,0:T(8,128)(2,1)S(1)} %bitcast.51), custom_call_target="tpu_custom_call" | custom-call | tf_op jit(solution)/shard_map/early/pallas_call | solution.py:219
  41.7 2.1 %collective-permute-start = (bf16[240,288]{1,0:T(8,128)(2,1)S(1)}, bf16[240,288]{1,0:T(8,128)(2,1)S(1)}, u32[]{:S(2)}, u32[]{:S(2)}) collective-permute-start(bf16[240,288]{1,0:T(8,128)(2,1)S(1)} %get-tuple-element.40), channel_id=1, source_target_pairs={{0,192},{192,384},{384,576},{576,0},{1,193},{193,385},{385,577},{5... | collective-permute-start | bytes 414728 | tf_op jit(solution)/shard_map/ppermute | solution.py:184
  43.7 1.9 %collective-permute-start.1 = (bf16[240,288]{1,0:T(8,128)(2,1)S(1)}, bf16[240,288]{1,0:T(8,128)(2,1)S(1)}, u32[]{:S(2)}, u32[]{:S(2)}) collective-permute-start(bf16[240,288]{1,0:T(8,128)(2,1)S(1)} %get-tuple-element.39), channel_id=1, source_target_pairs={{0,384},{192,576},{384,0},{576,192},{1,385},{193,577},{385,1},{577... | collective-permute-start | bytes 414728 | tf_op jit(solution)/shard_map/ppermute | solution.py:184
  45.6 6.0 %collective-permute-start.2 = (bf16[240,288]{1,0:T(8,128)(2,1)S(1)}, bf16[240,288]{1,0:T(8,128)(2,1)S(1)}, u32[]{:S(2)}, u32[]{:S(2)}) collective-permute-start(bf16[240,288]{1,0:T(8,128)(2,1)S(1)} %get-tuple-element.38), channel_id=1, source_target_pairs={{0,576},{192,0},{384,192},{576,384},{1,577},{193,1},{385,193},{577... | collective-permute-start | bytes 414728 | tf_op jit(solution)/shard_map/ppermute | solution.py:184
  51.7 5.7 %collective-permute-done = bf16[240,288]{1,0:T(8,128)(2,1)S(1)} collective-permute-done((bf16[240,288]{1,0:T(8,128)(2,1)S(1)}, bf16[240,288]{1,0:T(8,128)(2,1)S(1)}, u32[]{:S(2)}, u32[]{:S(2)}) %collective-permute-start) | collective-permute-done | bytes 138272 | tf_op jit(solution)/shard_map/ppermute | solution.py:184
  57.4 10.0 %collective-permute-done.2 = bf16[240,288]{1,0:T(8,128)(2,1)S(1)} collective-permute-done((bf16[240,288]{1,0:T(8,128)(2,1)S(1)}, bf16[240,288]{1,0:T(8,128)(2,1)S(1)}, u32[]{:S(2)}, u32[]{:S(2)}) %collective-permute-start.2) | collective-permute-done | bytes 138272 | tf_op jit(solution)/shard_map/ppermute | solution.py:184
  67.4 1.2 concatenate.3
  68.6 1.8 %share.1 = (bf16[288,256]{1,0:T(8,128)(2,1)S(1)}, bf16[4,288,512]{2,1,0:T(8,128)(2,1)}) custom-call(s32[3]{0:T(128)S(1)} %pad_add_fusion.place_ref, bf16[4,288,256]{2,1,0:T(8,128)(2,1)S(1)} %all-to-all-done.1.parts_ref, bf16[288,1024]{1,0:T(8,128)(2,1)S(1)} %bitcast.40, bf16[288,1024]{1,0:T(8,128)(2,1)S(1)} %bitcast.42), custom_call_target="tpu_custom_call" | custom-call | tf_op jit(solution)/shard_map/share/pallas_call | solution.py:245
  70.4 3.5 %all-to-all-start.2 = ((bf16[4,288,512]{2,1,0:T(8,128)(2,1)}), bf16[4,288,512]{2,1,0:T(8,128)(2,1)S(1)}, u32[]{:S(2)}, u32[]{:S(2)}) async-start(bf16[4,288,512]{2,1,0:T(8,128)(2,1)} %get-tuple-element.23), calls=%async_computation.2 | async-start | bytes 2359296 | tf_op jit(solution)/shard_map/all_to_all | solution.py:255
  74.0 13.4 %all-gather = bf16[1152,256]{1,0:T(8,128)(2,1)S(1)} all-gather(bf16[288,256]{1,0:T(8,128)(2,1)S(1)} %get-tuple-element.24), channel_id=2, replica_groups=mesh['y'=4,'zh'=3,'zl'=4,'node'=4,'local'=4] {'node'}, dimensions={0}, use_global_device_ids=true | all-gather | bytes 737280 | tf_op jit(solution)/shard_map/all_gather | solution.py:257
  87.4 1.5 copy-done.4
  88.9 1.6 copy-done.5
  90.5 3.8 %slot_input.1 = bf16[4,72,1024]{2,1,0:T(8,128)(2,1)S(1)} custom-call(s32[3]{0:T(128)S(1)} %pad_add_fusion.place_ref, bf16[4,288,256]{2,1,0:T(8,128)(2,1)S(1)} %bitcast.39, bf16[288,1024]{1,0:T(8,128)(2,1)S(1)} %bitcast.41, bf16[288,1024]{1,0:T(8,128)(2,1)S(1)} %bitcast.43, bf16[960,1024]{1,0:T(8,128)(2,1)S(1)} %bitcast.47, bf16[960,1024]{1,0:T(8,128)(2,1)S(1)} %bitcast.48), custom_call_target="tpu_custom_call" | custom-call | tf_op jit(solution)/shard_map/slot_input/pallas_call | solution.py:258
  94.2 8.8 %all-to-all-done.2.delta_ref = bf16[4,288,512]{2,1,0:T(8,128)(2,1)S(1)} async-done(((bf16[4,288,512]{2,1,0:T(8,128)(2,1)}), bf16[4,288,512]{2,1,0:T(8,128)(2,1)S(1)}, u32[]{:S(2)}, u32[]{:S(2)}) %all-to-all-start.2) | async-done | bytes 1179680 | tf_op jit(solution)/shard_map/all_to_all | solution.py:255
  103.1 2.2 %all-gather.4.cloned.1.call-done = bf16[960,1152]{1,0:T(8,128)(2,1)} async-done(((bf16[240,1152]{1,0:T(8,128)(2,1)}), bf16[960,1152]{1,0:T(8,128)(2,1)}) %all-gather.4.cloned.1.call-update) | async-done | bytes 2211856 | tf_op jit(solution)/shard_map/all_gather | solution.py:243
  105.3 1.6 copy-done.2
  106.9 2.9 %grads.1 = bf16[4,3,4,80,128]{4,3,2,1,0:T(8,128)(2,1)} custom-call(s32[3]{0:T(128)S(1)} %pad_add_fusion.place_ref, bf16[4,288,512]{2,1,0:T(8,128)(2,1)S(1)} %all-to-all-done.2.delta_ref, bf16[4,240,1152]{2,1,0:T(8,128)(2,1)S(1)} %bitcast.45), custom_call_target="tpu_custom_call" | custom-call | tf_op jit(solution)/shard_map/grads/pallas_call | solution.py:278
  109.9 5.1 %all-to-all-start.3 = ((bf16[4,3,4,80,128]{4,3,2,1,0:T(8,128)(2,1)}), bf16[4,3,4,80,128]{4,3,2,1,0:T(8,128)(2,1)S(1)}, u32[]{:S(2)}, u32[]{:S(2)}) async-start(bf16[4,3,4,80,128]{4,3,2,1,0:T(8,128)(2,1)} %grads.1), calls=%async_computation.3 | async-start | bytes 1966080 | tf_op jit(solution)/shard_map/all_to_all | solution.py:286
  115.0 1.9 %collective-permute-start.3 = (bf16[72,1024]{1,0:T(8,128)(2,1)S(1)}, bf16[72,1024]{1,0:T(8,128)(2,1)S(1)}, u32[]{:S(2)}, u32[]{:S(2)}) collective-permute-start(bf16[72,1024]{1,0:T(8,128)(2,1)S(1)} %get-tuple-element.44), channel_id=1, source_target_pairs={{0,1},{1,0},{2,3},{3,2},{4,5},{5,4},{6,7},{7,6},{8,9},{9,8},{10,11... | collective-permute-start | bytes 442376 | tf_op jit(solution)/shard_map/ppermute | solution.py:288
  117.0 3.4 %collective-permute-start.4 = (bf16[72,1024]{1,0:T(8,128)(2,1)S(1)}, bf16[72,1024]{1,0:T(8,128)(2,1)S(1)}, u32[]{:S(2)}, u32[]{:S(2)}) collective-permute-start(bf16[72,1024]{1,0:T(8,128)(2,1)S(1)} %get-tuple-element.43), channel_id=1, source_target_pairs={{0,2},{1,3},{2,0},{3,1},{4,6},{5,7},{6,4},{7,5},{8,10},{9,11},{10,... | collective-permute-start | bytes 442376 | tf_op jit(solution)/shard_map/ppermute | solution.py:288
  120.4 2.3 %collective-permute-start.5 = (bf16[72,1024]{1,0:T(8,128)(2,1)S(1)}, bf16[72,1024]{1,0:T(8,128)(2,1)S(1)}, u32[]{:S(2)}, u32[]{:S(2)}) collective-permute-start(bf16[72,1024]{1,0:T(8,128)(2,1)S(1)} %get-tuple-element.42), channel_id=1, source_target_pairs={{0,3},{1,2},{2,1},{3,0},{4,7},{5,6},{6,5},{7,4},{8,11},{9,10},{10,... | collective-permute-start | bytes 442376 | tf_op jit(solution)/shard_map/ppermute | solution.py:288
  122.7 2.5 %collective-permute-done.4.rest_2_ = bf16[72,1024]{1,0:T(8,128)(2,1)S(1)} collective-permute-done((bf16[72,1024]{1,0:T(8,128)(2,1)S(1)}, bf16[72,1024]{1,0:T(8,128)(2,1)S(1)}, u32[]{:S(2)}, u32[]{:S(2)}) %collective-permute-start.4) | collective-permute-done | bytes 147488 | tf_op jit(solution)/shard_map/ppermute | solution.py:288
  125.1 3.0 %collective-permute-done.5.rest_3_ = bf16[72,1024]{1,0:T(8,128)(2,1)S(1)} collective-permute-done((bf16[72,1024]{1,0:T(8,128)(2,1)S(1)}, bf16[72,1024]{1,0:T(8,128)(2,1)S(1)}, u32[]{:S(2)}, u32[]{:S(2)}) %collective-permute-start.5) | collective-permute-done | bytes 147488 | tf_op jit(solution)/shard_map/ppermute | solution.py:288
  128.1 2.2 %combine.1 = (bf16[960,128]{1,0:T(8,128)(2,1)}, bf16[2,128]{1,0:T(2,128)(2,1)}) custom-call(s32[3]{0:T(128)S(1)} %pad_add_fusion.place_ref, s32[2,128]{1,0:T(2,128)S(1)} %bitcast.54, bf16[2,128]{1,0:T(2,128)(2,1)S(1)} %bitcast.56, bf16[72,1024]{1,0:T(8,128)(2,1)S(1)} %get-tuple-element.45.rest_0_, bf16[72,1024]{1,0:T(8,128)(2,1)S(1)} %collective-permute-done.3.rest_1_, ...), custom_call_target="tpu_custom_call" | custom-call | tf_op jit(solution)/shard_map/combine/pallas_call | solution.py:291
  130.3 9.0 %all-to-all-done.3.parts_ref = bf16[4,3,4,80,128]{4,3,2,1,0:T(8,128)(2,1)S(1)} async-done(((bf16[4,3,4,80,128]{4,3,2,1,0:T(8,128)(2,1)}), bf16[4,3,4,80,128]{4,3,2,1,0:T(8,128)(2,1)S(1)}, u32[]{:S(2)}, u32[]{:S(2)}) %all-to-all-start.3) | async-done | bytes 983072 | tf_op jit(solution)/shard_map/all_to_all | solution.py:286
  139.5 22.7 %all_to_all.25 = bf16[12,80,128]{2,1,0:T(8,128)(2,1)S(1)} all-to-all(bf16[12,80,128]{2,1,0:T(8,128)(2,1)S(1)} %bitcast.49), channel_id=1, replica_groups=mesh['y'=4,'zh'=3,'zl'=4,'node'=4,'local'=4] {'zh','node'}, dimensions={0} | all-to-all | bytes 491520 | tf_op jit(solution)/shard_map/all_to_all | solution.py:309
  (30 shorter events, 2.5 us)
Async XLA Ops:
  7.2 17.1 %copy-start.3 = (bf16[1,1024,960]{1,2,0:T(8,128)(2,1)S(1)}, bf16[1,1024,960]{1,2,0:T(8,128)(2,1)}, u32[]{:S(2)}) copy-start(bf16[1,1024,960]{1,2,0:T(8,128)(2,1)} %param.17) | copy-start | bytes 5898244
  7.2 1.1 copy-start.7
  8.3 0.7 copy-start.8
  8.9 0.7 copy-start.10
  11.3 13.0 %all-to-all-start = ((bf16[4,72,960]{2,1,0:T(8,128)(2,1)}), bf16[4,72,960]{2,1,0:T(8,128)(2,1)S(1)}, u32[]{:S(2)}, u32[]{:S(2)}) async-start(bf16[4,72,960]{2,1,0:T(8,128)(2,1)} %dispatch.1), calls=%async_computation | async-start | bytes 1179648 | tf_op jit(solution)/shard_map/all_to_all | solution.py:216
  24.3 15.5 %copy-start.6 = (bf16[1,1,4,72,960]{4,3,2,1,0:T(8,128)(2,1)S(1)}, bf16[1,1,4,72,960]{4,3,2,1,0:T(8,128)(2,1)}, u32[]{:S(2)}) copy-start(bf16[1,1,4,72,960]{4,3,2,1,0:T(8,128)(2,1)} %param.12) | copy-start | bytes 1658884
  26.8 40.6 %all-to-all-start.1 = ((bf16[4,288,256]{2,1,0:T(8,128)(2,1)}), bf16[4,288,256]{2,1,0:T(8,128)(2,1)S(1)}, u32[]{:S(2)}, u32[]{:S(2)}) async-start(bf16[4,288,256]{2,1,0:T(8,128)(2,1)} %raw.1), calls=%async_computation.1 | async-start | bytes 1179648 | tf_op jit(solution)/shard_map/all_to_all | solution.py:240
  39.7 65.6 %all-gather.4.cloned.1.call-start = ((), (), s32[]{:S(2)}) async-start(), calls=%async_computation.5 | async-start | bytes 2764800 | tf_op jit(solution)/shard_map/all_gather | solution.py:243
  41.5 27.1 %copy-start = (bf16[1,1,4,72,1024]{4,3,2,1,0:T(8,128)(2,1)S(1)}, bf16[1,1,4,72,1024]{4,3,2,1,0:T(8,128)(2,1)}, u32[]{:S(2)}) copy-start(bf16[1,1,4,72,1024]{4,3,2,1,0:T(8,128)(2,1)} %param.13) | copy-start | bytes 1769476
  41.6 27.1 %copy-start.1 = (bf16[1,1,4,72,1024]{4,3,2,1,0:T(8,128)(2,1)S(1)}, bf16[1,1,4,72,1024]{4,3,2,1,0:T(8,128)(2,1)}, u32[]{:S(2)}) copy-start(bf16[1,1,4,72,1024]{4,3,2,1,0:T(8,128)(2,1)} %param.14) | copy-start | bytes 1769476
  41.7 15.8 %collective-permute-start = (bf16[240,288]{1,0:T(8,128)(2,1)S(1)}, bf16[240,288]{1,0:T(8,128)(2,1)S(1)}, u32[]{:S(2)}, u32[]{:S(2)}) collective-permute-start(bf16[240,288]{1,0:T(8,128)(2,1)S(1)} %get-tuple-element.40), channel_id=1, source_target_pairs={{0,192},{192,384},{384,576},{576,0},{1,193},{193,385},{385,577},{5... | collective-permute-start | bytes 414728 | tf_op jit(solution)/shard_map/ppermute | solution.py:184
  43.7 13.7 %collective-permute-start.1 = (bf16[240,288]{1,0:T(8,128)(2,1)S(1)}, bf16[240,288]{1,0:T(8,128)(2,1)S(1)}, u32[]{:S(2)}, u32[]{:S(2)}) collective-permute-start(bf16[240,288]{1,0:T(8,128)(2,1)S(1)} %get-tuple-element.39), channel_id=1, source_target_pairs={{0,384},{192,576},{384,0},{576,192},{1,385},{193,577},{385,1},{577... | collective-permute-start | bytes 414728 | tf_op jit(solution)/shard_map/ppermute | solution.py:184
  45.6 21.7 %collective-permute-start.2 = (bf16[240,288]{1,0:T(8,128)(2,1)S(1)}, bf16[240,288]{1,0:T(8,128)(2,1)S(1)}, u32[]{:S(2)}, u32[]{:S(2)}) collective-permute-start(bf16[240,288]{1,0:T(8,128)(2,1)S(1)} %get-tuple-element.38), channel_id=1, source_target_pairs={{0,576},{192,0},{384,192},{576,384},{1,577},{193,1},{385,193},{577... | collective-permute-start | bytes 414728 | tf_op jit(solution)/shard_map/ppermute | solution.py:184
  70.4 32.6 %all-to-all-start.2 = ((bf16[4,288,512]{2,1,0:T(8,128)(2,1)}), bf16[4,288,512]{2,1,0:T(8,128)(2,1)S(1)}, u32[]{:S(2)}, u32[]{:S(2)}) async-start(bf16[4,288,512]{2,1,0:T(8,128)(2,1)} %get-tuple-element.23), calls=%async_computation.2 | async-start | bytes 2359296 | tf_op jit(solution)/shard_map/all_to_all | solution.py:255
  87.4 1.5 copy-start.4
  88.9 1.6 copy-start.5
  105.3 1.6 copy-start.2
  109.9 18.2 %copy-start.9 = (s32[128,2]{0,1:T(2,128)S(1)}, s32[128,2]{0,1:T(2,128)}, u32[]{:S(2)}) copy-start(s32[128,2]{0,1:T(2,128)} %param.10) | copy-start | bytes 3076
  109.9 18.2 %copy-start.11 = (bf16[128,2]{0,1:T(2,128)(2,1)S(1)}, bf16[128,2]{0,1:T(2,128)(2,1)}, u32[]{:S(2)}) copy-start(bf16[128,2]{0,1:T(2,128)(2,1)} %param.11) | copy-start | bytes 1540
  109.9 29.4 %all-to-all-start.3 = ((bf16[4,3,4,80,128]{4,3,2,1,0:T(8,128)(2,1)}), bf16[4,3,4,80,128]{4,3,2,1,0:T(8,128)(2,1)S(1)}, u32[]{:S(2)}, u32[]{:S(2)}) async-start(bf16[4,3,4,80,128]{4,3,2,1,0:T(8,128)(2,1)} %grads.1), calls=%async_computation.3 | async-start | bytes 1966080 | tf_op jit(solution)/shard_map/all_to_all | solution.py:286
  115.0 7.6 %collective-permute-start.3 = (bf16[72,1024]{1,0:T(8,128)(2,1)S(1)}, bf16[72,1024]{1,0:T(8,128)(2,1)S(1)}, u32[]{:S(2)}, u32[]{:S(2)}) collective-permute-start(bf16[72,1024]{1,0:T(8,128)(2,1)S(1)} %get-tuple-element.44), channel_id=1, source_target_pairs={{0,1},{1,0},{2,3},{3,2},{4,5},{5,4},{6,7},{7,6},{8,9},{9,8},{10,11... | collective-permute-start | bytes 442376 | tf_op jit(solution)/shard_map/ppermute | solution.py:288
  117.0 8.1 %collective-permute-start.4 = (bf16[72,1024]{1,0:T(8,128)(2,1)S(1)}, bf16[72,1024]{1,0:T(8,128)(2,1)S(1)}, u32[]{:S(2)}, u32[]{:S(2)}) collective-permute-start(bf16[72,1024]{1,0:T(8,128)(2,1)S(1)} %get-tuple-element.43), channel_id=1, source_target_pairs={{0,2},{1,3},{2,0},{3,1},{4,6},{5,7},{6,4},{7,5},{8,10},{9,11},{10,... | collective-permute-start | bytes 442376 | tf_op jit(solution)/shard_map/ppermute | solution.py:288
  120.4 7.7 %collective-permute-start.5 = (bf16[72,1024]{1,0:T(8,128)(2,1)S(1)}, bf16[72,1024]{1,0:T(8,128)(2,1)S(1)}, u32[]{:S(2)}, u32[]{:S(2)}) collective-permute-start(bf16[72,1024]{1,0:T(8,128)(2,1)S(1)} %get-tuple-element.42), channel_id=1, source_target_pairs={{0,3},{1,2},{2,1},{3,0},{4,7},{5,6},{6,5},{7,4},{8,11},{9,10},{10,... | collective-permute-start | bytes 442376 | tf_op jit(solution)/shard_map/ppermute | solution.py:288
Sparse Core Ops, SparseCore 0:
  68.7 36.5 all-gather.3

commit v4 on v3

--- a/solution.py
+++ b/solution.py
@@ -13,7 +13,7 @@
 MIB = 1 << 20
 
 
-CUT = (4, 3, 4)
+CUT = (4, 12)
 
 
 def picks_of(routes, n_local, capacity, turn=None):
@@ -54,22 +54,6 @@
     return u * sig * (1.0 + g * (1.0 - sig)), g * sig
 
 
-def early_kernel(n_y, place_ref, x_ref, out_ref):
-    y = place_ref[0]
-    feat = x_ref.shape[1]
-    part = feat // n_y
-    at = lax.broadcasted_iota(jnp.int32, (part, feat), 1) - lax.broadcasted_iota(
-        jnp.int32, (part, feat), 0
-    )
-    x = x_ref[...]
-    for k in range(n_y):
-        first = jnp.bitwise_and(y + k, n_y - 1) * part
-        chosen = jnp.where(at == first, 1.0, 0.0).astype(BF)
-        out_ref[k] = lax.dot_general(
-            chosen, x, (((1,), (1,)), ((), ())), preferred_element_type=F32
-        ).astype(BF)
-
-
 def share_kernel(place_ref, parts_ref, gate_ref, up_ref, raw_ref, delta_ref):
     quarter = raw_ref.shape[1]
     raw = parts_ref[0].astype(F32)
@@ -80,33 +64,21 @@
     for_gate, for_up = factors(gate_ref[:, here].astype(F32), up_ref[:, here].astype(F32))
     gate_delta = (raw * for_gate).astype(BF)
     up_delta = (raw * for_up).astype(BF)
-    for k in range(delta_ref.shape[0]):
-        delta_ref[k, :, :quarter] = gate_delta
-        delta_ref[k, :, quarter:] = up_delta
-
-
-def grads_kernel(own, place_ref, delta_ref, x_ref, out_ref, ordered):
-    n_y, slots, _ = delta_ref.shape
-    for k in range(n_y):
-        copy = jnp.bitwise_and(place_ref[0] + n_y - k, n_y - 1)
-        ordered[k * slots : (k + 1) * slots] = delta_ref[copy]
-    d = ordered[...]
-    n_zl, n_zh, n_node = out_ref.shape[:3]
-    for b in range(n_node):
-        res = jnp.dot(x_ref[b], d, preferred_element_type=F32)
-        for i in range(n_zh * n_zl):
-            piece = res[i * own : (i + 1) * own]
-            tall = jnp.concatenate(
-                [piece[:, c * 128 : (c + 1) * 128] for c in range(piece.shape[1] // 128)], axis=0
-            )
-            out_ref[i % n_zl, i // n_zl, b] = tall.astype(BF)
-
-
-def sum_kernel(parts_ref, out_ref):
-    total = parts_ref[0].astype(F32)
-    for i in range(1, parts_ref.shape[0]):
-        total = total + parts_ref[i].astype(F32)
-    out_ref[...] = total.astype(BF)
+    delta_ref[:, :quarter] = gate_delta
+    delta_ref[:, quarter:] = up_delta
+
+
+def grads_kernel(own, x_ref, delta_ref, out_ref):
+    n_z, n_y = out_ref.shape[:2]
+    res = lax.dot_general(
+        x_ref[0], delta_ref[...], (((0,), (0,)), ((), ())), preferred_element_type=F32
+    )
+    for i in range(n_y * n_z):
+        piece = res[i * own : (i + 1) * own]
+        tall = jnp.concatenate(
+            [piece[:, c * 128 : (c + 1) * 128] for c in range(piece.shape[1] // 128)], axis=0
+        )
+        out_ref[i % n_z, i // n_z, 0] = tall.astype(BF)
 
 
 def input_kernel(capacity, place_ref, raw_ref, gate_ref, up_ref, wg_ref, wu_ref, out_ref, total, side):
@@ -179,11 +151,6 @@
     return pltpu.CompilerParams(vmem_limit_bytes=mib * MIB, **more)
 
 
-def ring(x, axis, step):
-    n = lax.axis_size(axis)
-    return lax.ppermute(x, axis, [(i, (i + step) % n) for i in range(n)])
-
-
 SMEM = pl.BlockSpec(memory_space=pltpu.SMEM)
 VMEM = pl.BlockSpec(memory_space=pltpu.VMEM)
 
@@ -192,17 +159,16 @@
     tokens, top = routes.shape
     n_local = lax.axis_size("local")
     n_node = lax.axis_size("node")
-    n_zl, n_zh, n_y = lax.axis_size("zl"), lax.axis_size("zh"), lax.axis_size("y")
-    n_copies = n_y * n_zh * n_zl
+    n_z, n_y = lax.axis_size("z"), lax.axis_size("y")
+    n_copies = n_y * n_z
     capacity = expert_inputs.shape[3]
     feat = token_grads.shape[1]
     hidden = gate_pre.shape[4]
     quarter = hidden // n_node
     slots = n_local * capacity
     own = feat // n_copies
-    part = feat // n_y
     wide = -(-(feat + 1) // 128) * 128
-    place = jnp.stack([lax.axis_index(a) for a in ("y", "node", "local")]).astype(jnp.int32)
+    place = jnp.stack([lax.axis_index(a) for a in ("z", "node", "local")]).astype(jnp.int32)
     gate_rows = gate_pre.reshape(slots, hidden)
     up_rows = up_pre.reshape(slots, hidden)
     x_rows = expert_inputs.reshape(slots, feat)
@@ -215,15 +181,7 @@
     )(routes.T, gates.T, token_grads.T)
     arrived = lax.all_to_all(outgoing, "local", split_axis=0, concat_axis=0, tiled=True)
 
-    x_rows, _ = lax.optimization_barrier((x_rows, outgoing))
-    slabs = pl.pallas_call(
-        functools.partial(early_kernel, n_y),
-        in_specs=[SMEM, VMEM],
-        out_shape=jax.ShapeDtypeStruct((n_y, part, slots), BF),
-        compiler_params=params(),
-        name="early",
-    )(place, x_rows)
-    copies_x = [slabs[0]] + [ring(slabs[k], "y", k) for k in range(1, n_y)]
+    node_x = lax.all_gather(x_rows, "node", axis=0, tiled=False)
 
     raw_parts = pl.pallas_call(
         raw_kernel,
@@ -239,21 +197,35 @@
     )(arrived.reshape(slots, feat), w_down[0].T)
     raw_shares = lax.all_to_all(raw_parts, "node", split_axis=0, concat_axis=0, tiled=True)
 
-    *copies_x, raw_shares = lax.optimization_barrier((*copies_x, raw_shares))
-    node_x = lax.all_gather(jnp.concatenate(copies_x, axis=1), "node", axis=0, tiled=False)
-
     raw_share, deltas = pl.pallas_call(
         share_kernel,
         in_specs=[SMEM, VMEM, VMEM, VMEM],
         out_shape=[
             jax.ShapeDtypeStruct((slots, quarter), BF),
-            jax.ShapeDtypeStruct((n_y, slots, 2 * quarter), BF),
+            jax.ShapeDtypeStruct((slots, 2 * quarter), BF),
         ],
         compiler_params=params(),
         name="share",
     )(place, raw_shares, gate_rows, up_rows)
-    all_deltas = lax.all_to_all(deltas, "y", split_axis=0, concat_axis=0, tiled=True)
-
+
+    tall = own * 2 * quarter // 128
+    grads = pl.pallas_call(
+        functools.partial(grads_kernel, own),
+        grid=(n_node,),
+        in_specs=[
+            pl.BlockSpec((1, slots, feat), lambda i: (i, 0, 0)),
+            pl.BlockSpec((slots, 2 * quarter), lambda i: (0, 0)),
+        ],
+        out_specs=pl.BlockSpec((n_z, n_y, 1, tall, 128), lambda i: (0, 0, i, 0, 0)),
+        out_shape=jax.ShapeDtypeStruct((n_z, n_y, n_node, tall, 128), BF),
+        compiler_params=params(),
+        name="grads",
+    )(node_x, deltas)
+    z_sum = lax.psum_scatter(
+        grads.reshape(n_z * n_y * n_node * tall, 128), "z", scatter_dimension=0, tiled=True
+    )
+
+    raw_share, _ = lax.optimization_barrier((raw_share, grads))
     raw = lax.all_gather(raw_share, "node", axis=0, tiled=False)
     slot_input = pl.pallas_call(
         functools.partial(input_kernel, capacity),
@@ -272,18 +244,6 @@
         compiler_params=params(),
         name="slot_input",
     )(place, raw, gate_rows, up_rows, w_gate[0], w_up[0])
-    all_deltas, slot_input = lax.optimization_barrier((all_deltas, slot_input))
-
-    tall = own * 2 * quarter // 128
-    grads = pl.pallas_call(
-        functools.partial(grads_kernel, own),
-        in_specs=[SMEM, VMEM, VMEM],
-        out_shape=jax.ShapeDtypeStruct((n_zl, n_zh, n_node, tall, 128), BF),
-        scratch_shapes=[pltpu.VMEM((n_y * slots, 2 * quarter), BF)],
-        compiler_params=params(),
-        name="grads",
-    )(place, all_deltas, node_x)
-    near = lax.all_to_all(grads, "zl", split_axis=0, concat_axis=0, tiled=True)
     back = [slot_input[0]] + [
         lax.ppermute(slot_input[k], "local", [(i, i ^ k) for i in range(n_local)])
         for k in range(1, n_local)
@@ -299,27 +259,20 @@
         name="combine",
     )(place, routes.T, gates.T, *back)
 
-    near, input_grads, gate_grads = lax.optimization_barrier((near, input_grads, gate_grads))
-    near_sum = pl.pallas_call(
-        sum_kernel,
-        out_shape=jax.ShapeDtypeStruct((n_zh, n_node, tall, 128), BF),
-        compiler_params=params(),
-        name="near_sum",
-    )(near)
+    z_sum, input_grads, gate_grads = lax.optimization_barrier((z_sum, input_grads, gate_grads))
     parts = lax.all_to_all(
-        near_sum.reshape(n_zh * n_node, tall, 128),
-        ("zh", "node"),
+        z_sum.reshape(n_y * n_node, tall, 128),
+        ("y", "node"),
         split_axis=0,
         concat_axis=0,
         tiled=True,
     )
-
     gate_sum, up_sum = pl.pallas_call(
         functools.partial(final_kernel, n_copies, own),
         out_shape=[jax.ShapeDtypeStruct((own, hidden // 128, 128), F32)] * 2,
         compiler_params=params(),
         name="final",
-    )(parts.reshape(n_zh, n_node, tall, 128))
+    )(parts.reshape(n_y, n_node, tall, 128))
     rows = own * hidden // 128
     return (
         input_grads.T,
@@ -331,8 +284,8 @@
 
 def solution(mesh):
     shape = mesh.devices.shape
-    cut = Mesh(mesh.devices.reshape(*CUT, shape[1], shape[2]), ("y", "zh", "zl", "node", "local"))
-    replica = ("y", "zh", "zl")
+    cut = Mesh(mesh.devices.reshape(*CUT, shape[1], shape[2]), ("y", "z", "node", "local"))
+    replica = ("y", "z")
     placed = (
         P((*replica, "local"), "node"),
         P((*replica, "local"), None),

time: 171 us -> 166 us (0.971)
  starting transfers between devices: 42.6 us -> 20.3 us
  waiting for transfers between devices: 50.8 us -> 64.2 us
  blocking collectives: 36.1 us -> 44.9 us
  Pallas kernels: 17.5 us -> 14 us
    reduce_scatter x0 -> x1, waiting for transfers between devices: none -> 36.6 us  [local(): lax.psum_scatter(grads.reshape(n_z * n_y * n_node * tall, 128), 'z', scat...]
    all_to_all x3 -> x0, waiting for transfers between devices: 27.4 us -> none  [the longest x1 9.51 us: local(): lax.all_to_all(outgoing, 'local', split_axis=0, concat_axis=0, tiled=True)]
    ppermute x3 -> x0, waiting for transfers between devices: 15.7 us -> none  [ring(): return lax.ppermute(x, axis, [(i, (i + step) % n) for i in range(n)])]
    all_to_all x1, waiting for transfers between devices: 0.01 us -> 15.3 us  [local(): lax.all_to_all(raw_parts, 'node', split_axis=0, concat_axis=0, tiled=True)]
    all_to_all x3 -> x0, starting transfers between devices: 12.1 us -> none  [the longest x1 5.12 us: local(): near = lax.all_to_all(grads, 'zl', split_axis=0, concat_axis=0, tiled=True)]
    ppermute x3 -> x0, starting transfers between devices: 10 us -> none  [ring(): return lax.ppermute(x, axis, [(i, (i + step) % n) for i in range(n)])]
    all_to_all x1 -> x2, blocking collectives: 22.7 us -> 31.9 us  [the longest x1 19.7 us: local(): lax.all_to_all(z_sum.reshape(n_y * n_node, tall, 128), ('y', 'node'), spl...]
    all_gather x1, waiting for transfers between devices: 2.25 us -> 7.99 us  [local(): node_x = lax.all_gather(x_rows, 'node', axis=0, tiled=False)]
  transfers between devices with their start and end apart: 11 -> 6, of which waited for: 8 -> 5; matrix products, arithmetic and copies ran while one was open for 0% -> 0% of each run, Pallas kernels for 6% -> 6%
where the time goes in v4:
time: 166 us; the launch traced here: 165 us
  waiting for transfers between devices  64.2 us (39%)
  blocking collectives  44.9 us (27%)
  starting transfers between devices  20.3 us (12%)
  between operations  14.1 us (8%)
  Pallas kernels  14 us (8%)
  local copies, waits for them, and re-layouts  7.39 us (4%)
    reduce_scatter x1, waiting for transfers between devices, local(): lax.psum_scatter(grads.reshape(n_z * n_y * n_node * tall, 128), 'z', scat...  36.6 us
    all_to_all x1, blocking collectives, local(): lax.all_to_all(z_sum.reshape(n_y * n_node, tall, 128), ('y', 'node'), spl...  19.7 us
    all_to_all x1, waiting for transfers between devices, local(): lax.all_to_all(raw_parts, 'node', split_axis=0, concat_axis=0, tiled=True)  15.3 us
    all_gather x1, blocking collectives, local(): raw = lax.all_gather(raw_share, 'node', axis=0, tiled=False)  13 us
    all_to_all x1, starting transfers between devices, local(): lax.all_to_all(raw_parts, 'node', split_axis=0, concat_axis=0, tiled=True)  12.7 us
    all_to_all x1, blocking collectives, local(): lax.all_to_all(outgoing, 'local', split_axis=0, concat_axis=0, tiled=True)  12.2 us
    all_gather x1, waiting for transfers between devices, local(): node_x = lax.all_gather(x_rows, 'node', axis=0, tiled=False)  7.99 us
    ppermute x3, starting transfers between devices, local(): lax.ppermute(slot_input[k], 'local', [(i, i ^ k) for i in range(n_local)])  7.59 us
  transfers between devices with their start and end apart: 6, of which 5 were waited for; matrix products, arithmetic and copies ran while one was open for 0% of the time, Pallas kernels for 6%

profile of v4, /device:TPU:6, one launch (start us, length us, event | category | flops | bytes accessed | tf_op | source)
XLA Modules:
  0.0 165.0 jit_solution(315866444107382022)
XLA Ops:
  7.2 0.0 all-gather.3.cloned.1.call-start
  7.2 0.7 all-gather.3.cloned.1.call-update
  7.9 0.9 copy-done.7
  8.9 0.7 copy-done.8
  9.5 0.7 copy-done.10
  10.2 0.8 dispatch.1
  11.0 12.2 %all_to_all.15 = bf16[4,72,960]{2,1,0:T(8,128)(2,1)S(1)} all-to-all(bf16[4,72,960]{2,1,0:T(8,128)(2,1)S(1)} %dispatch.1), channel_id=1, replica_groups=mesh['y'=4,'z'=12,'node'=4,'local'=4] {'local'}, dimensions={0} | all-to-all | bytes 1105920 | tf_op jit(solution)/shard_map/all_to_all | solution.py:182
  23.2 0.0 copy-done.4
  23.2 2.5 %raw.1 = bf16[4,288,256]{2,1,0:T(8,128)(2,1)} custom-call(bf16[288,960]{1,0:T(8,128)(2,1)S(1)} %bitcast.37, bf16[960,1024]{1,0:T(8,128)(2,1)S(1)} %bitcast.38), custom_call_target="tpu_custom_call" | custom-call | tf_op jit(solution)/shard_map/raw/pallas_call | solution.py:186
  25.8 12.7 %all-to-all-start.1 = ((bf16[4,288,256]{2,1,0:T(8,128)(2,1)}), bf16[4,288,256]{2,1,0:T(8,128)(2,1)S(1)}, u32[]{:S(2)}, u32[]{:S(2)}) async-start(bf16[4,288,256]{2,1,0:T(8,128)(2,1)} %raw.1), calls=%async_computation.1 | async-start | bytes 1179648 | tf_op jit(solution)/shard_map/all_to_all | solution.py:198
  38.5 0.1 pad_add_fusion.place_ref
  38.5 15.3 %all-to-all-done.1.parts_ref = bf16[4,288,256]{2,1,0:T(8,128)(2,1)S(1)} async-done(((bf16[4,288,256]{2,1,0:T(8,128)(2,1)}), bf16[4,288,256]{2,1,0:T(8,128)(2,1)S(1)}, u32[]{:S(2)}, u32[]{:S(2)}) %all-to-all-start.1) | async-done | bytes 589856 | tf_op jit(solution)/shard_map/all_to_all | solution.py:198
  53.9 0.8 share.1
  54.7 8.0 %all-gather.3.cloned.1.call-done.x_ref = bf16[4,288,960]{2,1,0:T(8,128)(2,1)} async-done(((bf16[1,288,960]{2,1,0:T(8,128)(2,1)}), bf16[4,288,960]{2,1,0:T(8,128)(2,1)}) %all-gather.3.cloned.1.call-update) | async-done | bytes 2211856 | tf_op jit(solution)/shard_map/all_gather | solution.py:184
  62.6 1.7 %copy-done.1 = bf16[4,288,960]{2,1,0:T(8,128)(2,1)S(1)} copy-done((bf16[4,288,960]{2,1,0:T(8,128)(2,1)S(1)}, bf16[4,288,960]{2,1,0:T(8,128)(2,1)}, u32[]{:S(2)}) %copy-start.1) | copy-done | bytes 2211864
  64.3 3.1 %grads.1 = bf16[12,4,4,80,128]{4,3,2,1,0:T(8,128)(2,1)S(1)} custom-call(bf16[4,288,960]{2,1,0:T(8,128)(2,1)S(1)} %copy-done.1, bf16[288,512]{1,0:T(8,128)(2,1)S(1)} %get-tuple-element.14.delta_ref), custom_call_target="tpu_custom_call" | custom-call | tf_op jit(solution)/shard_map/grads/pallas_call | solution.py:212
  67.5 1.8 %copy-done = bf16[12,4,4,80,128]{4,3,2,1,0:T(8,128)(2,1)} copy-done((bf16[12,4,4,80,128]{4,3,2,1,0:T(8,128)(2,1)}, bf16[12,4,4,80,128]{4,3,2,1,0:T(8,128)(2,1)S(1)}, u32[]{:S(2)}) %copy-start) | copy-done | bytes 3932184
  69.3 0.0 reduce-scatter.2.cloned.1.call-update
  69.3 13.0 %all-gather = bf16[1152,256]{1,0:T(8,128)(2,1)S(1)} all-gather(bf16[288,256]{1,0:T(8,128)(2,1)S(1)} %get-tuple-element.16), channel_id=2, replica_groups=mesh['y'=4,'z'=12,'node'=4,'local'=4] {'node'}, dimensions={0}, use_global_device_ids=true | all-gather | bytes 737280 | tf_op jit(solution)/shard_map/all_gather | solution.py:229
  82.4 0.0 copy-done.5
  82.4 1.5 copy-done.6
  83.9 3.8 %slot_input.1 = bf16[4,72,1024]{2,1,0:T(8,128)(2,1)S(1)} custom-call(s32[3]{0:T(128)S(1)} %pad_add_fusion.place_ref, bf16[4,288,256]{2,1,0:T(8,128)(2,1)S(1)} %bitcast.32, bf16[288,1024]{1,0:T(8,128)(2,1)S(1)} %bitcast.34, bf16[288,1024]{1,0:T(8,128)(2,1)S(1)} %bitcast.36, bf16[960,1024]{1,0:T(8,128)(2,1)S(1)} %bitcast.39, bf16[960,1024]{1,0:T(8,128)(2,1)S(1)} %bitcast.40), custom_call_target="tpu_custom_call" | custom-call | tf_op jit(solution)/shard_map/slot_input/pallas_call | solution.py:230
  87.7 1.9 %collective-permute-start.2 = (bf16[72,1024]{1,0:T(8,128)(2,1)S(1)}, bf16[72,1024]{1,0:T(8,128)(2,1)S(1)}, u32[]{:S(2)}, u32[]{:S(2)}) collective-permute-start(bf16[72,1024]{1,0:T(8,128)(2,1)S(1)} %get-tuple-element.24), channel_id=1, source_target_pairs={{0,3},{1,2},{2,1},{3,0},{4,7},{5,6},{6,5},{7,4},{8,11},{9,10},{10,... | collective-permute-start | bytes 442376 | tf_op jit(solution)/shard_map/ppermute | solution.py:248
  89.7 3.4 %collective-permute-start.1 = (bf16[72,1024]{1,0:T(8,128)(2,1)S(1)}, bf16[72,1024]{1,0:T(8,128)(2,1)S(1)}, u32[]{:S(2)}, u32[]{:S(2)}) collective-permute-start(bf16[72,1024]{1,0:T(8,128)(2,1)S(1)} %get-tuple-element.25), channel_id=1, source_target_pairs={{0,2},{1,3},{2,0},{3,1},{4,6},{5,7},{6,4},{7,5},{8,10},{9,11},{10,... | collective-permute-start | bytes 442376 | tf_op jit(solution)/shard_map/ppermute | solution.py:248
  93.1 2.2 %collective-permute-start = (bf16[72,1024]{1,0:T(8,128)(2,1)S(1)}, bf16[72,1024]{1,0:T(8,128)(2,1)S(1)}, u32[]{:S(2)}, u32[]{:S(2)}) collective-permute-start(bf16[72,1024]{1,0:T(8,128)(2,1)S(1)} %get-tuple-element.26), channel_id=1, source_target_pairs={{0,1},{1,0},{2,3},{3,2},{4,5},{5,4},{6,7},{7,6},{8,9},{9,8},{10,11... | collective-permute-start | bytes 442376 | tf_op jit(solution)/shard_map/ppermute | solution.py:248
  95.4 0.4 collective-permute-done.2.rest_3_
  95.7 3.2 %collective-permute-done.1.rest_2_ = bf16[72,1024]{1,0:T(8,128)(2,1)S(1)} collective-permute-done((bf16[72,1024]{1,0:T(8,128)(2,1)S(1)}, bf16[72,1024]{1,0:T(8,128)(2,1)S(1)}, u32[]{:S(2)}, u32[]{:S(2)}) %collective-permute-start.1) | collective-permute-done | bytes 147488 | tf_op jit(solution)/shard_map/ppermute | solution.py:248
  98.9 0.0 collective-permute-done.rest_1_
  98.9 2.2 %combine.1 = (bf16[960,128]{1,0:T(8,128)(2,1)}, bf16[2,128]{1,0:T(2,128)(2,1)}) custom-call(s32[3]{0:T(128)S(1)} %pad_add_fusion.place_ref, s32[2,128]{1,0:T(2,128)S(1)} %bitcast.44, bf16[2,128]{1,0:T(2,128)(2,1)S(1)} %bitcast.46, bf16[72,1024]{1,0:T(8,128)(2,1)S(1)} %get-tuple-element.27.rest_0_, bf16[72,1024]{1,0:T(8,128)(2,1)S(1)} %collective-permute-done.rest_1_, ...), custom_call_target="tpu_custom_call" | custom-call | tf_op jit(solution)/shard_map/combine/pallas_call | solution.py:251
  101.1 36.6 %reduce-scatter.2.cloned.1.call-done = bf16[1280,128]{1,0:T(8,128)(2,1)} async-done(((bf16[15360,128]{1,0:T(8,128)(2,1)}), bf16[1280,128]{1,0:T(8,128)(2,1)}) %reduce-scatter.2.cloned.1.call-update) | async-done | bytes 327696 | tf_op jit(solution)/shard_map/reduce_scatter | solution.py:224
  137.7 19.7 %all_to_all.16 = bf16[16,80,128]{2,1,0:T(8,128)(2,1)S(1)} all-to-all(bf16[16,80,128]{2,1,0:T(8,128)(2,1)} %bitcast.48), channel_id=1, replica_groups=mesh['y'=4,'z'=12,'node'=4,'local'=4] {'y','node'}, dimensions={0} | all-to-all | bytes 655360 | tf_op jit(solution)/shard_map/all_to_all | solution.py:263
  157.4 0.8 final.1
  (18 shorter events, 0.1 us)
Async XLA Ops:
  7.2 16.1 %copy-start.4 = (bf16[1,1024,960]{1,2,0:T(8,128)(2,1)S(1)}, bf16[1,1024,960]{1,2,0:T(8,128)(2,1)}, u32[]{:S(2)}) copy-start(bf16[1,1024,960]{1,2,0:T(8,128)(2,1)} %param.17) | copy-start | bytes 5898244
  7.2 55.5 %all-gather.3.cloned.1.call-start = ((), (), s32[]{:S(2)}) async-start(), calls=%async_computation.4 | async-start | bytes 2949120 | tf_op jit(solution)/shard_map/all_gather | solution.py:184
  7.9 0.9 copy-start.7
  8.9 0.7 copy-start.8
  9.5 0.7 copy-start.10
  23.2 30.6 %copy-start.2 = (bf16[1,1,4,72,1024]{4,3,2,1,0:T(8,128)(2,1)S(1)}, bf16[1,1,4,72,1024]{4,3,2,1,0:T(8,128)(2,1)}, u32[]{:S(2)}) copy-start(bf16[1,1,4,72,1024]{4,3,2,1,0:T(8,128)(2,1)} %param.13) | copy-start | bytes 1769476
  23.2 30.6 %copy-start.3 = (bf16[1,1,4,72,1024]{4,3,2,1,0:T(8,128)(2,1)S(1)}, bf16[1,1,4,72,1024]{4,3,2,1,0:T(8,128)(2,1)}, u32[]{:S(2)}) copy-start(bf16[1,1,4,72,1024]{4,3,2,1,0:T(8,128)(2,1)} %param.14) | copy-start | bytes 1769476
  25.8 28.1 %all-to-all-start.1 = ((bf16[4,288,256]{2,1,0:T(8,128)(2,1)}), bf16[4,288,256]{2,1,0:T(8,128)(2,1)S(1)}, u32[]{:S(2)}, u32[]{:S(2)}) async-start(bf16[4,288,256]{2,1,0:T(8,128)(2,1)} %raw.1), calls=%async_computation.1 | async-start | bytes 1179648 | tf_op jit(solution)/shard_map/all_to_all | solution.py:198
  38.5 99.3 %reduce-scatter.2.cloned.1.call-start = ((), (), s32[]{:S(2)}) async-start(), calls=%async_computation.5 | async-start | bytes 4259840 | tf_op jit(solution)/shard_map/reduce_scatter | solution.py:224
  62.6 1.7 %copy-start.1 = (bf16[4,288,960]{2,1,0:T(8,128)(2,1)S(1)}, bf16[4,288,960]{2,1,0:T(8,128)(2,1)}, u32[]{:S(2)}) copy-start(bf16[4,288,960]{2,1,0:T(8,128)(2,1)} %all-gather.3.cloned.1.call-done.x_ref) | copy-start | bytes 6635524
  67.4 1.9 %copy-start = (bf16[12,4,4,80,128]{4,3,2,1,0:T(8,128)(2,1)}, bf16[12,4,4,80,128]{4,3,2,1,0:T(8,128)(2,1)S(1)}, u32[]{:S(2)}) copy-start(bf16[12,4,4,80,128]{4,3,2,1,0:T(8,128)(2,1)S(1)} %grads.1) | copy-start | bytes 11796484
  69.3 13.1 %copy-start.5 = (bf16[1,960,1024]{2,1,0:T(8,128)(2,1)S(1)}, bf16[1,960,1024]{2,1,0:T(8,128)(2,1)}, u32[]{:S(2)}) copy-start(bf16[1,960,1024]{2,1,0:T(8,128)(2,1)} %param.15) | copy-start | bytes 5898244
  82.4 1.5 copy-start.6
  83.9 15.0 %copy-start.9 = (s32[128,2]{0,1:T(2,128)S(1)}, s32[128,2]{0,1:T(2,128)}, u32[]{:S(2)}) copy-start(s32[128,2]{0,1:T(2,128)} %param.10) | copy-start | bytes 3076
  83.9 15.0 %copy-start.11 = (bf16[128,2]{0,1:T(2,128)(2,1)S(1)}, bf16[128,2]{0,1:T(2,128)(2,1)}, u32[]{:S(2)}) copy-start(bf16[128,2]{0,1:T(2,128)(2,1)} %param.11) | copy-start | bytes 1540
  87.7 8.0 %collective-permute-start.2 = (bf16[72,1024]{1,0:T(8,128)(2,1)S(1)}, bf16[72,1024]{1,0:T(8,128)(2,1)S(1)}, u32[]{:S(2)}, u32[]{:S(2)}) collective-permute-start(bf16[72,1024]{1,0:T(8,128)(2,1)S(1)} %get-tuple-element.24), channel_id=1, source_target_pairs={{0,3},{1,2},{2,1},{3,0},{4,7},{5,6},{6,5},{7,4},{8,11},{9,10},{10,... | collective-permute-start | bytes 442376 | tf_op jit(solution)/shard_map/ppermute | solution.py:248
  89.7 9.2 %collective-permute-start.1 = (bf16[72,1024]{1,0:T(8,128)(2,1)S(1)}, bf16[72,1024]{1,0:T(8,128)(2,1)S(1)}, u32[]{:S(2)}, u32[]{:S(2)}) collective-permute-start(bf16[72,1024]{1,0:T(8,128)(2,1)S(1)} %get-tuple-element.25), channel_id=1, source_target_pairs={{0,2},{1,3},{2,0},{3,1},{4,6},{5,7},{6,4},{7,5},{8,10},{9,11},{10,... | collective-permute-start | bytes 442376 | tf_op jit(solution)/shard_map/ppermute | solution.py:248
  93.1 5.8 %collective-permute-start = (bf16[72,1024]{1,0:T(8,128)(2,1)S(1)}, bf16[72,1024]{1,0:T(8,128)(2,1)S(1)}, u32[]{:S(2)}, u32[]{:S(2)}) collective-permute-start(bf16[72,1024]{1,0:T(8,128)(2,1)S(1)} %get-tuple-element.26), channel_id=1, source_target_pairs={{0,1},{1,0},{2,3},{3,2},{4,5},{5,4},{6,7},{7,6},{8,9},{9,8},{10,11... | collective-permute-start | bytes 442376 | tf_op jit(solution)/shard_map/ppermute | solution.py:248
Sparse Core Ops, SparseCore 0:
  10.4 52.2 all-gather.2
  69.4 68.2 reduce-scatter.1

commit v5 on v4

--- a/solution.py
+++ b/solution.py
@@ -68,17 +68,30 @@
     delta_ref[:, quarter:] = up_delta
 
 
-def grads_kernel(own, x_ref, delta_ref, out_ref):
+def grads_kernel(own, place_ref, own_ref, prev_ref, next_ref, half_refs, delta_ref, out_ref):
+    step = pl.program_id(0)
     n_z, n_y = out_ref.shape[:2]
-    res = lax.dot_general(
-        x_ref[0], delta_ref[...], (((0,), (0,)), ((), ())), preferred_element_type=F32
-    )
-    for i in range(n_y * n_z):
-        piece = res[i * own : (i + 1) * own]
-        tall = jnp.concatenate(
-            [piece[:, c * 128 : (c + 1) * 128] for c in range(piece.shape[1] // 128)], axis=0
+
+    def block(x):
+        res = lax.dot_general(
+            x, delta_ref[...], (((0,), (0,)), ((), ())), preferred_element_type=F32
         )
-        out_ref[i % n_z, i // n_z, 0] = tall.astype(BF)
+        for i in range(n_y * n_z):
+            piece = res[i * own : (i + 1) * own]
+            tall = jnp.concatenate(
+                [piece[:, c * 128 : (c + 1) * 128] for c in range(piece.shape[1] // 128)], axis=0
+            )
+            out_ref[i % n_z, i // n_z, 0] = tall.astype(BF)
+
+    for k, ref in enumerate((own_ref, prev_ref, next_ref)):
+
+        @pl.when(step == k)
+        def _(ref=ref):
+            block(ref[...])
+
+    @pl.when(step == 3)
+    def _():
+        block(jnp.concatenate([half_refs[0][...], half_refs[1][...]], axis=0))
 
 
 def input_kernel(capacity, place_ref, raw_ref, gate_ref, up_ref, wg_ref, wu_ref, out_ref, total, side):
@@ -151,6 +164,11 @@
     return pltpu.CompilerParams(vmem_limit_bytes=mib * MIB, **more)
 
 
+def ring(x, axis, step):
+    n = lax.axis_size(axis)
+    return lax.ppermute(x, axis, [(i, (i + step) % n) for i in range(n)])
+
+
 SMEM = pl.BlockSpec(memory_space=pltpu.SMEM)
 VMEM = pl.BlockSpec(memory_space=pltpu.VMEM)
 
@@ -181,7 +199,8 @@
     )(routes.T, gates.T, token_grads.T)
     arrived = lax.all_to_all(outgoing, "local", split_axis=0, concat_axis=0, tiled=True)
 
-    node_x = lax.all_gather(x_rows, "node", axis=0, tiled=False)
+    x_rows, _ = lax.optimization_barrier((x_rows, outgoing))
+    x_prev, x_next = ring(x_rows, "node", 1), ring(x_rows, "node", -1)
 
     raw_parts = pl.pallas_call(
         raw_kernel,
@@ -197,6 +216,10 @@
     )(arrived.reshape(slots, feat), w_down[0].T)
     raw_shares = lax.all_to_all(raw_parts, "node", split_axis=0, concat_axis=0, tiled=True)
 
+    half = slots // 2
+    x_prev, x_next, _ = lax.optimization_barrier((x_prev, x_next, raw_parts))
+    x_across = (ring(x_prev[:half], "node", 1), ring(x_next[half:], "node", -1))
+
     raw_share, deltas = pl.pallas_call(
         share_kernel,
         in_specs=[SMEM, VMEM, VMEM, VMEM],
@@ -211,16 +234,25 @@
     tall = own * 2 * quarter // 128
     grads = pl.pallas_call(
         functools.partial(grads_kernel, own),
-        grid=(n_node,),
-        in_specs=[
-            pl.BlockSpec((1, slots, feat), lambda i: (i, 0, 0)),
-            pl.BlockSpec((slots, 2 * quarter), lambda i: (0, 0)),
-        ],
-        out_specs=pl.BlockSpec((n_z, n_y, 1, tall, 128), lambda i: (0, 0, i, 0, 0)),
+        grid_spec=pltpu.PrefetchScalarGridSpec(
+            num_scalar_prefetch=1,
+            grid=(n_node,),
+            in_specs=[
+                pl.BlockSpec((slots, feat), lambda i, p: (0, 0)),
+                pl.BlockSpec((slots, feat), lambda i, p: (0, 0)),
+                pl.BlockSpec((slots, feat), lambda i, p: (0, 0)),
+                [pl.BlockSpec((half, feat), lambda i, p: (0, 0))] * 2,
+                pl.BlockSpec((slots, 2 * quarter), lambda i, p: (0, 0)),
+            ],
+            out_specs=pl.BlockSpec(
+                (n_z, n_y, 1, tall, 128),
+                lambda i, p: (0, 0, (p[1] + jnp.where(i < 2, 3 * i, i - 1)) % n_node, 0, 0),
+            ),
+        ),
         out_shape=jax.ShapeDtypeStruct((n_z, n_y, n_node, tall, 128), BF),
         compiler_params=params(),
         name="grads",
-    )(node_x, deltas)
+    )(place, x_rows, x_prev, x_next, list(x_across), deltas)
     z_sum = lax.psum_scatter(
         grads.reshape(n_z * n_y * n_node * tall, 128), "z", scatter_dimension=0, tiled=True
     )

time: 166 us -> 161 us (0.970)
  starting transfers between devices: 20.3 us -> 41.3 us
  waiting for transfers between devices: 64.2 us -> 44.7 us
  blocking collectives: 44.9 us -> 34 us
  Pallas kernels: 14 us -> 16.7 us
  local copies, waits for them, and re-layouts: 7.39 us -> 9.18 us
    ppermute x0 -> x4, starting transfers between devices: none -> 20.8 us  [ring(): return lax.ppermute(x, axis, [(i, (i + step) % n) for i in range(n)])]
    all_to_all x1, waiting for transfers between devices: 15.3 us -> 0.01 us  [local(): lax.all_to_all(raw_parts, 'node', split_axis=0, concat_axis=0, tiled=True)]
    all_to_all x1 -> x0, blocking collectives: 12.2 us -> none  [local(): lax.all_to_all(outgoing, 'local', split_axis=0, concat_axis=0, tiled=True)]
    all_gather x1 -> x0, waiting for transfers between devices: 7.99 us -> none  [local(): node_x = lax.all_gather(x_rows, 'node', axis=0, tiled=False)]
    ppermute x0 -> x4, waiting for transfers between devices: none -> 7.63 us  [ring(): return lax.ppermute(x, axis, [(i, (i + step) % n) for i in range(n)])]
    all_to_all x1, starting transfers between devices: 12.7 us -> 9.21 us  [local(): lax.all_to_all(raw_parts, 'node', split_axis=0, concat_axis=0, tiled=True)]
    all_to_all x0 -> x1, starting transfers between devices: none -> 3.48 us  [local(): lax.all_to_all(outgoing, 'local', split_axis=0, concat_axis=0, tiled=True)]
    reduce_scatter x1, waiting for transfers between devices: 36.6 us -> 34.1 us  [local(): lax.psum_scatter(grads.reshape(n_z * n_y * n_node * tall, 128), 'z', scat...]
  transfers between devices with their start and end apart: 6 -> 10, of which waited for: 5 -> 6; matrix products, arithmetic and copies ran while one was open for 0% -> 2% of each run, Pallas kernels for 6% -> 6%
where the time goes in v5:
time: 161 us; the launch traced here: 160 us
  waiting for transfers between devices  44.7 us (28%)
  starting transfers between devices  41.3 us (26%)
  blocking collectives  34 us (21%)
  Pallas kernels  16.7 us (10%)
  between operations  14.2 us (9%)
  local copies, waits for them, and re-layouts  9.18 us (6%)
    reduce_scatter x1, waiting for transfers between devices, local(): lax.psum_scatter(grads.reshape(n_z * n_y * n_node * tall, 128), 'z', scat...  34.1 us
    ppermute x4, starting transfers between devices, ring(): return lax.ppermute(x, axis, [(i, (i + step) % n) for i in range(n)])  20.8 us
    all_to_all x1, blocking collectives, local(): lax.all_to_all(z_sum.reshape(n_y * n_node, tall, 128), ('y', 'node'), spl...  19.7 us
    all_gather x1, blocking collectives, local(): raw = lax.all_gather(raw_share, 'node', axis=0, tiled=False)  14.2 us
    all_to_all x1, starting transfers between devices, local(): lax.all_to_all(raw_parts, 'node', split_axis=0, concat_axis=0, tiled=True)  9.21 us
    ppermute x3, starting transfers between devices, local(): lax.ppermute(slot_input[k], 'local', [(i, i ^ k) for i in range(n_local)])  7.8 us
    ppermute x4, waiting for transfers between devices, ring(): return lax.ppermute(x, axis, [(i, (i + step) % n) for i in range(n)])  7.63 us
    unnamed x28, local copies, waits for them, and re-layouts  6.73 us
  transfers between devices with their start and end apart: 10, of which 6 were waited for; matrix products, arithmetic and copies ran while one was open for 2% of the time, Pallas kernels for 6%

profile of v5, /device:TPU:6, one launch (start us, length us, event | category | flops | bytes accessed | tf_op | source)
XLA Modules:
  0.0 160.1 jit_solution(14364229277478456334)
XLA Ops:
  7.2 1.1 copy-done.7
  8.3 0.7 copy-done.10
  8.9 0.7 copy-done.12
  9.6 1.7 %dispatch.1 = bf16[4,72,960]{2,1,0:T(8,128)(2,1)} custom-call(s32[2,128]{1,0:T(2,128)S(1)} %bitcast.46, bf16[2,128]{1,0:T(2,128)(2,1)S(1)} %bitcast.48, bf16[960,128]{1,0:T(8,128)(2,1)S(1)} %bitcast.45), custom_call_target="tpu_custom_call" | custom-call | tf_op jit(solution)/shard_map/dispatch/pallas_call | solution.py:194
  11.3 3.5 %all-to-all-start = ((bf16[4,72,960]{2,1,0:T(8,128)(2,1)}), bf16[4,72,960]{2,1,0:T(8,128)(2,1)S(1)}, u32[]{:S(2)}, u32[]{:S(2)}) async-start(bf16[4,72,960]{2,1,0:T(8,128)(2,1)} %dispatch.1), calls=%async_computation | async-start | bytes 1179648 | tf_op jit(solution)/shard_map/all_to_all | solution.py:200
  14.8 2.7 %collective-permute-start.1 = (bf16[288,960]{1,0:T(8,128)(2,1)}, bf16[288,960]{1,0:T(8,128)(2,1)S(1)}, u32[]{:S(2)}, u32[]{:S(2)}) collective-permute-start(bf16[288,960]{1,0:T(8,128)(2,1)} %bitcast.42), channel_id=1, source_target_pairs={{0,12},{4,0},{8,4},{12,8},{1,13},{5,1},{9,5},{13,9},{2,14},{6,2},{... | collective-permute-start | bytes 1658888 | tf_op jit(solution)/shard_map/ppermute | solution.py:169
  17.5 10.6 %collective-permute-start = (bf16[288,960]{1,0:T(8,128)(2,1)}, bf16[288,960]{1,0:T(8,128)(2,1)}, u32[]{:S(2)}, u32[]{:S(2)}) collective-permute-start(bf16[288,960]{1,0:T(8,128)(2,1)} %bitcast.43), channel_id=1, source_target_pairs={{0,4},{4,8},{8,12},{12,0},{1,5},{5,9},{9,13},{13,1},{2,6},{6,10},{... | collective-permute-start | bytes 1658888 | tf_op jit(solution)/shard_map/ppermute | solution.py:169
  28.1 2.5 %raw.1 = bf16[4,288,256]{2,1,0:T(8,128)(2,1)} custom-call(bf16[288,960]{1,0:T(8,128)(2,1)S(1)} %bitcast.37, bf16[960,1024]{1,0:T(8,128)(2,1)S(1)} %bitcast.38), custom_call_target="tpu_custom_call" | custom-call | tf_op jit(solution)/shard_map/raw/pallas_call | solution.py:205
  30.6 9.2 %all-to-all-start.1 = ((bf16[4,288,256]{2,1,0:T(8,128)(2,1)}), bf16[4,288,256]{2,1,0:T(8,128)(2,1)S(1)}, u32[]{:S(2)}, u32[]{:S(2)}) async-start(bf16[4,288,256]{2,1,0:T(8,128)(2,1)} %raw.1), calls=%async_computation.1 | async-start | bytes 1179648 | tf_op jit(solution)/shard_map/all_to_all | solution.py:217
  39.8 0.5 collective-permute-done.1.next_ref
  40.3 1.7 %collective-permute-done.prev_ref = bf16[288,960]{1,0:T(8,128)(2,1)} collective-permute-done((bf16[288,960]{1,0:T(8,128)(2,1)}, bf16[288,960]{1,0:T(8,128)(2,1)}, u32[]{:S(2)}, u32[]{:S(2)}) %collective-permute-start) | collective-permute-done | bytes 552992 | tf_op jit(solution)/shard_map/ppermute | solution.py:169
  42.0 1.7 %slice.18 = bf16[144,960]{1,0:T(8,128)(2,1)} slice(bf16[288,960]{1,0:T(8,128)(2,1)} %collective-permute-done.prev_ref), slice={[0:144], [0:960]} | slice | bytes 552960 | tf_op jit(solution)/shard_map/slice | solution.py:221
  43.7 0.7 slice.19
  44.4 3.8 %collective-permute-start.3 = (bf16[144,960]{1,0:T(8,128)(2,1)}, bf16[144,960]{1,0:T(8,128)(2,1)S(1)}, u32[]{:S(2)}, u32[]{:S(2)}) collective-permute-start(bf16[144,960]{1,0:T(8,128)(2,1)} %slice.19), channel_id=1, source_target_pairs={{0,12},{4,0},{8,4},{12,8},{1,13},{5,1},{9,5},{13,9},{2,14},{6,2},{... | collective-permute-start | bytes 829448 | tf_op jit(solution)/shard_map/ppermute | solution.py:169
  48.2 3.7 %collective-permute-start.2 = (bf16[144,960]{1,0:T(8,128)(2,1)}, bf16[144,960]{1,0:T(8,128)(2,1)}, u32[]{:S(2)}, u32[]{:S(2)}) collective-permute-start(bf16[144,960]{1,0:T(8,128)(2,1)} %slice.18), channel_id=1, source_target_pairs={{0,4},{4,8},{8,12},{12,0},{1,5},{5,9},{9,13},{13,1},{2,6},{6,10},{... | collective-permute-start | bytes 829448 | tf_op jit(solution)/shard_map/ppermute | solution.py:169
  52.1 0.8 share.1
  52.9 3.8 %collective-permute-done.3.half_refs_1_ = bf16[144,960]{1,0:T(8,128)(2,1)S(1)} collective-permute-done((bf16[144,960]{1,0:T(8,128)(2,1)}, bf16[144,960]{1,0:T(8,128)(2,1)S(1)}, u32[]{:S(2)}, u32[]{:S(2)}) %collective-permute-start.3) | collective-permute-done | bytes 276512 | tf_op jit(solution)/shard_map/ppermute | solution.py:169
  56.6 1.7 %collective-permute-done.2.half_refs_0_ = bf16[144,960]{1,0:T(8,128)(2,1)} collective-permute-done((bf16[144,960]{1,0:T(8,128)(2,1)}, bf16[144,960]{1,0:T(8,128)(2,1)}, u32[]{:S(2)}, u32[]{:S(2)}) %collective-permute-start.2) | collective-permute-done | bytes 276512 | tf_op jit(solution)/shard_map/ppermute | solution.py:169
  58.3 5.0 %grads.1 = bf16[12,4,4,80,128]{4,3,2,1,0:T(8,128)(2,1)S(1)} custom-call(s32[3]{0:T(128)S(1)} %pad_add_fusion.place_ref, bf16[288,960]{1,0:T(8,128)(2,1)S(1)} %bitcast.44, bf16[288,960]{1,0:T(8,128)(2,1)} %collective-permute-done.prev_ref, bf16[288,960]{1,0:T(8,128)(2,1)S(1)} %collective-permute-done.1.next_ref, ...), custom_call_target="tpu_custom_call" | custom-call | tf_op jit(solution)/shard_map/grads/pallas_call | solution.py:235
  63.3 1.9 %copy-done = bf16[12,4,4,80,128]{4,3,2,1,0:T(8,128)(2,1)} copy-done((bf16[12,4,4,80,128]{4,3,2,1,0:T(8,128)(2,1)}, bf16[12,4,4,80,128]{4,3,2,1,0:T(8,128)(2,1)S(1)}, u32[]{:S(2)}) %copy-start) | copy-done | bytes 3932184
  65.2 0.9 copy-done.9
  66.1 14.2 %all-gather = bf16[1152,256]{1,0:T(8,128)(2,1)S(1)} all-gather(bf16[288,256]{1,0:T(8,128)(2,1)S(1)} %copy-done.9), channel_id=2, replica_groups=mesh['y'=4,'z'=12,'node'=4,'local'=4] {'node'}, dimensions={0}, use_global_device_ids=true | all-gather | bytes 737280 | tf_op jit(solution)/shard_map/all_gather | solution.py:261
  80.3 1.5 copy-done.5
  81.9 3.8 %slot_input.1 = bf16[4,72,1024]{2,1,0:T(8,128)(2,1)S(1)} custom-call(s32[3]{0:T(128)S(1)} %pad_add_fusion.place_ref, bf16[4,288,256]{2,1,0:T(8,128)(2,1)S(1)} %bitcast.32, bf16[288,1024]{1,0:T(8,128)(2,1)S(1)} %bitcast.34, bf16[288,1024]{1,0:T(8,128)(2,1)S(1)} %bitcast.36, bf16[960,1024]{1,0:T(8,128)(2,1)S(1)} %bitcast.39, bf16[960,1024]{1,0:T(8,128)(2,1)S(1)} %bitcast.40), custom_call_target="tpu_custom_call" | custom-call | tf_op jit(solution)/shard_map/slot_input/pallas_call | solution.py:262
  85.7 1.9 %collective-permute-start.6 = (bf16[72,1024]{1,0:T(8,128)(2,1)S(1)}, bf16[72,1024]{1,0:T(8,128)(2,1)S(1)}, u32[]{:S(2)}, u32[]{:S(2)}) collective-permute-start(bf16[72,1024]{1,0:T(8,128)(2,1)S(1)} %get-tuple-element.30), channel_id=1, source_target_pairs={{0,3},{1,2},{2,1},{3,0},{4,7},{5,6},{6,5},{7,4},{8,11},{9,10},{10,... | collective-permute-start | bytes 442376 | tf_op jit(solution)/shard_map/ppermute | solution.py:280
  87.6 3.9 %collective-permute-start.5 = (bf16[72,1024]{1,0:T(8,128)(2,1)S(1)}, bf16[72,1024]{1,0:T(8,128)(2,1)S(1)}, u32[]{:S(2)}, u32[]{:S(2)}) collective-permute-start(bf16[72,1024]{1,0:T(8,128)(2,1)S(1)} %get-tuple-element.31), channel_id=1, source_target_pairs={{0,2},{1,3},{2,0},{3,1},{4,6},{5,7},{6,4},{7,5},{8,10},{9,11},{10,... | collective-permute-start | bytes 442376 | tf_op jit(solution)/shard_map/ppermute | solution.py:280
  91.5 2.0 %collective-permute-start.4 = (bf16[72,1024]{1,0:T(8,128)(2,1)S(1)}, bf16[72,1024]{1,0:T(8,128)(2,1)S(1)}, u32[]{:S(2)}, u32[]{:S(2)}) collective-permute-start(bf16[72,1024]{1,0:T(8,128)(2,1)S(1)} %get-tuple-element.32), channel_id=1, source_target_pairs={{0,1},{1,0},{2,3},{3,2},{4,5},{5,4},{6,7},{7,6},{8,9},{9,8},{10,11... | collective-permute-start | bytes 442376 | tf_op jit(solution)/shard_map/ppermute | solution.py:280
  93.5 2.9 %collective-permute-done.5.rest_2_ = bf16[72,1024]{1,0:T(8,128)(2,1)S(1)} collective-permute-done((bf16[72,1024]{1,0:T(8,128)(2,1)S(1)}, bf16[72,1024]{1,0:T(8,128)(2,1)S(1)}, u32[]{:S(2)}, u32[]{:S(2)}) %collective-permute-start.5) | collective-permute-done | bytes 147488 | tf_op jit(solution)/shard_map/ppermute | solution.py:280
  96.4 2.2 %combine.1 = (bf16[960,128]{1,0:T(8,128)(2,1)}, bf16[2,128]{1,0:T(2,128)(2,1)}) custom-call(s32[3]{0:T(128)S(1)} %pad_add_fusion.place_ref, s32[2,128]{1,0:T(2,128)S(1)} %bitcast.47, bf16[2,128]{1,0:T(2,128)(2,1)S(1)} %bitcast.49, bf16[72,1024]{1,0:T(8,128)(2,1)S(1)} %get-tuple-element.33.rest_0_, bf16[72,1024]{1,0:T(8,128)(2,1)S(1)} %collective-permute-done.4.rest_1_, ...), custom_call_target="tpu_custom_call" | custom-call | tf_op jit(solution)/shard_map/combine/pallas_call | solution.py:283
  98.6 34.1 %reduce-scatter.2.cloned.1.call-done = bf16[1280,128]{1,0:T(8,128)(2,1)} async-done(((bf16[15360,128]{1,0:T(8,128)(2,1)}), bf16[1280,128]{1,0:T(8,128)(2,1)}) %reduce-scatter.2.cloned.1.call-update) | async-done | bytes 327696 | tf_op jit(solution)/shard_map/reduce_scatter | solution.py:256
  132.8 19.7 %all_to_all.15 = bf16[16,80,128]{2,1,0:T(8,128)(2,1)S(1)} all-to-all(bf16[16,80,128]{2,1,0:T(8,128)(2,1)} %bitcast.50), channel_id=1, replica_groups=mesh['y'=4,'z'=12,'node'=4,'local'=4] {'y','node'}, dimensions={0} | all-to-all | bytes 655360 | tf_op jit(solution)/shard_map/all_to_all | solution.py:295
  152.5 0.8 final.1
  (30 shorter events, 0.2 us)
Async XLA Ops:
  7.2 21.0 %copy-start.3 = (bf16[1,1024,960]{1,2,0:T(8,128)(2,1)S(1)}, bf16[1,1024,960]{1,2,0:T(8,128)(2,1)}, u32[]{:S(2)}) copy-start(bf16[1,1024,960]{1,2,0:T(8,128)(2,1)} %param.17) | copy-start | bytes 5898244
  7.2 1.1 copy-start.7
  8.3 0.7 copy-start.10
  8.9 0.7 copy-start.12
  11.3 16.8 %all-to-all-start = ((bf16[4,72,960]{2,1,0:T(8,128)(2,1)}), bf16[4,72,960]{2,1,0:T(8,128)(2,1)S(1)}, u32[]{:S(2)}, u32[]{:S(2)}) async-start(bf16[4,72,960]{2,1,0:T(8,128)(2,1)} %dispatch.1), calls=%async_computation | async-start | bytes 1179648 | tf_op jit(solution)/shard_map/all_to_all | solution.py:200
  14.8 25.6 %collective-permute-start.1 = (bf16[288,960]{1,0:T(8,128)(2,1)}, bf16[288,960]{1,0:T(8,128)(2,1)S(1)}, u32[]{:S(2)}, u32[]{:S(2)}) collective-permute-start(bf16[288,960]{1,0:T(8,128)(2,1)} %bitcast.42), channel_id=1, source_target_pairs={{0,12},{4,0},{8,4},{12,8},{1,13},{5,1},{9,5},{13,9},{2,14},{6,2},{... | collective-permute-start | bytes 1658888 | tf_op jit(solution)/shard_map/ppermute | solution.py:169
  17.5 24.5 %collective-permute-start = (bf16[288,960]{1,0:T(8,128)(2,1)}, bf16[288,960]{1,0:T(8,128)(2,1)}, u32[]{:S(2)}, u32[]{:S(2)}) collective-permute-start(bf16[288,960]{1,0:T(8,128)(2,1)} %bitcast.43), channel_id=1, source_target_pairs={{0,4},{4,8},{8,12},{12,0},{1,5},{5,9},{9,13},{13,1},{2,6},{6,10},{... | collective-permute-start | bytes 1658888 | tf_op jit(solution)/shard_map/ppermute | solution.py:169
  30.6 21.4 %copy-start.1 = (bf16[1,1,4,72,1024]{4,3,2,1,0:T(8,128)(2,1)S(1)}, bf16[1,1,4,72,1024]{4,3,2,1,0:T(8,128)(2,1)}, u32[]{:S(2)}) copy-start(bf16[1,1,4,72,1024]{4,3,2,1,0:T(8,128)(2,1)} %param.13) | copy-start | bytes 1769476
  30.6 21.4 %copy-start.2 = (bf16[1,1,4,72,1024]{4,3,2,1,0:T(8,128)(2,1)S(1)}, bf16[1,1,4,72,1024]{4,3,2,1,0:T(8,128)(2,1)}, u32[]{:S(2)}) copy-start(bf16[1,1,4,72,1024]{4,3,2,1,0:T(8,128)(2,1)} %param.14) | copy-start | bytes 1769476
  30.6 27.7 %copy-start.6 = (bf16[1,1,4,72,960]{4,3,2,1,0:T(8,128)(2,1)S(1)}, bf16[1,1,4,72,960]{4,3,2,1,0:T(8,128)(2,1)}, u32[]{:S(2)}) copy-start(bf16[1,1,4,72,960]{4,3,2,1,0:T(8,128)(2,1)} %param.12) | copy-start | bytes 1658884
  30.6 21.4 %all-to-all-start.1 = ((bf16[4,288,256]{2,1,0:T(8,128)(2,1)}), bf16[4,288,256]{2,1,0:T(8,128)(2,1)S(1)}, u32[]{:S(2)}, u32[]{:S(2)}) async-start(bf16[4,288,256]{2,1,0:T(8,128)(2,1)} %raw.1), calls=%async_computation.1 | async-start | bytes 1179648 | tf_op jit(solution)/shard_map/all_to_all | solution.py:217
  39.8 92.9 %reduce-scatter.2.cloned.1.call-start = ((), (), s32[]{:S(2)}) async-start(), calls=%async_computation.4 | async-start | bytes 4259840 | tf_op jit(solution)/shard_map/reduce_scatter | solution.py:256
  44.4 12.2 %collective-permute-start.3 = (bf16[144,960]{1,0:T(8,128)(2,1)}, bf16[144,960]{1,0:T(8,128)(2,1)S(1)}, u32[]{:S(2)}, u32[]{:S(2)}) collective-permute-start(bf16[144,960]{1,0:T(8,128)(2,1)} %slice.19), channel_id=1, source_target_pairs={{0,12},{4,0},{8,4},{12,8},{1,13},{5,1},{9,5},{13,9},{2,14},{6,2},{... | collective-permute-start | bytes 829448 | tf_op jit(solution)/shard_map/ppermute | solution.py:169
  48.2 10.1 %collective-permute-start.2 = (bf16[144,960]{1,0:T(8,128)(2,1)}, bf16[144,960]{1,0:T(8,128)(2,1)}, u32[]{:S(2)}, u32[]{:S(2)}) collective-permute-start(bf16[144,960]{1,0:T(8,128)(2,1)} %slice.18), channel_id=1, source_target_pairs={{0,4},{4,8},{8,12},{12,0},{1,5},{5,9},{9,13},{13,1},{2,6},{6,10},{... | collective-permute-start | bytes 829448 | tf_op jit(solution)/shard_map/ppermute | solution.py:169
  52.9 10.4 %copy-start.8 = (bf16[288,256]{1,0:T(8,128)(2,1)}, bf16[288,256]{1,0:T(8,128)(2,1)S(1)}, u32[]{:S(2)}) copy-start(bf16[288,256]{1,0:T(8,128)(2,1)S(1)} %get-tuple-element.22) | copy-start | bytes 442372
  63.3 1.9 %copy-start = (bf16[12,4,4,80,128]{4,3,2,1,0:T(8,128)(2,1)}, bf16[12,4,4,80,128]{4,3,2,1,0:T(8,128)(2,1)S(1)}, u32[]{:S(2)}) copy-start(bf16[12,4,4,80,128]{4,3,2,1,0:T(8,128)(2,1)S(1)} %grads.1) | copy-start | bytes 11796484
  65.2 0.9 copy-start.9
  65.2 15.2 %copy-start.4 = (bf16[1,960,1024]{2,1,0:T(8,128)(2,1)S(1)}, bf16[1,960,1024]{2,1,0:T(8,128)(2,1)}, u32[]{:S(2)}) copy-start(bf16[1,960,1024]{2,1,0:T(8,128)(2,1)} %param.15) | copy-start | bytes 5898244
  80.3 1.5 copy-start.5
  81.9 14.5 %copy-start.11 = (s32[128,2]{0,1:T(2,128)S(1)}, s32[128,2]{0,1:T(2,128)}, u32[]{:S(2)}) copy-start(s32[128,2]{0,1:T(2,128)} %param.10) | copy-start | bytes 3076
  81.9 14.5 %copy-start.13 = (bf16[128,2]{0,1:T(2,128)(2,1)S(1)}, bf16[128,2]{0,1:T(2,128)(2,1)}, u32[]{:S(2)}) copy-start(bf16[128,2]{0,1:T(2,128)(2,1)} %param.11) | copy-start | bytes 1540
  85.7 7.8 %collective-permute-start.6 = (bf16[72,1024]{1,0:T(8,128)(2,1)S(1)}, bf16[72,1024]{1,0:T(8,128)(2,1)S(1)}, u32[]{:S(2)}, u32[]{:S(2)}) collective-permute-start(bf16[72,1024]{1,0:T(8,128)(2,1)S(1)} %get-tuple-element.30), channel_id=1, source_target_pairs={{0,3},{1,2},{2,1},{3,0},{4,7},{5,6},{6,5},{7,4},{8,11},{9,10},{10,... | collective-permute-start | bytes 442376 | tf_op jit(solution)/shard_map/ppermute | solution.py:280
  87.6 8.8 %collective-permute-start.5 = (bf16[72,1024]{1,0:T(8,128)(2,1)S(1)}, bf16[72,1024]{1,0:T(8,128)(2,1)S(1)}, u32[]{:S(2)}, u32[]{:S(2)}) collective-permute-start(bf16[72,1024]{1,0:T(8,128)(2,1)S(1)} %get-tuple-element.31), channel_id=1, source_target_pairs={{0,2},{1,3},{2,0},{3,1},{4,6},{5,7},{6,4},{7,5},{8,10},{9,11},{10,... | collective-permute-start | bytes 442376 | tf_op jit(solution)/shard_map/ppermute | solution.py:280
  91.5 4.9 %collective-permute-start.4 = (bf16[72,1024]{1,0:T(8,128)(2,1)S(1)}, bf16[72,1024]{1,0:T(8,128)(2,1)S(1)}, u32[]{:S(2)}, u32[]{:S(2)}) collective-permute-start(bf16[72,1024]{1,0:T(8,128)(2,1)S(1)} %get-tuple-element.32), channel_id=1, source_target_pairs={{0,1},{1,0},{2,3},{3,2},{4,5},{5,4},{6,7},{7,6},{8,9},{9,8},{10,11... | collective-permute-start | bytes 442376 | tf_op jit(solution)/shard_map/ppermute | solution.py:280
Sparse Core Ops, SparseCore 0:
  65.3 67.3 reduce-scatter.1

commit v6 on v3

--- a/solution.py
+++ b/solution.py
@@ -58,16 +58,14 @@
     y = place_ref[0]
     feat = x_ref.shape[1]
     part = feat // n_y
-    at = lax.broadcasted_iota(jnp.int32, (part, feat), 1) - lax.broadcasted_iota(
-        jnp.int32, (part, feat), 0
+    at = lax.broadcasted_iota(jnp.int32, (feat, part), 0) - lax.broadcasted_iota(
+        jnp.int32, (feat, part), 1
     )
     x = x_ref[...]
     for k in range(n_y):
         first = jnp.bitwise_and(y + k, n_y - 1) * part
         chosen = jnp.where(at == first, 1.0, 0.0).astype(BF)
-        out_ref[k] = lax.dot_general(
-            chosen, x, (((1,), (1,)), ((), ())), preferred_element_type=F32
-        ).astype(BF)
+        out_ref[k] = jnp.dot(x, chosen, preferred_element_type=F32).astype(BF)
 
 
 def share_kernel(place_ref, parts_ref, gate_ref, up_ref, raw_ref, delta_ref):
@@ -91,22 +89,29 @@
         copy = jnp.bitwise_and(place_ref[0] + n_y - k, n_y - 1)
         ordered[k * slots : (k + 1) * slots] = delta_ref[copy]
     d = ordered[...]
-    n_zl, n_zh, n_node = out_ref.shape[:3]
+    n_zl, n_node, n_zh = out_ref.shape[:3]
     for b in range(n_node):
-        res = jnp.dot(x_ref[b], d, preferred_element_type=F32)
+        res = lax.dot_general(
+            x_ref[b], d, (((0,), (0,)), ((), ())), preferred_element_type=F32
+        )
         for i in range(n_zh * n_zl):
             piece = res[i * own : (i + 1) * own]
             tall = jnp.concatenate(
                 [piece[:, c * 128 : (c + 1) * 128] for c in range(piece.shape[1] // 128)], axis=0
             )
-            out_ref[i % n_zl, i // n_zl, b] = tall.astype(BF)
-
-
-def sum_kernel(parts_ref, out_ref):
-    total = parts_ref[0].astype(F32)
-    for i in range(1, parts_ref.shape[0]):
-        total = total + parts_ref[i].astype(F32)
-    out_ref[...] = total.astype(BF)
+            out_ref[i % n_zl, b, i // n_zl] = tall.astype(BF)
+
+
+def near_kernel(place_ref, parts_ref, out_ref):
+    n_zl, n_node, n_zh = parts_ref.shape[:3]
+    for k in range(n_zh):
+        to = place_ref[3] + k
+        to = jnp.where(to >= n_zh, to - n_zh, to)
+        for x in range(n_node):
+            total = parts_ref[0, x, to].astype(F32)
+            for i in range(1, n_zl):
+                total = total + parts_ref[i, x, to].astype(F32)
+            out_ref[k, x] = total.astype(BF)
 
 
 def input_kernel(capacity, place_ref, raw_ref, gate_ref, up_ref, wg_ref, wu_ref, out_ref, total, side):
@@ -162,12 +167,12 @@
         grads_ref[k : k + 1, :] = (sums / gates[k : k + 1, :]).astype(BF)
 
 
-def final_kernel(n_copies, own, parts_ref, gate_ref, up_ref):
-    copies, n_node = parts_ref.shape[0], parts_ref.shape[1]
-    for x in range(n_node):
-        total = parts_ref[0, x].astype(F32)
-        for i in range(1, copies):
-            total = total + parts_ref[i, x].astype(F32)
+def final_kernel(n_copies, own, *refs):
+    parts_refs, (gate_ref, up_ref) = refs[:-2], refs[-2:]
+    for x in range(parts_refs[0].shape[0]):
+        total = parts_refs[0][x].astype(F32)
+        for ref in parts_refs[1:]:
+            total = total + ref[x].astype(F32)
         total = total * (1.0 / n_copies)
         per = total.shape[0] // own // 2
         for c in range(2 * per):
@@ -202,7 +207,7 @@
     own = feat // n_copies
     part = feat // n_y
     wide = -(-(feat + 1) // 128) * 128
-    place = jnp.stack([lax.axis_index(a) for a in ("y", "node", "local")]).astype(jnp.int32)
+    place = jnp.stack([lax.axis_index(a) for a in ("y", "node", "local", "zh")]).astype(jnp.int32)
     gate_rows = gate_pre.reshape(slots, hidden)
     up_rows = up_pre.reshape(slots, hidden)
     x_rows = expert_inputs.reshape(slots, feat)
@@ -219,12 +224,15 @@
     slabs = pl.pallas_call(
         functools.partial(early_kernel, n_y),
         in_specs=[SMEM, VMEM],
-        out_shape=jax.ShapeDtypeStruct((n_y, part, slots), BF),
+        out_shape=jax.ShapeDtypeStruct((n_y, slots, part), BF),
         compiler_params=params(),
         name="early",
     )(place, x_rows)
     copies_x = [slabs[0]] + [ring(slabs[k], "y", k) for k in range(1, n_y)]
 
+    arrived, copies_x[1], copies_x[3] = lax.optimization_barrier(
+        (arrived, copies_x[1], copies_x[3])
+    )
     raw_parts = pl.pallas_call(
         raw_kernel,
         grid=(n_node,),
@@ -239,8 +247,8 @@
     )(arrived.reshape(slots, feat), w_down[0].T)
     raw_shares = lax.all_to_all(raw_parts, "node", split_axis=0, concat_axis=0, tiled=True)
 
-    *copies_x, raw_shares = lax.optimization_barrier((*copies_x, raw_shares))
-    node_x = lax.all_gather(jnp.concatenate(copies_x, axis=1), "node", axis=0, tiled=False)
+    copies_x[2], raw_shares = lax.optimization_barrier((copies_x[2], raw_shares))
+    node_x = lax.all_gather(jnp.concatenate(copies_x, axis=0), "node", axis=0, tiled=False)
 
     raw_share, deltas = pl.pallas_call(
         share_kernel,
@@ -278,12 +286,18 @@
     grads = pl.pallas_call(
         functools.partial(grads_kernel, own),
         in_specs=[SMEM, VMEM, VMEM],
-        out_shape=jax.ShapeDtypeStruct((n_zl, n_zh, n_node, tall, 128), BF),
+        out_shape=jax.ShapeDtypeStruct((n_zl, n_node, n_zh, tall, 128), BF),
         scratch_shapes=[pltpu.VMEM((n_y * slots, 2 * quarter), BF)],
         compiler_params=params(),
         name="grads",
     )(place, all_deltas, node_x)
-    near = lax.all_to_all(grads, "zl", split_axis=0, concat_axis=0, tiled=True)
+    near = lax.all_to_all(
+        grads.reshape(n_zl * n_node, n_zh, tall, 128),
+        ("zl", "node"),
+        split_axis=0,
+        concat_axis=0,
+        tiled=True,
+    )
     back = [slot_input[0]] + [
         lax.ppermute(slot_input[k], "local", [(i, i ^ k) for i in range(n_local)])
         for k in range(1, n_local)
@@ -301,25 +315,19 @@
 
     near, input_grads, gate_grads = lax.optimization_barrier((near, input_grads, gate_grads))
     near_sum = pl.pallas_call(
-        sum_kernel,
+        near_kernel,
+        in_specs=[SMEM, VMEM],
         out_shape=jax.ShapeDtypeStruct((n_zh, n_node, tall, 128), BF),
         compiler_params=params(),
         name="near_sum",
-    )(near)
-    parts = lax.all_to_all(
-        near_sum.reshape(n_zh * n_node, tall, 128),
-        ("zh", "node"),
-        split_axis=0,
-        concat_axis=0,
-        tiled=True,
-    )
-
+    )(place, near.reshape(n_zl, n_node, n_zh, tall, 128))
+    parts = [near_sum[0]] + [ring(near_sum[k], "zh", k) for k in range(1, n_zh)]
     gate_sum, up_sum = pl.pallas_call(
         functools.partial(final_kernel, n_copies, own),
         out_shape=[jax.ShapeDtypeStruct((own, hidden // 128, 128), F32)] * 2,
         compiler_params=params(),
         name="final",
-    )(parts.reshape(n_zh, n_node, tall, 128))
+    )(*parts)
     rows = own * hidden // 128
     return (
         input_grads.T,

time: 171 us -> 165 us (0.965)
  blocking collectives: 36.1 us -> 13.3 us
  starting transfers between devices: 42.6 us -> 57.4 us
  waiting for transfers between devices: 50.8 us -> 53.4 us
    all_to_all x1 -> x0, blocking collectives: 22.7 us -> none  [local(): lax.all_to_all(near_sum.reshape(n_zh * n_node, tall, 128), ('zh', 'node')...]
    ppermute x3 -> x5, waiting for transfers between devices: 15.7 us -> 28.6 us  [ring(): return lax.ppermute(x, axis, [(i, (i + step) % n) for i in range(n)])]
    ppermute x3 -> x5, starting transfers between devices: 10 us -> 22 us  [ring(): return lax.ppermute(x, axis, [(i, (i + step) % n) for i in range(n)])]
    all_gather x1, waiting for transfers between devices: 2.25 us -> 12.1 us  [local(): lax.all_gather(jnp.concatenate(copies_x, axis=0), 'node', axis=0, tiled=F...]
    all_to_all x1, waiting for transfers between devices: 9.51 us -> 0.01 us  [local(): lax.all_to_all(outgoing, 'local', split_axis=0, concat_axis=0, tiled=True)]
    all_to_all x1, waiting for transfers between devices: 8.84 us -> 0.01 us  [local(): lax.all_to_all(deltas, 'y', split_axis=0, concat_axis=0, tiled=True)]
    all_to_all x1, starting transfers between devices: 5.12 us -> 8.74 us  [local(): lax.all_to_all(grads.reshape(n_zl * n_node, n_zh, tall, 128), ('zl', 'nod...]
    all_to_all x1, starting transfers between devices: 12.9 us -> 10.1 us  [local(): lax.all_to_all(raw_parts, 'node', split_axis=0, concat_axis=0, tiled=True)]
  transfers between devices with their start and end apart: 11 -> 13, of which waited for: 8 -> 9; matrix products, arithmetic and copies ran while one was open for 0% -> 0% of each run, Pallas kernels for 6% -> 6%
where the time goes in v6:
time: 165 us; the launch traced here: 164 us
  starting transfers between devices  57.4 us (35%)
  waiting for transfers between devices  53.4 us (32%)
  Pallas kernels  17.7 us (11%)
  between operations  14.2 us (9%)
  blocking collectives  13.3 us (8%)
  local copies, waits for them, and re-layouts  7.22 us (4%)
    ppermute x5, waiting for transfers between devices, ring(): return lax.ppermute(x, axis, [(i, (i + step) % n) for i in range(n)])  28.6 us
    ppermute x5, starting transfers between devices, ring(): return lax.ppermute(x, axis, [(i, (i + step) % n) for i in range(n)])  22 us
    all_gather x1, blocking collectives, local(): raw = lax.all_gather(raw_share, 'node', axis=0, tiled=False)  13.3 us
    all_gather x1, waiting for transfers between devices, local(): lax.all_gather(jnp.concatenate(copies_x, axis=0), 'node', axis=0, tiled=F...  12.1 us
    all_to_all x1, starting transfers between devices, local(): lax.all_to_all(raw_parts, 'node', split_axis=0, concat_axis=0, tiled=True)  10.1 us
    all_to_all x1, starting transfers between devices, local(): lax.all_to_all(grads.reshape(n_zl * n_node, n_zh, tall, 128), ('zl', 'nod...  8.74 us
    ppermute x3, starting transfers between devices, local(): lax.ppermute(slot_input[k], 'local', [(i, i ^ k) for i in range(n_local)])  7.59 us
    all_to_all x1, waiting for transfers between devices, local(): lax.all_to_all(grads.reshape(n_zl * n_node, n_zh, tall, 128), ('zl', 'nod...  7.22 us
  transfers between devices with their start and end apart: 13, of which 9 were waited for; matrix products, arithmetic and copies ran while one was open for 0% of the time, Pallas kernels for 6%

profile of v6, /device:TPU:6, one launch (start us, length us, event | category | flops | bytes accessed | tf_op | source)
XLA Modules:
  0.0 164.2 jit_solution(731125692506271258)
XLA Ops:
  7.2 1.0 copy-done.7
  9.5 1.7 %dispatch.1 = bf16[4,72,960]{2,1,0:T(8,128)(2,1)} custom-call(s32[2,128]{1,0:T(2,128)S(1)} %bitcast.59, bf16[2,128]{1,0:T(2,128)(2,1)S(1)} %bitcast.61, bf16[960,128]{1,0:T(8,128)(2,1)S(1)} %bitcast.58), custom_call_target="tpu_custom_call" | custom-call | tf_op jit(solution)/shard_map/dispatch/pallas_call | solution.py:215
  11.2 3.5 %all-to-all-start = ((bf16[4,72,960]{2,1,0:T(8,128)(2,1)}), bf16[4,72,960]{2,1,0:T(8,128)(2,1)S(1)}, u32[]{:S(2)}, u32[]{:S(2)}) async-start(bf16[4,72,960]{2,1,0:T(8,128)(2,1)} %dispatch.1), calls=%async_computation | async-start | bytes 1179648 | tf_op jit(solution)/shard_map/all_to_all | solution.py:221
  14.8 1.3 early.1
  16.1 4.5 %collective-permute-start.1 = (bf16[288,240]{1,0:T(8,128)(2,1)S(1)}, bf16[288,240]{1,0:T(8,128)(2,1)S(1)}, u32[]{:S(2)}, u32[]{:S(2)}) collective-permute-start(bf16[288,240]{1,0:T(8,128)(2,1)S(1)} %get-tuple-element.44), channel_id=1, source_target_pairs={{0,192},{192,384},{384,576},{576,0},{1,193},{193,385},{385,577},{5... | collective-permute-start | bytes 414728 | tf_op jit(solution)/shard_map/ppermute | solution.py:189
  20.7 3.6 %collective-permute-start.2 = (bf16[288,240]{1,0:T(8,128)(2,1)S(1)}, bf16[288,240]{1,0:T(8,128)(2,1)S(1)}, u32[]{:S(2)}, u32[]{:S(2)}) collective-permute-start(bf16[288,240]{1,0:T(8,128)(2,1)S(1)} %get-tuple-element.43), channel_id=1, source_target_pairs={{0,576},{192,0},{384,192},{576,384},{1,577},{193,1},{385,193},{577... | collective-permute-start | bytes 414728 | tf_op jit(solution)/shard_map/ppermute | solution.py:189
  24.3 8.8 %collective-permute-done.1 = bf16[288,240]{1,0:T(8,128)(2,1)S(1)} collective-permute-done((bf16[288,240]{1,0:T(8,128)(2,1)S(1)}, bf16[288,240]{1,0:T(8,128)(2,1)S(1)}, u32[]{:S(2)}, u32[]{:S(2)}) %collective-permute-start.1) | collective-permute-done | bytes 138272 | tf_op jit(solution)/shard_map/ppermute | solution.py:189
  33.5 2.5 %raw.1 = bf16[4,288,256]{2,1,0:T(8,128)(2,1)} custom-call(bf16[288,960]{1,0:T(8,128)(2,1)S(1)} %bitcast.53, bf16[960,1024]{1,0:T(8,128)(2,1)S(1)} %bitcast.54), custom_call_target="tpu_custom_call" | custom-call | tf_op jit(solution)/shard_map/raw/pallas_call | solution.py:236
  36.1 10.1 %all-to-all-start.1 = ((bf16[4,288,256]{2,1,0:T(8,128)(2,1)}), bf16[4,288,256]{2,1,0:T(8,128)(2,1)S(1)}, u32[]{:S(2)}, u32[]{:S(2)}) async-start(bf16[4,288,256]{2,1,0:T(8,128)(2,1)} %raw.1), calls=%async_computation.1 | async-start | bytes 1179648 | tf_op jit(solution)/shard_map/all_to_all | solution.py:248
  46.2 4.2 %collective-permute-start = (bf16[288,240]{1,0:T(8,128)(2,1)S(1)}, bf16[288,240]{1,0:T(8,128)(2,1)S(1)}, u32[]{:S(2)}, u32[]{:S(2)}) collective-permute-start(bf16[288,240]{1,0:T(8,128)(2,1)S(1)} %get-tuple-element.45), channel_id=1, source_target_pairs={{0,384},{192,576},{384,0},{576,192},{1,385},{193,577},{385,1},{577... | collective-permute-start | bytes 414728 | tf_op jit(solution)/shard_map/ppermute | solution.py:189
  50.4 7.5 %collective-permute-done = bf16[288,240]{1,0:T(8,128)(2,1)S(1)} collective-permute-done((bf16[288,240]{1,0:T(8,128)(2,1)S(1)}, bf16[288,240]{1,0:T(8,128)(2,1)S(1)}, u32[]{:S(2)}, u32[]{:S(2)}) %collective-permute-start) | collective-permute-done | bytes 138272 | tf_op jit(solution)/shard_map/ppermute | solution.py:189
  57.9 0.9 pad_maximum_fusion
  58.9 1.8 %share.1 = (bf16[288,256]{1,0:T(8,128)(2,1)S(1)}, bf16[4,288,512]{2,1,0:T(8,128)(2,1)}) custom-call(s32[4]{0:T(128)S(1)} %pad_add_fusion.place_ref, bf16[4,288,256]{2,1,0:T(8,128)(2,1)S(1)} %all-to-all-done.1.parts_ref, bf16[288,1024]{1,0:T(8,128)(2,1)S(1)} %bitcast.48, bf16[288,1024]{1,0:T(8,128)(2,1)S(1)} %bitcast.50), custom_call_target="tpu_custom_call" | custom-call | tf_op jit(solution)/shard_map/share/pallas_call | solution.py:253
  60.7 5.5 %all-to-all-start.2 = ((bf16[4,288,512]{2,1,0:T(8,128)(2,1)}), bf16[4,288,512]{2,1,0:T(8,128)(2,1)S(1)}, u32[]{:S(2)}, u32[]{:S(2)}) async-start(bf16[4,288,512]{2,1,0:T(8,128)(2,1)} %get-tuple-element.24), calls=%async_computation.2 | async-start | bytes 2359296 | tf_op jit(solution)/shard_map/all_to_all | solution.py:263
  66.1 13.3 %all-gather = bf16[1152,256]{1,0:T(8,128)(2,1)S(1)} all-gather(bf16[288,256]{1,0:T(8,128)(2,1)S(1)} %get-tuple-element.25), channel_id=2, replica_groups=mesh['y'=4,'zh'=3,'zl'=4,'node'=4,'local'=4] {'node'}, dimensions={0}, use_global_device_ids=true | all-gather | bytes 737280 | tf_op jit(solution)/shard_map/all_gather | solution.py:265
  79.4 1.5 copy-done.4
  81.0 1.6 copy-done.5
  82.5 3.8 %slot_input.1 = bf16[4,72,1024]{2,1,0:T(8,128)(2,1)S(1)} custom-call(s32[4]{0:T(128)S(1)} %pad_add_fusion.place_ref, bf16[4,288,256]{2,1,0:T(8,128)(2,1)S(1)} %bitcast.47, bf16[288,1024]{1,0:T(8,128)(2,1)S(1)} %bitcast.49, bf16[288,1024]{1,0:T(8,128)(2,1)S(1)} %bitcast.51, bf16[960,1024]{1,0:T(8,128)(2,1)S(1)} %bitcast.55, bf16[960,1024]{1,0:T(8,128)(2,1)S(1)} %bitcast.56), custom_call_target="tpu_custom_call" | custom-call | tf_op jit(solution)/shard_map/slot_input/pallas_call | solution.py:266
  86.3 12.1 %all-gather.4.cloned.1.call-done = bf16[4608,240]{1,0:T(8,128)(2,1)} async-done(((bf16[1152,240]{1,0:T(8,128)(2,1)}), bf16[4608,240]{1,0:T(8,128)(2,1)}) %all-gather.4.cloned.1.call-update) | async-done | bytes 2211856 | tf_op jit(solution)/shard_map/all_gather | solution.py:251
  98.4 1.7 %copy-done.2 = bf16[4608,240]{1,0:T(8,128)(2,1)S(1)} copy-done((bf16[4608,240]{1,0:T(8,128)(2,1)S(1)}, bf16[4608,240]{1,0:T(8,128)(2,1)}, u32[]{:S(2)}) %copy-start.2) | copy-done | bytes 2211864
  100.0 3.0 %grads.1 = bf16[4,4,3,80,128]{4,3,2,1,0:T(8,128)(2,1)} custom-call(s32[4]{0:T(128)S(1)} %pad_add_fusion.place_ref, bf16[4,288,512]{2,1,0:T(8,128)(2,1)S(1)} %all-to-all-done.2.delta_ref, bf16[4,1152,240]{2,1,0:T(8,128)(2,1)S(1)} %bitcast.52), custom_call_target="tpu_custom_call" | custom-call | tf_op jit(solution)/shard_map/grads/pallas_call | solution.py:286
  103.0 8.7 %all-to-all-start.3 = ((bf16[16,3,80,128]{3,2,1,0:T(8,128)(2,1)}), bf16[16,3,80,128]{3,2,1,0:T(8,128)(2,1)S(1)}, u32[]{:S(2)}, u32[]{:S(2)}) async-start(bf16[16,3,80,128]{3,2,1,0:T(8,128)(2,1)} %bitcast.21), calls=%async_computation.3 | async-start | bytes 1966080 | tf_op jit(solution)/shard_map/all_to_all | solution.py:294
  111.8 1.9 %collective-permute-start.3 = (bf16[72,1024]{1,0:T(8,128)(2,1)S(1)}, bf16[72,1024]{1,0:T(8,128)(2,1)S(1)}, u32[]{:S(2)}, u32[]{:S(2)}) collective-permute-start(bf16[72,1024]{1,0:T(8,128)(2,1)S(1)} %get-tuple-element.40), channel_id=1, source_target_pairs={{0,1},{1,0},{2,3},{3,2},{4,5},{5,4},{6,7},{7,6},{8,9},{9,8},{10,11... | collective-permute-start | bytes 442376 | tf_op jit(solution)/shard_map/ppermute | solution.py:302
  113.7 3.4 %collective-permute-start.4 = (bf16[72,1024]{1,0:T(8,128)(2,1)S(1)}, bf16[72,1024]{1,0:T(8,128)(2,1)S(1)}, u32[]{:S(2)}, u32[]{:S(2)}) collective-permute-start(bf16[72,1024]{1,0:T(8,128)(2,1)S(1)} %get-tuple-element.39), channel_id=1, source_target_pairs={{0,2},{1,3},{2,0},{3,1},{4,6},{5,7},{6,4},{7,5},{8,10},{9,11},{10,... | collective-permute-start | bytes 442376 | tf_op jit(solution)/shard_map/ppermute | solution.py:302
  117.1 2.3 %collective-permute-start.5 = (bf16[72,1024]{1,0:T(8,128)(2,1)S(1)}, bf16[72,1024]{1,0:T(8,128)(2,1)S(1)}, u32[]{:S(2)}, u32[]{:S(2)}) collective-permute-start(bf16[72,1024]{1,0:T(8,128)(2,1)S(1)} %get-tuple-element.38), channel_id=1, source_target_pairs={{0,3},{1,2},{2,1},{3,0},{4,7},{5,6},{6,5},{7,4},{8,11},{9,10},{10,... | collective-permute-start | bytes 442376 | tf_op jit(solution)/shard_map/ppermute | solution.py:302
  119.4 2.5 %collective-permute-done.4.rest_2_ = bf16[72,1024]{1,0:T(8,128)(2,1)S(1)} collective-permute-done((bf16[72,1024]{1,0:T(8,128)(2,1)S(1)}, bf16[72,1024]{1,0:T(8,128)(2,1)S(1)}, u32[]{:S(2)}, u32[]{:S(2)}) %collective-permute-start.4) | collective-permute-done | bytes 147488 | tf_op jit(solution)/shard_map/ppermute | solution.py:302
  121.9 3.0 %collective-permute-done.5.rest_3_ = bf16[72,1024]{1,0:T(8,128)(2,1)S(1)} collective-permute-done((bf16[72,1024]{1,0:T(8,128)(2,1)S(1)}, bf16[72,1024]{1,0:T(8,128)(2,1)S(1)}, u32[]{:S(2)}, u32[]{:S(2)}) %collective-permute-start.5) | collective-permute-done | bytes 147488 | tf_op jit(solution)/shard_map/ppermute | solution.py:302
  124.9 2.2 %combine.1 = (bf16[960,128]{1,0:T(8,128)(2,1)}, bf16[2,128]{1,0:T(2,128)(2,1)}) custom-call(s32[4]{0:T(128)S(1)} %pad_add_fusion.place_ref, s32[2,128]{1,0:T(2,128)S(1)} %bitcast.60, bf16[2,128]{1,0:T(2,128)(2,1)S(1)} %bitcast.62, bf16[72,1024]{1,0:T(8,128)(2,1)S(1)} %get-tuple-element.41.rest_0_, bf16[72,1024]{1,0:T(8,128)(2,1)S(1)} %collective-permute-done.3.rest_1_, ...), custom_call_target="tpu_custom_call" | custom-call | tf_op jit(solution)/shard_map/combine/pallas_call | solution.py:305
  127.1 7.2 %all-to-all-done.3 = bf16[16,3,80,128]{3,2,1,0:T(8,128)(2,1)S(1)} async-done(((bf16[16,3,80,128]{3,2,1,0:T(8,128)(2,1)}), bf16[16,3,80,128]{3,2,1,0:T(8,128)(2,1)S(1)}, u32[]{:S(2)}, u32[]{:S(2)}) %all-to-all-start.3) | async-done | bytes 983072 | tf_op jit(solution)/shard_map/all_to_all | solution.py:294
  135.0 7.7 %collective-permute-start.6 = (bf16[4,80,128]{2,1,0:T(8,128)(2,1)S(1)}, bf16[4,80,128]{2,1,0:T(8,128)(2,1)S(1)}, u32[]{:S(2)}, u32[]{:S(2)}) collective-permute-start(bf16[4,80,128]{2,1,0:T(8,128)(2,1)S(1)} %get-tuple-element.47), channel_id=1, source_target_pairs={{0,64},{64,128},{128,0},{1,65},{65,129},{129,1},{2,66},{66,130},{1... | collective-permute-start | bytes 245768 | tf_op jit(solution)/shard_map/ppermute | solution.py:189
  142.7 2.1 %collective-permute-start.7 = (bf16[4,80,128]{2,1,0:T(8,128)(2,1)S(1)}, bf16[4,80,128]{2,1,0:T(8,128)(2,1)S(1)}, u32[]{:S(2)}, u32[]{:S(2)}) collective-permute-start(bf16[4,80,128]{2,1,0:T(8,128)(2,1)S(1)} %get-tuple-element.46), channel_id=1, source_target_pairs={{0,128},{64,0},{128,64},{1,129},{65,1},{129,65},{2,130},{66,2},{13... | collective-permute-start | bytes 245768 | tf_op jit(solution)/shard_map/ppermute | solution.py:189
  145.4 11.1 %collective-permute-done.7.refs_2_ = bf16[4,80,128]{2,1,0:T(8,128)(2,1)S(1)} collective-permute-done((bf16[4,80,128]{2,1,0:T(8,128)(2,1)S(1)}, bf16[4,80,128]{2,1,0:T(8,128)(2,1)S(1)}, u32[]{:S(2)}, u32[]{:S(2)}) %collective-permute-start.7) | collective-permute-done | bytes 81952 | tf_op jit(solution)/shard_map/ppermute | solution.py:189
  (34 shorter events, 4.1 us)
Async XLA Ops:
  7.2 7.6 %copy-start.6 = (bf16[1,1,4,72,960]{4,3,2,1,0:T(8,128)(2,1)S(1)}, bf16[1,1,4,72,960]{4,3,2,1,0:T(8,128)(2,1)}, u32[]{:S(2)}) copy-start(bf16[1,1,4,72,960]{4,3,2,1,0:T(8,128)(2,1)} %param.12) | copy-start | bytes 1658884
  7.2 1.0 copy-start.7
  8.2 0.7 copy-start.8
  8.9 0.7 copy-start.10
  11.2 22.3 %all-to-all-start = ((bf16[4,72,960]{2,1,0:T(8,128)(2,1)}), bf16[4,72,960]{2,1,0:T(8,128)(2,1)S(1)}, u32[]{:S(2)}, u32[]{:S(2)}) async-start(bf16[4,72,960]{2,1,0:T(8,128)(2,1)} %dispatch.1), calls=%async_computation | async-start | bytes 1179648 | tf_op jit(solution)/shard_map/all_to_all | solution.py:221
  14.8 18.8 %copy-start.3 = (bf16[1,1024,960]{1,2,0:T(8,128)(2,1)S(1)}, bf16[1,1024,960]{1,2,0:T(8,128)(2,1)}, u32[]{:S(2)}) copy-start(bf16[1,1024,960]{1,2,0:T(8,128)(2,1)} %param.17) | copy-start | bytes 5898244
  16.1 16.9 %collective-permute-start.1 = (bf16[288,240]{1,0:T(8,128)(2,1)S(1)}, bf16[288,240]{1,0:T(8,128)(2,1)S(1)}, u32[]{:S(2)}, u32[]{:S(2)}) collective-permute-start(bf16[288,240]{1,0:T(8,128)(2,1)S(1)} %get-tuple-element.44), channel_id=1, source_target_pairs={{0,192},{192,384},{384,576},{576,0},{1,193},{193,385},{385,577},{5... | collective-permute-start | bytes 414728 | tf_op jit(solution)/shard_map/ppermute | solution.py:189
  20.7 12.9 %collective-permute-start.2 = (bf16[288,240]{1,0:T(8,128)(2,1)S(1)}, bf16[288,240]{1,0:T(8,128)(2,1)S(1)}, u32[]{:S(2)}, u32[]{:S(2)}) collective-permute-start(bf16[288,240]{1,0:T(8,128)(2,1)S(1)} %get-tuple-element.43), channel_id=1, source_target_pairs={{0,576},{192,0},{384,192},{576,384},{1,577},{193,1},{385,193},{577... | collective-permute-start | bytes 414728 | tf_op jit(solution)/shard_map/ppermute | solution.py:189
  36.1 21.9 %all-to-all-start.1 = ((bf16[4,288,256]{2,1,0:T(8,128)(2,1)}), bf16[4,288,256]{2,1,0:T(8,128)(2,1)S(1)}, u32[]{:S(2)}, u32[]{:S(2)}) async-start(bf16[4,288,256]{2,1,0:T(8,128)(2,1)} %raw.1), calls=%async_computation.1 | async-start | bytes 1179648 | tf_op jit(solution)/shard_map/all_to_all | solution.py:248
  46.2 12.6 %copy-start = (bf16[1,1,4,72,1024]{4,3,2,1,0:T(8,128)(2,1)S(1)}, bf16[1,1,4,72,1024]{4,3,2,1,0:T(8,128)(2,1)}, u32[]{:S(2)}) copy-start(bf16[1,1,4,72,1024]{4,3,2,1,0:T(8,128)(2,1)} %param.13) | copy-start | bytes 1769476
  46.2 12.6 %copy-start.1 = (bf16[1,1,4,72,1024]{4,3,2,1,0:T(8,128)(2,1)S(1)}, bf16[1,1,4,72,1024]{4,3,2,1,0:T(8,128)(2,1)}, u32[]{:S(2)}) copy-start(bf16[1,1,4,72,1024]{4,3,2,1,0:T(8,128)(2,1)} %param.14) | copy-start | bytes 1769476
  46.2 52.2 %all-gather.4.cloned.1.call-start = ((), (), s32[]{:S(2)}) async-start(), calls=%async_computation.4 | async-start | bytes 2949120 | tf_op jit(solution)/shard_map/all_gather | solution.py:251
  46.2 11.7 %collective-permute-start = (bf16[288,240]{1,0:T(8,128)(2,1)S(1)}, bf16[288,240]{1,0:T(8,128)(2,1)S(1)}, u32[]{:S(2)}, u32[]{:S(2)}) collective-permute-start(bf16[288,240]{1,0:T(8,128)(2,1)S(1)} %get-tuple-element.45), channel_id=1, source_target_pairs={{0,384},{192,576},{384,0},{576,192},{1,385},{193,577},{385,1},{577... | collective-permute-start | bytes 414728 | tf_op jit(solution)/shard_map/ppermute | solution.py:189
  60.7 25.6 %all-to-all-start.2 = ((bf16[4,288,512]{2,1,0:T(8,128)(2,1)}), bf16[4,288,512]{2,1,0:T(8,128)(2,1)S(1)}, u32[]{:S(2)}, u32[]{:S(2)}) async-start(bf16[4,288,512]{2,1,0:T(8,128)(2,1)} %get-tuple-element.24), calls=%async_computation.2 | async-start | bytes 2359296 | tf_op jit(solution)/shard_map/all_to_all | solution.py:263
  79.4 1.5 copy-start.4
  81.0 1.6 copy-start.5
  98.4 1.7 %copy-start.2 = (bf16[4608,240]{1,0:T(8,128)(2,1)S(1)}, bf16[4608,240]{1,0:T(8,128)(2,1)}, u32[]{:S(2)}) copy-start(bf16[4608,240]{1,0:T(8,128)(2,1)} %all-gather.4.cloned.1.call-done) | copy-start | bytes 6635524
  103.0 21.9 %copy-start.9 = (s32[128,2]{0,1:T(2,128)S(1)}, s32[128,2]{0,1:T(2,128)}, u32[]{:S(2)}) copy-start(s32[128,2]{0,1:T(2,128)} %param.10) | copy-start | bytes 3076
  103.0 21.9 %copy-start.11 = (bf16[128,2]{0,1:T(2,128)(2,1)S(1)}, bf16[128,2]{0,1:T(2,128)(2,1)}, u32[]{:S(2)}) copy-start(bf16[128,2]{0,1:T(2,128)(2,1)} %param.11) | copy-start | bytes 1540
  103.0 31.3 %all-to-all-start.3 = ((bf16[16,3,80,128]{3,2,1,0:T(8,128)(2,1)}), bf16[16,3,80,128]{3,2,1,0:T(8,128)(2,1)S(1)}, u32[]{:S(2)}, u32[]{:S(2)}) async-start(bf16[16,3,80,128]{3,2,1,0:T(8,128)(2,1)} %bitcast.21), calls=%async_computation.3 | async-start | bytes 1966080 | tf_op jit(solution)/shard_map/all_to_all | solution.py:294
  111.8 7.6 %collective-permute-start.3 = (bf16[72,1024]{1,0:T(8,128)(2,1)S(1)}, bf16[72,1024]{1,0:T(8,128)(2,1)S(1)}, u32[]{:S(2)}, u32[]{:S(2)}) collective-permute-start(bf16[72,1024]{1,0:T(8,128)(2,1)S(1)} %get-tuple-element.40), channel_id=1, source_target_pairs={{0,1},{1,0},{2,3},{3,2},{4,5},{5,4},{6,7},{7,6},{8,9},{9,8},{10,11... | collective-permute-start | bytes 442376 | tf_op jit(solution)/shard_map/ppermute | solution.py:302
  113.7 8.1 %collective-permute-start.4 = (bf16[72,1024]{1,0:T(8,128)(2,1)S(1)}, bf16[72,1024]{1,0:T(8,128)(2,1)S(1)}, u32[]{:S(2)}, u32[]{:S(2)}) collective-permute-start(bf16[72,1024]{1,0:T(8,128)(2,1)S(1)} %get-tuple-element.39), channel_id=1, source_target_pairs={{0,2},{1,3},{2,0},{3,1},{4,6},{5,7},{6,4},{7,5},{8,10},{9,11},{10,... | collective-permute-start | bytes 442376 | tf_op jit(solution)/shard_map/ppermute | solution.py:302
  117.1 7.7 %collective-permute-start.5 = (bf16[72,1024]{1,0:T(8,128)(2,1)S(1)}, bf16[72,1024]{1,0:T(8,128)(2,1)S(1)}, u32[]{:S(2)}, u32[]{:S(2)}) collective-permute-start(bf16[72,1024]{1,0:T(8,128)(2,1)S(1)} %get-tuple-element.38), channel_id=1, source_target_pairs={{0,3},{1,2},{2,1},{3,0},{4,7},{5,6},{6,5},{7,4},{8,11},{9,10},{10,... | collective-permute-start | bytes 442376 | tf_op jit(solution)/shard_map/ppermute | solution.py:302
  135.0 10.5 %collective-permute-start.6 = (bf16[4,80,128]{2,1,0:T(8,128)(2,1)S(1)}, bf16[4,80,128]{2,1,0:T(8,128)(2,1)S(1)}, u32[]{:S(2)}, u32[]{:S(2)}) collective-permute-start(bf16[4,80,128]{2,1,0:T(8,128)(2,1)S(1)} %get-tuple-element.47), channel_id=1, source_target_pairs={{0,64},{64,128},{128,0},{1,65},{65,129},{129,1},{2,66},{66,130},{1... | collective-permute-start | bytes 245768 | tf_op jit(solution)/shard_map/ppermute | solution.py:189
  142.7 13.9 %collective-permute-start.7 = (bf16[4,80,128]{2,1,0:T(8,128)(2,1)S(1)}, bf16[4,80,128]{2,1,0:T(8,128)(2,1)S(1)}, u32[]{:S(2)}, u32[]{:S(2)}) collective-permute-start(bf16[4,80,128]{2,1,0:T(8,128)(2,1)S(1)} %get-tuple-element.46), channel_id=1, source_target_pairs={{0,128},{64,0},{128,64},{1,129},{65,1},{129,65},{2,130},{66,2},{13... | collective-permute-start | bytes 245768 | tf_op jit(solution)/shard_map/ppermute | solution.py:189
Sparse Core Ops, SparseCore 0:
  59.0 39.3 all-gather.3

commit v7 on v5

--- a/solution.py
+++ b/solution.py
@@ -34,10 +34,22 @@
     return masks
 
 
-def dispatch_kernel(n_local, capacity, routes_ref, gates_ref, rows_ref, out_ref):
+def dispatch_kernel(
+    n_local, capacity, routes_in, gates_in, rows_in, out_ref, routes_ref, gates_ref, rows_ref, sems
+):
+    copies = [
+        pltpu.make_async_copy(routes_in, routes_ref, sems.at[0]),
+        pltpu.make_async_copy(gates_in, gates_ref, sems.at[1]),
+        pltpu.make_async_copy(rows_in, rows_ref, sems.at[2]),
+    ]
+    for copy in copies:
+        copy.start()
+    copies[0].wait()
     masks = picks_of(routes_ref[...].T, n_local, capacity)
+    copies[1].wait()
     gates = gates_ref[...].astype(F32).T
     scaled = sum(jnp.where(m, gates[:, k : k + 1], 0.0) for k, m in enumerate(masks)).astype(BF)
+    copies[2].wait()
     out = lax.dot_general(
         scaled, rows_ref[...], (((0,), (1,)), ((), ())), preferred_element_type=F32
     ).astype(BF)
@@ -68,8 +80,8 @@
     delta_ref[:, quarter:] = up_delta
 
 
-def grads_kernel(own, place_ref, own_ref, prev_ref, next_ref, half_refs, delta_ref, out_ref):
-    step = pl.program_id(0)
+def grads_kernel(own, place_ref, delta_ref, *refs):
+    out_ref = refs[-1]
     n_z, n_y = out_ref.shape[:2]
 
     def block(x):
@@ -83,15 +95,20 @@
             )
             out_ref[i % n_z, i // n_z, 0] = tall.astype(BF)
 
-    for k, ref in enumerate((own_ref, prev_ref, next_ref)):
+    if len(refs) == 4:
+        block(jnp.concatenate([refs[0][...], refs[1][...]], axis=0))
+        return
+    step = pl.program_id(0)
+
+    @pl.when(step == 0)
+    def _():
+        block(refs[0][...])
+
+    for k in (1, 2):
 
         @pl.when(step == k)
-        def _(ref=ref):
-            block(ref[...])
-
-    @pl.when(step == 3)
-    def _():
-        block(jnp.concatenate([half_refs[0][...], half_refs[1][...]], axis=0))
+        def _(k=k):
+            block(jnp.concatenate([refs[2 * k - 1][...], refs[2 * k][...]], axis=0))
 
 
 def input_kernel(capacity, place_ref, raw_ref, gate_ref, up_ref, wg_ref, wu_ref, out_ref, total, side):
@@ -193,14 +210,24 @@
 
     outgoing = pl.pallas_call(
         functools.partial(dispatch_kernel, n_local, capacity),
+        in_specs=[pl.BlockSpec(memory_space=pl.ANY)] * 3,
+        scratch_shapes=[
+            pltpu.VMEM((top, tokens), jnp.int32),
+            pltpu.VMEM((top, tokens), BF),
+            pltpu.VMEM((feat, tokens), BF),
+            pltpu.SemaphoreType.DMA((3,)),
+        ],
         out_shape=jax.ShapeDtypeStruct((n_local, capacity, feat), BF),
-        compiler_params=params(),
+        compiler_params=params(56),
         name="dispatch",
     )(routes.T, gates.T, token_grads.T)
     arrived = lax.all_to_all(outgoing, "local", split_axis=0, concat_axis=0, tiled=True)
 
+    half = slots // 2
     x_rows, _ = lax.optimization_barrier((x_rows, outgoing))
-    x_prev, x_next = ring(x_rows, "node", 1), ring(x_rows, "node", -1)
+    x_halves = (x_rows[:half], x_rows[half:])
+    x_prev = [ring(x, "node", 1) for x in x_halves]
+    x_next = [ring(x, "node", -1) for x in x_halves]
 
     raw_parts = pl.pallas_call(
         raw_kernel,
@@ -216,9 +243,8 @@
     )(arrived.reshape(slots, feat), w_down[0].T)
     raw_shares = lax.all_to_all(raw_parts, "node", split_axis=0, concat_axis=0, tiled=True)
 
-    half = slots // 2
-    x_prev, x_next, _ = lax.optimization_barrier((x_prev, x_next, raw_parts))
-    x_across = (ring(x_prev[:half], "node", 1), ring(x_next[half:], "node", -1))
+    x_prev[0], x_next[1], _ = lax.optimization_barrier((x_prev[0], x_next[1], raw_parts))
+    x_across = (ring(x_prev[0], "node", 1), ring(x_next[1], "node", -1))
 
     raw_share, deltas = pl.pallas_call(
         share_kernel,
@@ -232,27 +258,28 @@
     )(place, raw_shares, gate_rows, up_rows)
 
     tall = own * 2 * quarter // 128
-    grads = pl.pallas_call(
-        functools.partial(grads_kernel, own),
-        grid_spec=pltpu.PrefetchScalarGridSpec(
-            num_scalar_prefetch=1,
-            grid=(n_node,),
-            in_specs=[
-                pl.BlockSpec((slots, feat), lambda i, p: (0, 0)),
-                pl.BlockSpec((slots, feat), lambda i, p: (0, 0)),
-                pl.BlockSpec((slots, feat), lambda i, p: (0, 0)),
-                [pl.BlockSpec((half, feat), lambda i, p: (0, 0))] * 2,
-                pl.BlockSpec((slots, 2 * quarter), lambda i, p: (0, 0)),
-            ],
-            out_specs=pl.BlockSpec(
-                (n_z, n_y, 1, tall, 128),
-                lambda i, p: (0, 0, (p[1] + jnp.where(i < 2, 3 * i, i - 1)) % n_node, 0, 0),
+    def products(count, pieces, turn, before):
+        return pl.pallas_call(
+            functools.partial(grads_kernel, own),
+            grid_spec=pltpu.PrefetchScalarGridSpec(
+                num_scalar_prefetch=1,
+                grid=(count,),
+                in_specs=[pl.BlockSpec((slots, 2 * quarter), lambda i, p: (0, 0))]
+                + [pl.BlockSpec(x.shape, lambda i, p: (0, 0)) for x in pieces]
+                + [pl.BlockSpec(memory_space=pl.ANY)] * len(before),
+                out_specs=pl.BlockSpec(
+                    (n_z, n_y, 1, tall, 128),
+                    lambda i, p: (0, 0, (p[1] + turn(i)) % n_node, 0, 0),
+                ),
             ),
-        ),
-        out_shape=jax.ShapeDtypeStruct((n_z, n_y, n_node, tall, 128), BF),
-        compiler_params=params(),
-        name="grads",
-    )(place, x_rows, x_prev, x_next, list(x_across), deltas)
+            out_shape=jax.ShapeDtypeStruct((n_z, n_y, n_node, tall, 128), BF),
+            input_output_aliases={2 + len(pieces): 0} if before else {},
+            compiler_params=params(56),
+            name="grads",
+        )(place, deltas, *pieces, *before)
+
+    grads = products(3, (x_rows, *x_prev, *x_next), lambda i: jnp.where(i < 2, 3 * i, 1), ())
+    grads = products(1, x_across, lambda i: 2 + i, (grads,))
     z_sum = lax.psum_scatter(
         grads.reshape(n_z * n_y * n_node * tall, 128), "z", scatter_dimension=0, tiled=True
     )

time: 161 us -> 159 us (0.988)
  waiting for transfers between devices: 44.7 us -> 38.9 us
  Pallas kernels: 16.7 us -> 21.9 us
  local copies, waits for them, and re-layouts: 9.18 us -> 5.46 us
  starting transfers between devices: 41.3 us -> 44.3 us
    ppermute x4 -> x6, waiting for transfers between devices: 7.63 us -> 2.07 us  [ring(): return lax.ppermute(x, axis, [(i, (i + step) % n) for i in range(n)])]
    pallas_call x2 -> x3, Pallas kernels: 6.67 us -> 11.9 us  [the longest x2 9.24 us: products(): pl.pallas_call(functools.partial(grads_kernel, own), grid_spec=pltpu.Pref...]
    ppermute x4 -> x6, starting transfers between devices: 20.8 us -> 25 us  [ring(): return lax.ppermute(x, axis, [(i, (i + step) % n) for i in range(n)])]
    unnamed x28 -> x30, local copies, waits for them, and re-layouts: 6.73 us -> 4.54 us
  transfers between devices with their start and end apart: 10 -> 12, of which waited for: 6 -> 4; matrix products, arithmetic and copies ran while one was open for 2% -> 1% of each run, Pallas kernels for 6% -> 9%
where the time goes in v7:
time: 159 us; the launch traced here: 158 us
  starting transfers between devices  44.3 us (28%)
  waiting for transfers between devices  38.9 us (24%)
  blocking collectives  32.9 us (21%)
  Pallas kernels  21.9 us (14%)
  between operations  14.3 us (9%)
  local copies, waits for them, and re-layouts  5.46 us (3%)
    reduce_scatter x1, waiting for transfers between devices, local(): lax.psum_scatter(grads.reshape(n_z * n_y * n_node * tall, 128), 'z', scat...  33.9 us
    ppermute x6, starting transfers between devices, ring(): return lax.ppermute(x, axis, [(i, (i + step) % n) for i in range(n)])  25 us
    all_to_all x1, blocking collectives, local(): lax.all_to_all(z_sum.reshape(n_y * n_node, tall, 128), ('y', 'node'), spl...  19.3 us
    all_gather x1, blocking collectives, local(): raw = lax.all_gather(raw_share, 'node', axis=0, tiled=False)  13.6 us
    pallas_call x2, Pallas kernels, products(): pl.pallas_call(functools.partial(grads_kernel, own), grid_spec=pltpu.Pref...  9.24 us
    all_to_all x1, starting transfers between devices, local(): lax.all_to_all(raw_parts, 'node', split_axis=0, concat_axis=0, tiled=True)  8.23 us
    ppermute x3, starting transfers between devices, local(): lax.ppermute(slot_input[k], 'local', [(i, i ^ k) for i in range(n_local)])  7.59 us
    unnamed x30, local copies, waits for them, and re-layouts  4.54 us
  transfers between devices with their start and end apart: 12, of which 4 were waited for; matrix products, arithmetic and copies ran while one was open for 1% of the time, Pallas kernels for 9%

profile of v7, /device:TPU:6, one launch (start us, length us, event | category | flops | bytes accessed | tf_op | source)
XLA Modules:
  0.0 157.7 jit_solution(8877146723197646396)
XLA Ops:
  7.2 2.6 %dispatch.1 = bf16[4,72,960]{2,1,0:T(8,128)(2,1)} custom-call(s32[2,128]{1,0:T(2,128)} %bitcast.41, bf16[2,128]{1,0:T(2,128)(2,1)} %bitcast.43, bf16[960,128]{1,0:T(8,128)(2,1)} %bitcast.49), custom_call_target="tpu_custom_call" | custom-call | tf_op jit(solution)/shard_map/dispatch/pallas_call | solution.py:211
  9.8 3.5 %all-to-all-start = ((bf16[4,72,960]{2,1,0:T(8,128)(2,1)}), bf16[4,72,960]{2,1,0:T(8,128)(2,1)S(1)}, u32[]{:S(2)}, u32[]{:S(2)}) async-start(bf16[4,72,960]{2,1,0:T(8,128)(2,1)} %dispatch.1), calls=%async_computation | async-start | bytes 1179648 | tf_op jit(solution)/shard_map/all_to_all | solution.py:224
  13.3 0.9 fusion
  14.2 2.7 %collective-permute-start.1 = (bf16[144,960]{1,0:T(8,128)(2,1)}, bf16[144,960]{1,0:T(8,128)(2,1)S(1)}, u32[]{:S(2)}, u32[]{:S(2)}) collective-permute-start(bf16[144,960]{1,0:T(8,128)(2,1)} %get-tuple-element.34), channel_id=1, source_target_pairs={{0,12},{4,0},{8,4},{12,8},{1,13},{5,1},{9,5},{13,9},{2,14},{6,2},{... | collective-permute-start | bytes 829448 | tf_op jit(solution)/shard_map/ppermute | solution.py:186
  16.9 10.6 %collective-permute-start = (bf16[144,960]{1,0:T(8,128)(2,1)}, bf16[144,960]{1,0:T(8,128)(2,1)S(1)}, u32[]{:S(2)}, u32[]{:S(2)}) collective-permute-start(bf16[144,960]{1,0:T(8,128)(2,1)} %get-tuple-element.35), channel_id=1, source_target_pairs={{0,4},{4,8},{8,12},{12,0},{1,5},{5,9},{9,13},{13,1},{2,6},{6,10},{... | collective-permute-start | bytes 829448 | tf_op jit(solution)/shard_map/ppermute | solution.py:186
  27.5 1.5 copy-done.2
  29.1 2.5 %raw.1 = bf16[4,288,256]{2,1,0:T(8,128)(2,1)} custom-call(bf16[288,960]{1,0:T(8,128)(2,1)S(1)} %bitcast.36, bf16[960,1024]{1,0:T(8,128)(2,1)S(1)} %bitcast.37), custom_call_target="tpu_custom_call" | custom-call | tf_op jit(solution)/shard_map/raw/pallas_call | solution.py:232
  31.6 8.2 %all-to-all-start.1 = ((bf16[4,288,256]{2,1,0:T(8,128)(2,1)}), bf16[4,288,256]{2,1,0:T(8,128)(2,1)S(1)}, u32[]{:S(2)}, u32[]{:S(2)}) async-start(bf16[4,288,256]{2,1,0:T(8,128)(2,1)} %raw.1), calls=%async_computation.1 | async-start | bytes 1179648 | tf_op jit(solution)/shard_map/all_to_all | solution.py:244
  39.8 2.0 %collective-permute-start.4 = (bf16[144,960]{1,0:T(8,128)(2,1)}, bf16[144,960]{1,0:T(8,128)(2,1)S(1)}, u32[]{:S(2)}, u32[]{:S(2)}) collective-permute-start(bf16[144,960]{1,0:T(8,128)(2,1)} %get-tuple-element.34), channel_id=1, source_target_pairs={{0,4},{4,8},{8,12},{12,0},{1,5},{5,9},{9,13},{13,1},{2,6},{6,10},{... | collective-permute-start | bytes 829448 | tf_op jit(solution)/shard_map/ppermute | solution.py:186
  41.8 3.8 %collective-permute-start.5 = (bf16[144,960]{1,0:T(8,128)(2,1)}, bf16[144,960]{1,0:T(8,128)(2,1)S(1)}, u32[]{:S(2)}, u32[]{:S(2)}) collective-permute-start(bf16[144,960]{1,0:T(8,128)(2,1)} %get-tuple-element.35), channel_id=1, source_target_pairs={{0,12},{4,0},{8,4},{12,8},{1,13},{5,1},{9,5},{13,9},{2,14},{6,2},{... | collective-permute-start | bytes 829448 | tf_op jit(solution)/shard_map/ppermute | solution.py:186
  45.7 3.2 %collective-permute-start.2 = (bf16[144,960]{1,0:T(8,128)(2,1)S(1)}, bf16[144,960]{1,0:T(8,128)(2,1)}, u32[]{:S(2)}, u32[]{:S(2)}) collective-permute-start(bf16[144,960]{1,0:T(8,128)(2,1)S(1)} %collective-permute-done.refs_1_), channel_id=1, source_target_pairs={{0,4},{4,8},{8,12},{12,0},{1,5},{5,9},{9,13},{13,1},{2,6},{6,10},{... | collective-permute-start | bytes 829448 | tf_op jit(solution)/shard_map/ppermute | solution.py:186
  48.9 2.6 %collective-permute-start.3 = (bf16[144,960]{1,0:T(8,128)(2,1)S(1)}, bf16[144,960]{1,0:T(8,128)(2,1)}, u32[]{:S(2)}, u32[]{:S(2)}) collective-permute-start(bf16[144,960]{1,0:T(8,128)(2,1)S(1)} %collective-permute-done.1.refs_4_), channel_id=1, source_target_pairs={{0,12},{4,0},{8,4},{12,8},{1,13},{5,1},{9,5},{13,9},{2,14},{6,2},{... | collective-permute-start | bytes 829448 | tf_op jit(solution)/shard_map/ppermute | solution.py:186
  51.6 0.1 pad_add_fusion.place_ref
  51.7 0.8 share.1
  52.5 0.7 copy-done.5
  53.2 1.9 %collective-permute-done.4.refs_2_ = bf16[144,960]{1,0:T(8,128)(2,1)S(1)} collective-permute-done((bf16[144,960]{1,0:T(8,128)(2,1)}, bf16[144,960]{1,0:T(8,128)(2,1)S(1)}, u32[]{:S(2)}, u32[]{:S(2)}) %collective-permute-start.4) | collective-permute-done | bytes 276512 | tf_op jit(solution)/shard_map/ppermute | solution.py:186
  55.1 0.1 collective-permute-done.5.refs_3_
  55.2 0.6 copy-done.13
  55.8 0.1 copy-done.14
  55.9 5.7 %grads.2.refs_2_ = bf16[12,4,4,80,128]{4,3,2,1,0:T(8,128)(2,1)} custom-call(s32[3]{0:T(128)} %copy-done.6, bf16[288,512]{1,0:T(8,128)(2,1)} %copy-done.5, bf16[288,960]{1,0:T(8,128)(2,1)} %bitcast.46, bf16[144,960]{1,0:T(8,128)(2,1)} %copy-done.12, bf16[144,960]{1,0:T(8,128)(2,1)} %copy-done.13, bf16[144,960]{1,0:T(8,128)(2,1)} %copy-done.14, ...), custom_call_target="tpu_custom_call" | custom-call | tf_op jit(solution)/shard_map/grads/pallas_call | solution.py:262
  61.6 3.5 %grads.3 = bf16[12,4,4,80,128]{4,3,2,1,0:T(8,128)(2,1)} custom-call(s32[3]{0:T(128)} %copy-done.6, bf16[288,512]{1,0:T(8,128)(2,1)} %copy-done.5, bf16[144,960]{1,0:T(8,128)(2,1)} %collective-permute-done.2.refs_0_, bf16[144,960]{1,0:T(8,128)(2,1)} %collective-permute-done.3.refs_1_, ...), custom_call_target="tpu_custom_call", output_to_operand_aliasing={{}: (4, {})} | custom-call | tf_op jit(solution)/shard_map/grads/pallas_call | solution.py:262
  65.2 13.6 %all-gather = bf16[1152,256]{1,0:T(8,128)(2,1)S(1)} all-gather(bf16[288,256]{1,0:T(8,128)(2,1)S(1)} %get-tuple-element.22), channel_id=2, replica_groups=mesh['y'=4,'z'=12,'node'=4,'local'=4] {'node'}, dimensions={0}, use_global_device_ids=true | all-gather | bytes 737280 | tf_op jit(solution)/shard_map/all_gather | solution.py:288
  78.8 1.5 copy-done.4
  80.4 3.8 %slot_input.1 = bf16[4,72,1024]{2,1,0:T(8,128)(2,1)S(1)} custom-call(s32[3]{0:T(128)S(1)} %copy-done.7, bf16[4,288,256]{2,1,0:T(8,128)(2,1)S(1)} %bitcast.31, bf16[288,1024]{1,0:T(8,128)(2,1)S(1)} %bitcast.33, bf16[288,1024]{1,0:T(8,128)(2,1)S(1)} %bitcast.35, bf16[960,1024]{1,0:T(8,128)(2,1)S(1)} %bitcast.38, bf16[960,1024]{1,0:T(8,128)(2,1)S(1)} %bitcast.39), custom_call_target="tpu_custom_call" | custom-call | tf_op jit(solution)/shard_map/slot_input/pallas_call | solution.py:289
  84.2 1.9 %collective-permute-start.8 = (bf16[72,1024]{1,0:T(8,128)(2,1)S(1)}, bf16[72,1024]{1,0:T(8,128)(2,1)S(1)}, u32[]{:S(2)}, u32[]{:S(2)}) collective-permute-start(bf16[72,1024]{1,0:T(8,128)(2,1)S(1)} %get-tuple-element.30), channel_id=1, source_target_pairs={{0,3},{1,2},{2,1},{3,0},{4,7},{5,6},{6,5},{7,4},{8,11},{9,10},{10,... | collective-permute-start | bytes 442376 | tf_op jit(solution)/shard_map/ppermute | solution.py:307
  86.1 2.6 %collective-permute-start.7 = (bf16[72,1024]{1,0:T(8,128)(2,1)S(1)}, bf16[72,1024]{1,0:T(8,128)(2,1)S(1)}, u32[]{:S(2)}, u32[]{:S(2)}) collective-permute-start(bf16[72,1024]{1,0:T(8,128)(2,1)S(1)} %get-tuple-element.31), channel_id=1, source_target_pairs={{0,2},{1,3},{2,0},{3,1},{4,6},{5,7},{6,4},{7,5},{8,10},{9,11},{10,... | collective-permute-start | bytes 442376 | tf_op jit(solution)/shard_map/ppermute | solution.py:307
  88.7 3.1 %collective-permute-start.6 = (bf16[72,1024]{1,0:T(8,128)(2,1)S(1)}, bf16[72,1024]{1,0:T(8,128)(2,1)S(1)}, u32[]{:S(2)}, u32[]{:S(2)}) collective-permute-start(bf16[72,1024]{1,0:T(8,128)(2,1)S(1)} %get-tuple-element.32), channel_id=1, source_target_pairs={{0,1},{1,0},{2,3},{3,2},{4,5},{5,4},{6,7},{7,6},{8,9},{9,8},{10,11... | collective-permute-start | bytes 442376 | tf_op jit(solution)/shard_map/ppermute | solution.py:307
  91.8 2.8 %collective-permute-done.7.rest_2_ = bf16[72,1024]{1,0:T(8,128)(2,1)S(1)} collective-permute-done((bf16[72,1024]{1,0:T(8,128)(2,1)S(1)}, bf16[72,1024]{1,0:T(8,128)(2,1)S(1)}, u32[]{:S(2)}, u32[]{:S(2)}) %collective-permute-start.7) | collective-permute-done | bytes 147488 | tf_op jit(solution)/shard_map/ppermute | solution.py:307
  94.6 2.2 %combine.1 = (bf16[960,128]{1,0:T(8,128)(2,1)}, bf16[2,128]{1,0:T(2,128)(2,1)}) custom-call(s32[3]{0:T(128)S(1)} %copy-done.7, s32[2,128]{1,0:T(2,128)S(1)} %bitcast.42, bf16[2,128]{1,0:T(2,128)(2,1)S(1)} %bitcast.44, bf16[72,1024]{1,0:T(8,128)(2,1)S(1)} %get-tuple-element.33.rest_0_, bf16[72,1024]{1,0:T(8,128)(2,1)S(1)} %collective-permute-done.6.rest_1_, ...), custom_call_target="tpu_custom_call" | custom-call | tf_op jit(solution)/shard_map/combine/pallas_call | solution.py:310
  96.8 33.9 %reduce-scatter.2.cloned.1.call-done = bf16[1280,128]{1,0:T(8,128)(2,1)} async-done(((bf16[15360,128]{1,0:T(8,128)(2,1)}), bf16[1280,128]{1,0:T(8,128)(2,1)}) %reduce-scatter.2.cloned.1.call-update) | async-done | bytes 327696 | tf_op jit(solution)/shard_map/reduce_scatter | solution.py:283
  130.7 19.3 %all_to_all.15 = bf16[16,80,128]{2,1,0:T(8,128)(2,1)S(1)} all-to-all(bf16[16,80,128]{2,1,0:T(8,128)(2,1)} %bitcast.48), channel_id=1, replica_groups=mesh['y'=4,'z'=12,'node'=4,'local'=4] {'y','node'}, dimensions={0} | all-to-all | bytes 655360 | tf_op jit(solution)/shard_map/all_to_all | solution.py:322
  150.1 0.8 final.1
  (36 shorter events, 0.1 us)
Async XLA Ops:
  7.2 6.1 %copy-start.10 = (bf16[1,1,4,72,960]{4,3,2,1,0:T(8,128)(2,1)S(1)}, bf16[1,1,4,72,960]{4,3,2,1,0:T(8,128)(2,1)}, u32[]{:S(2)}) copy-start(bf16[1,1,4,72,960]{4,3,2,1,0:T(8,128)(2,1)} %param.12) | copy-start | bytes 1658884
  9.8 17.7 %all-to-all-start = ((bf16[4,72,960]{2,1,0:T(8,128)(2,1)}), bf16[4,72,960]{2,1,0:T(8,128)(2,1)S(1)}, u32[]{:S(2)}, u32[]{:S(2)}) async-start(bf16[4,72,960]{2,1,0:T(8,128)(2,1)} %dispatch.1), calls=%async_computation | async-start | bytes 1179648 | tf_op jit(solution)/shard_map/all_to_all | solution.py:224
  14.2 31.5 %collective-permute-start.1 = (bf16[144,960]{1,0:T(8,128)(2,1)}, bf16[144,960]{1,0:T(8,128)(2,1)S(1)}, u32[]{:S(2)}, u32[]{:S(2)}) collective-permute-start(bf16[144,960]{1,0:T(8,128)(2,1)} %get-tuple-element.34), channel_id=1, source_target_pairs={{0,12},{4,0},{8,4},{12,8},{1,13},{5,1},{9,5},{13,9},{2,14},{6,2},{... | collective-permute-start | bytes 829448 | tf_op jit(solution)/shard_map/ppermute | solution.py:186
  16.9 28.8 %collective-permute-start = (bf16[144,960]{1,0:T(8,128)(2,1)}, bf16[144,960]{1,0:T(8,128)(2,1)S(1)}, u32[]{:S(2)}, u32[]{:S(2)}) collective-permute-start(bf16[144,960]{1,0:T(8,128)(2,1)} %get-tuple-element.35), channel_id=1, source_target_pairs={{0,4},{4,8},{8,12},{12,0},{1,5},{5,9},{9,13},{13,1},{2,6},{6,10},{... | collective-permute-start | bytes 829448 | tf_op jit(solution)/shard_map/ppermute | solution.py:186
  27.5 1.5 copy-start.2
  29.1 22.6 %copy-start = (bf16[1,1,4,72,1024]{4,3,2,1,0:T(8,128)(2,1)S(1)}, bf16[1,1,4,72,1024]{4,3,2,1,0:T(8,128)(2,1)}, u32[]{:S(2)}) copy-start(bf16[1,1,4,72,1024]{4,3,2,1,0:T(8,128)(2,1)} %param.13) | copy-start | bytes 1769476
  29.1 22.6 %copy-start.1 = (bf16[1,1,4,72,1024]{4,3,2,1,0:T(8,128)(2,1)S(1)}, bf16[1,1,4,72,1024]{4,3,2,1,0:T(8,128)(2,1)}, u32[]{:S(2)}) copy-start(bf16[1,1,4,72,1024]{4,3,2,1,0:T(8,128)(2,1)} %param.14) | copy-start | bytes 1769476
  31.6 20.1 %all-to-all-start.1 = ((bf16[4,288,256]{2,1,0:T(8,128)(2,1)}), bf16[4,288,256]{2,1,0:T(8,128)(2,1)S(1)}, u32[]{:S(2)}, u32[]{:S(2)}) async-start(bf16[4,288,256]{2,1,0:T(8,128)(2,1)} %raw.1), calls=%async_computation.1 | async-start | bytes 1179648 | tf_op jit(solution)/shard_map/all_to_all | solution.py:244
  39.8 90.9 %reduce-scatter.2.cloned.1.call-start = ((), (), s32[]{:S(2)}) async-start(), calls=%async_computation.4 | async-start | bytes 4259840 | tf_op jit(solution)/shard_map/reduce_scatter | solution.py:283
  39.8 15.3 %collective-permute-start.4 = (bf16[144,960]{1,0:T(8,128)(2,1)}, bf16[144,960]{1,0:T(8,128)(2,1)S(1)}, u32[]{:S(2)}, u32[]{:S(2)}) collective-permute-start(bf16[144,960]{1,0:T(8,128)(2,1)} %get-tuple-element.34), channel_id=1, source_target_pairs={{0,4},{4,8},{8,12},{12,0},{1,5},{5,9},{9,13},{13,1},{2,6},{6,10},{... | collective-permute-start | bytes 829448 | tf_op jit(solution)/shard_map/ppermute | solution.py:186
  41.8 13.4 %collective-permute-start.5 = (bf16[144,960]{1,0:T(8,128)(2,1)}, bf16[144,960]{1,0:T(8,128)(2,1)S(1)}, u32[]{:S(2)}, u32[]{:S(2)}) collective-permute-start(bf16[144,960]{1,0:T(8,128)(2,1)} %get-tuple-element.35), channel_id=1, source_target_pairs={{0,12},{4,0},{8,4},{12,8},{1,13},{5,1},{9,5},{13,9},{2,14},{6,2},{... | collective-permute-start | bytes 829448 | tf_op jit(solution)/shard_map/ppermute | solution.py:186
  45.7 9.6 %copy-start.11 = (bf16[144,960]{1,0:T(8,128)(2,1)}, bf16[144,960]{1,0:T(8,128)(2,1)S(1)}, u32[]{:S(2)}) copy-start(bf16[144,960]{1,0:T(8,128)(2,1)S(1)} %collective-permute-done.1.refs_4_) | copy-start | bytes 829444
  45.7 9.5 %copy-start.12 = (bf16[144,960]{1,0:T(8,128)(2,1)}, bf16[144,960]{1,0:T(8,128)(2,1)S(1)}, u32[]{:S(2)}) copy-start(bf16[144,960]{1,0:T(8,128)(2,1)S(1)} %collective-permute-done.refs_1_) | copy-start | bytes 829444
  45.7 15.9 %collective-permute-start.2 = (bf16[144,960]{1,0:T(8,128)(2,1)S(1)}, bf16[144,960]{1,0:T(8,128)(2,1)}, u32[]{:S(2)}, u32[]{:S(2)}) collective-permute-start(bf16[144,960]{1,0:T(8,128)(2,1)S(1)} %collective-permute-done.refs_1_), channel_id=1, source_target_pairs={{0,4},{4,8},{8,12},{12,0},{1,5},{5,9},{9,13},{13,1},{2,6},{6,10},{... | collective-permute-start | bytes 829448 | tf_op jit(solution)/shard_map/ppermute | solution.py:186
  48.9 12.7 %collective-permute-start.3 = (bf16[144,960]{1,0:T(8,128)(2,1)S(1)}, bf16[144,960]{1,0:T(8,128)(2,1)}, u32[]{:S(2)}, u32[]{:S(2)}) collective-permute-start(bf16[144,960]{1,0:T(8,128)(2,1)S(1)} %collective-permute-done.1.refs_4_), channel_id=1, source_target_pairs={{0,12},{4,0},{8,4},{12,8},{1,13},{5,1},{9,5},{13,9},{2,14},{6,2},{... | collective-permute-start | bytes 829448 | tf_op jit(solution)/shard_map/ppermute | solution.py:186
  51.6 3.6 %copy-start.6 = (s32[3]{0:T(128)}, s32[3]{0:T(128)S(1)}, u32[]{:S(2)}) copy-start(s32[3]{0:T(128)S(1)} %pad_add_fusion.place_ref) | copy-start | bytes 40
  52.5 0.7 copy-start.5
  55.1 0.7 copy-start.13
  55.2 0.7 copy-start.14
  65.2 13.6 %copy-start.3 = (bf16[1,960,1024]{2,1,0:T(8,128)(2,1)S(1)}, bf16[1,960,1024]{2,1,0:T(8,128)(2,1)}, u32[]{:S(2)}) copy-start(bf16[1,960,1024]{2,1,0:T(8,128)(2,1)} %param.15) | copy-start | bytes 5898244
  65.2 13.6 %copy-start.7 = (s32[3]{0:T(128)S(1)}, s32[3]{0:T(128)}, u32[]{:S(2)}) copy-start(s32[3]{0:T(128)} %copy-done.6) | copy-start | bytes 40
  78.8 1.5 copy-start.4
  80.3 14.3 %copy-start.8 = (s32[128,2]{0,1:T(2,128)S(1)}, s32[128,2]{0,1:T(2,128)}, u32[]{:S(2)}) copy-start(s32[128,2]{0,1:T(2,128)} %param.10) | copy-start | bytes 3076
  80.3 14.3 %copy-start.9 = (bf16[128,2]{0,1:T(2,128)(2,1)S(1)}, bf16[128,2]{0,1:T(2,128)(2,1)}, u32[]{:S(2)}) copy-start(bf16[128,2]{0,1:T(2,128)(2,1)} %param.11) | copy-start | bytes 1540
  84.2 7.6 %collective-permute-start.8 = (bf16[72,1024]{1,0:T(8,128)(2,1)S(1)}, bf16[72,1024]{1,0:T(8,128)(2,1)S(1)}, u32[]{:S(2)}, u32[]{:S(2)}) collective-permute-start(bf16[72,1024]{1,0:T(8,128)(2,1)S(1)} %get-tuple-element.30), channel_id=1, source_target_pairs={{0,3},{1,2},{2,1},{3,0},{4,7},{5,6},{6,5},{7,4},{8,11},{9,10},{10,... | collective-permute-start | bytes 442376 | tf_op jit(solution)/shard_map/ppermute | solution.py:307
  86.1 8.5 %collective-permute-start.7 = (bf16[72,1024]{1,0:T(8,128)(2,1)S(1)}, bf16[72,1024]{1,0:T(8,128)(2,1)S(1)}, u32[]{:S(2)}, u32[]{:S(2)}) collective-permute-start(bf16[72,1024]{1,0:T(8,128)(2,1)S(1)} %get-tuple-element.31), channel_id=1, source_target_pairs={{0,2},{1,3},{2,0},{3,1},{4,6},{5,7},{6,4},{7,5},{8,10},{9,11},{10,... | collective-permute-start | bytes 442376 | tf_op jit(solution)/shard_map/ppermute | solution.py:307
  88.7 5.9 %collective-permute-start.6 = (bf16[72,1024]{1,0:T(8,128)(2,1)S(1)}, bf16[72,1024]{1,0:T(8,128)(2,1)S(1)}, u32[]{:S(2)}, u32[]{:S(2)}) collective-permute-start(bf16[72,1024]{1,0:T(8,128)(2,1)S(1)} %get-tuple-element.32), channel_id=1, source_target_pairs={{0,1},{1,0},{2,3},{3,2},{4,5},{5,4},{6,7},{7,6},{8,9},{9,8},{10,11... | collective-permute-start | bytes 442376 | tf_op jit(solution)/shard_map/ppermute | solution.py:307
Sparse Core Ops, SparseCore 0:
  65.3 65.3 reduce-scatter.1

commit v8 on v7

--- a/solution.py
+++ b/solution.py
@@ -80,11 +80,15 @@
     delta_ref[:, quarter:] = up_delta
 
 
-def grads_kernel(own, place_ref, delta_ref, *refs):
-    out_ref = refs[-1]
-    n_z, n_y = out_ref.shape[:2]
-
-    def block(x):
+def grads_kernel(own, groups, turns, place_ref, delta_ref, *refs):
+    out_ref, held, sems = refs[-3:]
+    n_z, n_y, n_node = out_ref.shape[:3]
+    copies = []
+    for k, (group, turn) in enumerate(zip(groups, turns)):
+        slot = k % held.shape[0]
+        if k >= held.shape[0]:
+            copies[k - held.shape[0]].wait()
+        x = jnp.concatenate([refs[i][...] for i in group], axis=0)
         res = lax.dot_general(
             x, delta_ref[...], (((0,), (0,)), ((), ())), preferred_element_type=F32
         )
@@ -93,22 +97,14 @@
             tall = jnp.concatenate(
                 [piece[:, c * 128 : (c + 1) * 128] for c in range(piece.shape[1] // 128)], axis=0
             )
-            out_ref[i % n_z, i // n_z, 0] = tall.astype(BF)
-
-    if len(refs) == 4:
-        block(jnp.concatenate([refs[0][...], refs[1][...]], axis=0))
-        return
-    step = pl.program_id(0)
-
-    @pl.when(step == 0)
-    def _():
-        block(refs[0][...])
-
-    for k in (1, 2):
-
-        @pl.when(step == k)
-        def _(k=k):
-            block(jnp.concatenate([refs[2 * k - 1][...], refs[2 * k][...]], axis=0))
+            held[slot, i % n_z, i // n_z] = tall.astype(BF)
+        to = lax.rem(place_ref[1] + turn, n_node)
+        copies.append(
+            pltpu.make_async_copy(held.at[slot], out_ref.at[:, :, to], sems.at[slot])
+        )
+        copies[k].start()
+    for copy in copies[-held.shape[0] :]:
+        copy.wait()
 
 
 def input_kernel(capacity, place_ref, raw_ref, gate_ref, up_ref, wg_ref, wu_ref, out_ref, total, side):
@@ -181,6 +177,10 @@
     return pltpu.CompilerParams(vmem_limit_bytes=mib * MIB, **more)
 
 
+def in_hbm(x):
+    return pltpu.with_memory_space_constraint(x, pltpu.HBM)
+
+
 def ring(x, axis, step):
     n = lax.axis_size(axis)
     return lax.ppermute(x, axis, [(i, (i + step) % n) for i in range(n)])
@@ -188,6 +188,7 @@
 
 SMEM = pl.BlockSpec(memory_space=pltpu.SMEM)
 VMEM = pl.BlockSpec(memory_space=pltpu.VMEM)
+HBM = pl.BlockSpec(memory_space=pltpu.HBM)
 
 
 def local(token_grads, routes, gates, expert_inputs, gate_pre, up_pre, w_gate, w_up, w_down):
@@ -210,7 +211,7 @@
 
     outgoing = pl.pallas_call(
         functools.partial(dispatch_kernel, n_local, capacity),
-        in_specs=[pl.BlockSpec(memory_space=pl.ANY)] * 3,
+        in_specs=[HBM] * 3,
         scratch_shapes=[
             pltpu.VMEM((top, tokens), jnp.int32),
             pltpu.VMEM((top, tokens), BF),
@@ -218,9 +219,9 @@
             pltpu.SemaphoreType.DMA((3,)),
         ],
         out_shape=jax.ShapeDtypeStruct((n_local, capacity, feat), BF),
-        compiler_params=params(56),
+        compiler_params=params(),
         name="dispatch",
-    )(routes.T, gates.T, token_grads.T)
+    )(*(in_hbm(a.T) for a in (routes, gates, token_grads)))
     arrived = lax.all_to_all(outgoing, "local", split_axis=0, concat_axis=0, tiled=True)
 
     half = slots // 2
@@ -240,7 +241,7 @@
         out_shape=jax.ShapeDtypeStruct((n_node, slots, quarter), BF),
         compiler_params=params(),
         name="raw",
-    )(arrived.reshape(slots, feat), w_down[0].T)
+    )(arrived.reshape(slots, feat), in_hbm(w_down[0].T))
     raw_shares = lax.all_to_all(raw_parts, "node", split_axis=0, concat_axis=0, tiled=True)
 
     x_prev[0], x_next[1], _ = lax.optimization_barrier((x_prev[0], x_next[1], raw_parts))
@@ -258,28 +259,26 @@
     )(place, raw_shares, gate_rows, up_rows)
 
     tall = own * 2 * quarter // 128
-    def products(count, pieces, turn, before):
+    def products(groups, turns, before):
+        pieces = [x for group in groups for x in group]
+        at = iter(range(len(pieces)))
+        count = min(2, len(groups))
         return pl.pallas_call(
-            functools.partial(grads_kernel, own),
-            grid_spec=pltpu.PrefetchScalarGridSpec(
-                num_scalar_prefetch=1,
-                grid=(count,),
-                in_specs=[pl.BlockSpec((slots, 2 * quarter), lambda i, p: (0, 0))]
-                + [pl.BlockSpec(x.shape, lambda i, p: (0, 0)) for x in pieces]
-                + [pl.BlockSpec(memory_space=pl.ANY)] * len(before),
-                out_specs=pl.BlockSpec(
-                    (n_z, n_y, 1, tall, 128),
-                    lambda i, p: (0, 0, (p[1] + turn(i)) % n_node, 0, 0),
-                ),
-            ),
-            out_shape=jax.ShapeDtypeStruct((n_z, n_y, n_node, tall, 128), BF),
+            functools.partial(grads_kernel, own, [[next(at) for _ in g] for g in groups], turns),
+            in_specs=[SMEM] + [VMEM] * (1 + len(pieces)) + [HBM] * len(before),
+            out_specs=HBM,
+            out_shape=pltpu.HBM((n_z, n_y, n_node, tall, 128), BF),
+            scratch_shapes=[
+                pltpu.VMEM((count, n_z, n_y, tall, 128), BF),
+                pltpu.SemaphoreType.DMA((count,)),
+            ],
             input_output_aliases={2 + len(pieces): 0} if before else {},
-            compiler_params=params(56),
+            compiler_params=params(24),
             name="grads",
         )(place, deltas, *pieces, *before)
 
-    grads = products(3, (x_rows, *x_prev, *x_next), lambda i: jnp.where(i < 2, 3 * i, 1), ())
-    grads = products(1, x_across, lambda i: 2 + i, (grads,))
+    grads = products(((x_rows,), x_prev, x_next), (0, n_node - 1, 1), ())
+    grads = products((x_across,), (2,), (grads,))
     z_sum = lax.psum_scatter(
         grads.reshape(n_z * n_y * n_node * tall, 128), "z", scatter_dimension=0, tiled=True
     )

time: 159 us -> 157 us (0.987)
    reduce_scatter x1, waiting for transfers between devices: 33.9 us -> 31.1 us  [local(): lax.psum_scatter(grads.reshape(n_z * n_y * n_node * tall, 128), 'z', scat...]
    pallas_call x2, Pallas kernels: 9.24 us -> 6.82 us  [products(): pl.pallas_call(functools.partial(grads_kernel, own, [[next(at) for _ in g...]
    ppermute x6, waiting for transfers between devices: 2.07 us -> 4.31 us  [ring(): return lax.ppermute(x, axis, [(i, (i + step) % n) for i in range(n)])]
    pallas_call x1, Pallas kernels: 2.5 us -> 4.17 us  [local(): pl.pallas_call(raw_kernel, grid=(n_node,), in_specs=[pl.BlockSpec((slots,...]
    unnamed x30 -> x18, local copies, waits for them, and re-layouts: 4.54 us -> 4.1 us
  transfers between devices with their start and end apart: 12 -> 12, of which waited for: 4 -> 6; matrix products, arithmetic and copies ran while one was open for 1% -> 1% of each run, Pallas kernels for 9% -> 10%
where the time goes in v8:
time: 157 us; the launch traced here: 156 us
  starting transfers between devices  44.3 us (28%)
  waiting for transfers between devices  38.1 us (24%)
  blocking collectives  33.1 us (21%)
  Pallas kernels  21.1 us (13%)
  between operations  14.3 us (9%)
  local copies, waits for them, and re-layouts  5.01 us (3%)
    reduce_scatter x1, waiting for transfers between devices, local(): lax.psum_scatter(grads.reshape(n_z * n_y * n_node * tall, 128), 'z', scat...  31.1 us
    ppermute x6, starting transfers between devices, ring(): return lax.ppermute(x, axis, [(i, (i + step) % n) for i in range(n)])  25 us
    all_to_all x1, blocking collectives, local(): lax.all_to_all(z_sum.reshape(n_y * n_node, tall, 128), ('y', 'node'), spl...  19.5 us
    all_gather x1, blocking collectives, local(): raw = lax.all_gather(raw_share, 'node', axis=0, tiled=False)  13.6 us
    all_to_all x1, starting transfers between devices, local(): lax.all_to_all(raw_parts, 'node', split_axis=0, concat_axis=0, tiled=True)  8.22 us
    ppermute x3, starting transfers between devices, local(): lax.ppermute(slot_input[k], 'local', [(i, i ^ k) for i in range(n_local)])  7.59 us
    pallas_call x2, Pallas kernels, products(): pl.pallas_call(functools.partial(grads_kernel, own, [[next(at) for _ in g...  6.82 us
    ppermute x6, waiting for transfers between devices, ring(): return lax.ppermute(x, axis, [(i, (i + step) % n) for i in range(n)])  4.31 us
  transfers between devices with their start and end apart: 12, of which 6 were waited for; matrix products, arithmetic and copies ran while one was open for 1% of the time, Pallas kernels for 10%

profile of v8, /device:TPU:6, one launch (start us, length us, event | category | flops | bytes accessed | tf_op | source)
XLA Modules:
  0.0 155.9 jit_solution(3611917872658730906)
XLA Ops:
  7.2 2.7 %dispatch.1 = bf16[4,72,960]{2,1,0:T(8,128)(2,1)} custom-call(s32[2,128]{1,0:T(2,128)} %bitcast.42, bf16[2,128]{1,0:T(2,128)(2,1)} %bitcast.44, bf16[960,128]{1,0:T(8,128)(2,1)} %bitcast.49), custom_call_target="tpu_custom_call" | custom-call | tf_op jit(solution)/shard_map/dispatch/pallas_call | solution.py:212
  9.8 3.5 %all-to-all-start = ((bf16[4,72,960]{2,1,0:T(8,128)(2,1)}), bf16[4,72,960]{2,1,0:T(8,128)(2,1)S(1)}, u32[]{:S(2)}, u32[]{:S(2)}) async-start(bf16[4,72,960]{2,1,0:T(8,128)(2,1)} %dispatch.1), calls=%async_computation | async-start | bytes 1179648 | tf_op jit(solution)/shard_map/all_to_all | solution.py:225
  13.4 0.9 fusion
  14.2 2.7 %collective-permute-start.1 = (bf16[144,960]{1,0:T(8,128)(2,1)}, bf16[144,960]{1,0:T(8,128)(2,1)S(1)}, u32[]{:S(2)}, u32[]{:S(2)}) collective-permute-start(bf16[144,960]{1,0:T(8,128)(2,1)} %get-tuple-element.34), channel_id=1, source_target_pairs={{0,12},{4,0},{8,4},{12,8},{1,13},{5,1},{9,5},{13,9},{2,14},{6,2},{... | collective-permute-start | bytes 829448 | tf_op jit(solution)/shard_map/ppermute | solution.py:186
  17.0 10.6 %collective-permute-start = (bf16[144,960]{1,0:T(8,128)(2,1)}, bf16[144,960]{1,0:T(8,128)(2,1)S(1)}, u32[]{:S(2)}, u32[]{:S(2)}) collective-permute-start(bf16[144,960]{1,0:T(8,128)(2,1)} %get-tuple-element.35), channel_id=1, source_target_pairs={{0,4},{4,8},{8,12},{12,0},{1,5},{5,9},{9,13},{13,1},{2,6},{6,10},{... | collective-permute-start | bytes 829448 | tf_op jit(solution)/shard_map/ppermute | solution.py:186
  27.6 4.2 %raw.1 = bf16[4,288,256]{2,1,0:T(8,128)(2,1)} custom-call(bf16[288,960]{1,0:T(8,128)(2,1)S(1)} %bitcast.38, bf16[960,1024]{1,0:T(8,128)(2,1)} %bitcast.47), custom_call_target="tpu_custom_call" | custom-call | tf_op jit(solution)/shard_map/raw/pallas_call | solution.py:233
  31.7 8.2 %all-to-all-start.1 = ((bf16[4,288,256]{2,1,0:T(8,128)(2,1)}), bf16[4,288,256]{2,1,0:T(8,128)(2,1)S(1)}, u32[]{:S(2)}, u32[]{:S(2)}) async-start(bf16[4,288,256]{2,1,0:T(8,128)(2,1)} %raw.1), calls=%async_computation.1 | async-start | bytes 1179648 | tf_op jit(solution)/shard_map/all_to_all | solution.py:245
  40.0 2.0 %collective-permute-start.4 = (bf16[144,960]{1,0:T(8,128)(2,1)}, bf16[144,960]{1,0:T(8,128)(2,1)S(1)}, u32[]{:S(2)}, u32[]{:S(2)}) collective-permute-start(bf16[144,960]{1,0:T(8,128)(2,1)} %get-tuple-element.34), channel_id=1, source_target_pairs={{0,4},{4,8},{8,12},{12,0},{1,5},{5,9},{9,13},{13,1},{2,6},{6,10},{... | collective-permute-start | bytes 829448 | tf_op jit(solution)/shard_map/ppermute | solution.py:186
  42.0 3.8 %collective-permute-start.5 = (bf16[144,960]{1,0:T(8,128)(2,1)}, bf16[144,960]{1,0:T(8,128)(2,1)S(1)}, u32[]{:S(2)}, u32[]{:S(2)}) collective-permute-start(bf16[144,960]{1,0:T(8,128)(2,1)} %get-tuple-element.35), channel_id=1, source_target_pairs={{0,12},{4,0},{8,4},{12,8},{1,13},{5,1},{9,5},{13,9},{2,14},{6,2},{... | collective-permute-start | bytes 829448 | tf_op jit(solution)/shard_map/ppermute | solution.py:186
  45.8 3.2 %collective-permute-start.2 = (bf16[144,960]{1,0:T(8,128)(2,1)S(1)}, bf16[144,960]{1,0:T(8,128)(2,1)}, u32[]{:S(2)}, u32[]{:S(2)}) collective-permute-start(bf16[144,960]{1,0:T(8,128)(2,1)S(1)} %collective-permute-done.refs_1_), channel_id=1, source_target_pairs={{0,4},{4,8},{8,12},{12,0},{1,5},{5,9},{9,13},{13,1},{2,6},{6,10},{... | collective-permute-start | bytes 829448 | tf_op jit(solution)/shard_map/ppermute | solution.py:186
  49.1 2.6 %collective-permute-start.3 = (bf16[144,960]{1,0:T(8,128)(2,1)S(1)}, bf16[144,960]{1,0:T(8,128)(2,1)}, u32[]{:S(2)}, u32[]{:S(2)}) collective-permute-start(bf16[144,960]{1,0:T(8,128)(2,1)S(1)} %collective-permute-done.1.refs_4_), channel_id=1, source_target_pairs={{0,12},{4,0},{8,4},{12,8},{1,13},{5,1},{9,5},{13,9},{2,14},{6,2},{... | collective-permute-start | bytes 829448 | tf_op jit(solution)/shard_map/ppermute | solution.py:186
  51.7 0.1 pad_add_fusion.place_ref
  51.8 0.8 share.1
  52.6 2.7 %collective-permute-done.4.refs_2_ = bf16[144,960]{1,0:T(8,128)(2,1)S(1)} collective-permute-done((bf16[144,960]{1,0:T(8,128)(2,1)}, bf16[144,960]{1,0:T(8,128)(2,1)S(1)}, u32[]{:S(2)}, u32[]{:S(2)}) %collective-permute-start.4) | collective-permute-done | bytes 276512 | tf_op jit(solution)/shard_map/ppermute | solution.py:186
  55.2 0.1 collective-permute-done.5.refs_3_
  55.4 4.0 %grads.2.refs_2_ = bf16[12,4,4,80,128]{4,3,2,1,0:T(8,128)(2,1)} custom-call(s32[3]{0:T(128)S(1)} %pad_add_fusion.place_ref, bf16[288,512]{1,0:T(8,128)(2,1)S(1)} %get-tuple-element.17.delta_ref, bf16[288,960]{1,0:T(8,128)(2,1)S(1)} %bitcast.32, bf16[144,960]{1,0:T(8,128)(2,1)S(1)} %collective-permute-done.refs_1_, ...), custom_call_target="tpu_custom_call" | custom-call | tf_op jit(solution)/shard_map/grads/pallas_call | solution.py:266
  59.4 0.9 collective-permute-done.2.refs_0_
  60.3 0.6 collective-permute-done.3.refs_1_
  60.9 2.8 %grads.3 = bf16[12,4,4,80,128]{4,3,2,1,0:T(8,128)(2,1)} custom-call(s32[3]{0:T(128)S(1)} %pad_add_fusion.place_ref, bf16[288,512]{1,0:T(8,128)(2,1)S(1)} %get-tuple-element.17.delta_ref, bf16[144,960]{1,0:T(8,128)(2,1)} %collective-permute-done.2.refs_0_, bf16[144,960]{1,0:T(8,128)(2,1)} %collective-permute-done.3.refs_1_, ...), custom_call_target="tpu_custom_call", output_to_operand_aliasing={{}: (4, {})} | custom-call | tf_op jit(solution)/shard_map/grads/pallas_call | solution.py:266
  63.8 0.9 copy-done.6
  64.6 13.6 %all-gather = bf16[1152,256]{1,0:T(8,128)(2,1)S(1)} all-gather(bf16[288,256]{1,0:T(8,128)(2,1)S(1)} %copy-done.6), channel_id=2, replica_groups=mesh['y'=4,'z'=12,'node'=4,'local'=4] {'node'}, dimensions={0}, use_global_device_ids=true | all-gather | bytes 737280 | tf_op jit(solution)/shard_map/all_gather | solution.py:287
  78.3 1.6 %copy-done.3 = bf16[1,960,1024]{2,1,0:T(8,128)(2,1)S(1)} copy-done((bf16[1,960,1024]{2,1,0:T(8,128)(2,1)S(1)}, bf16[1,960,1024]{2,1,0:T(8,128)(2,1)}, u32[]{:S(2)}) %copy-start.3) | copy-done | bytes 1966104
  79.9 1.5 copy-done.4
  81.4 3.8 %slot_input.1 = bf16[4,72,1024]{2,1,0:T(8,128)(2,1)S(1)} custom-call(s32[3]{0:T(128)S(1)} %pad_add_fusion.place_ref, bf16[4,288,256]{2,1,0:T(8,128)(2,1)S(1)} %bitcast.33, bf16[288,1024]{1,0:T(8,128)(2,1)S(1)} %bitcast.35, bf16[288,1024]{1,0:T(8,128)(2,1)S(1)} %bitcast.37, bf16[960,1024]{1,0:T(8,128)(2,1)S(1)} %bitcast.39, bf16[960,1024]{1,0:T(8,128)(2,1)S(1)} %bitcast.40), custom_call_target="tpu_custom_call" | custom-call | tf_op jit(solution)/shard_map/slot_input/pallas_call | solution.py:288
  85.3 1.9 %collective-permute-start.8 = (bf16[72,1024]{1,0:T(8,128)(2,1)S(1)}, bf16[72,1024]{1,0:T(8,128)(2,1)S(1)}, u32[]{:S(2)}, u32[]{:S(2)}) collective-permute-start(bf16[72,1024]{1,0:T(8,128)(2,1)S(1)} %get-tuple-element.30), channel_id=1, source_target_pairs={{0,3},{1,2},{2,1},{3,0},{4,7},{5,6},{6,5},{7,4},{8,11},{9,10},{10,... | collective-permute-start | bytes 442376 | tf_op jit(solution)/shard_map/ppermute | solution.py:306
  87.2 2.4 %collective-permute-start.7 = (bf16[72,1024]{1,0:T(8,128)(2,1)S(1)}, bf16[72,1024]{1,0:T(8,128)(2,1)S(1)}, u32[]{:S(2)}, u32[]{:S(2)}) collective-permute-start(bf16[72,1024]{1,0:T(8,128)(2,1)S(1)} %get-tuple-element.31), channel_id=1, source_target_pairs={{0,2},{1,3},{2,0},{3,1},{4,6},{5,7},{6,4},{7,5},{8,10},{9,11},{10,... | collective-permute-start | bytes 442376 | tf_op jit(solution)/shard_map/ppermute | solution.py:306
  89.6 3.3 %collective-permute-start.6 = (bf16[72,1024]{1,0:T(8,128)(2,1)S(1)}, bf16[72,1024]{1,0:T(8,128)(2,1)S(1)}, u32[]{:S(2)}, u32[]{:S(2)}) collective-permute-start(bf16[72,1024]{1,0:T(8,128)(2,1)S(1)} %get-tuple-element.32), channel_id=1, source_target_pairs={{0,1},{1,0},{2,3},{3,2},{4,5},{5,4},{6,7},{7,6},{8,9},{9,8},{10,11... | collective-permute-start | bytes 442376 | tf_op jit(solution)/shard_map/ppermute | solution.py:306
  92.9 2.6 %collective-permute-done.7.rest_2_ = bf16[72,1024]{1,0:T(8,128)(2,1)S(1)} collective-permute-done((bf16[72,1024]{1,0:T(8,128)(2,1)S(1)}, bf16[72,1024]{1,0:T(8,128)(2,1)S(1)}, u32[]{:S(2)}, u32[]{:S(2)}) %collective-permute-start.7) | collective-permute-done | bytes 147488 | tf_op jit(solution)/shard_map/ppermute | solution.py:306
  95.5 2.2 %combine.1 = (bf16[960,128]{1,0:T(8,128)(2,1)}, bf16[2,128]{1,0:T(2,128)(2,1)}) custom-call(s32[3]{0:T(128)S(1)} %pad_add_fusion.place_ref, s32[2,128]{1,0:T(2,128)S(1)} %bitcast.43, bf16[2,128]{1,0:T(2,128)(2,1)S(1)} %bitcast.45, bf16[72,1024]{1,0:T(8,128)(2,1)S(1)} %get-tuple-element.33.rest_0_, bf16[72,1024]{1,0:T(8,128)(2,1)S(1)} %collective-permute-done.6.rest_1_, ...), custom_call_target="tpu_custom_call" | custom-call | tf_op jit(solution)/shard_map/combine/pallas_call | solution.py:309
  97.7 31.1 %reduce-scatter.2.cloned.1.call-done = bf16[1280,128]{1,0:T(8,128)(2,1)} async-done(((bf16[15360,128]{1,0:T(8,128)(2,1)}), bf16[1280,128]{1,0:T(8,128)(2,1)}) %reduce-scatter.2.cloned.1.call-update) | async-done | bytes 327696 | tf_op jit(solution)/shard_map/reduce_scatter | solution.py:282
  128.8 19.5 %all_to_all.15 = bf16[16,80,128]{2,1,0:T(8,128)(2,1)S(1)} all-to-all(bf16[16,80,128]{2,1,0:T(8,128)(2,1)} %bitcast.48), channel_id=1, replica_groups=mesh['y'=4,'z'=12,'node'=4,'local'=4] {'y','node'}, dimensions={0} | all-to-all | bytes 655360 | tf_op jit(solution)/shard_map/all_to_all | solution.py:321
  148.3 0.8 final.1
  (24 shorter events, 0.1 us)
Async XLA Ops:
  7.2 6.2 %copy-start = (bf16[1,1,4,72,960]{4,3,2,1,0:T(8,128)(2,1)S(1)}, bf16[1,1,4,72,960]{4,3,2,1,0:T(8,128)(2,1)}, u32[]{:S(2)}) copy-start(bf16[1,1,4,72,960]{4,3,2,1,0:T(8,128)(2,1)} %param.12) | copy-start | bytes 1658884
  9.8 17.7 %all-to-all-start = ((bf16[4,72,960]{2,1,0:T(8,128)(2,1)}), bf16[4,72,960]{2,1,0:T(8,128)(2,1)S(1)}, u32[]{:S(2)}, u32[]{:S(2)}) async-start(bf16[4,72,960]{2,1,0:T(8,128)(2,1)} %dispatch.1), calls=%async_computation | async-start | bytes 1179648 | tf_op jit(solution)/shard_map/all_to_all | solution.py:225
  14.2 31.6 %collective-permute-start.1 = (bf16[144,960]{1,0:T(8,128)(2,1)}, bf16[144,960]{1,0:T(8,128)(2,1)S(1)}, u32[]{:S(2)}, u32[]{:S(2)}) collective-permute-start(bf16[144,960]{1,0:T(8,128)(2,1)} %get-tuple-element.34), channel_id=1, source_target_pairs={{0,12},{4,0},{8,4},{12,8},{1,13},{5,1},{9,5},{13,9},{2,14},{6,2},{... | collective-permute-start | bytes 829448 | tf_op jit(solution)/shard_map/ppermute | solution.py:186
  17.0 28.9 %collective-permute-start = (bf16[144,960]{1,0:T(8,128)(2,1)}, bf16[144,960]{1,0:T(8,128)(2,1)S(1)}, u32[]{:S(2)}, u32[]{:S(2)}) collective-permute-start(bf16[144,960]{1,0:T(8,128)(2,1)} %get-tuple-element.35), channel_id=1, source_target_pairs={{0,4},{4,8},{8,12},{12,0},{1,5},{5,9},{9,13},{13,1},{2,6},{6,10},{... | collective-permute-start | bytes 829448 | tf_op jit(solution)/shard_map/ppermute | solution.py:186
  27.6 24.2 %copy-start.1 = (bf16[1,1,4,72,1024]{4,3,2,1,0:T(8,128)(2,1)S(1)}, bf16[1,1,4,72,1024]{4,3,2,1,0:T(8,128)(2,1)}, u32[]{:S(2)}) copy-start(bf16[1,1,4,72,1024]{4,3,2,1,0:T(8,128)(2,1)} %param.13) | copy-start | bytes 1769476
  27.6 24.2 %copy-start.2 = (bf16[1,1,4,72,1024]{4,3,2,1,0:T(8,128)(2,1)S(1)}, bf16[1,1,4,72,1024]{4,3,2,1,0:T(8,128)(2,1)}, u32[]{:S(2)}) copy-start(bf16[1,1,4,72,1024]{4,3,2,1,0:T(8,128)(2,1)} %param.14) | copy-start | bytes 1769476
  31.7 20.0 %all-to-all-start.1 = ((bf16[4,288,256]{2,1,0:T(8,128)(2,1)}), bf16[4,288,256]{2,1,0:T(8,128)(2,1)S(1)}, u32[]{:S(2)}, u32[]{:S(2)}) async-start(bf16[4,288,256]{2,1,0:T(8,128)(2,1)} %raw.1), calls=%async_computation.1 | async-start | bytes 1179648 | tf_op jit(solution)/shard_map/all_to_all | solution.py:245
  40.0 88.9 %reduce-scatter.2.cloned.1.call-start = ((), (), s32[]{:S(2)}) async-start(), calls=%async_computation.4 | async-start | bytes 4259840 | tf_op jit(solution)/shard_map/reduce_scatter | solution.py:282
  40.0 15.3 %collective-permute-start.4 = (bf16[144,960]{1,0:T(8,128)(2,1)}, bf16[144,960]{1,0:T(8,128)(2,1)S(1)}, u32[]{:S(2)}, u32[]{:S(2)}) collective-permute-start(bf16[144,960]{1,0:T(8,128)(2,1)} %get-tuple-element.34), channel_id=1, source_target_pairs={{0,4},{4,8},{8,12},{12,0},{1,5},{5,9},{9,13},{13,1},{2,6},{6,10},{... | collective-permute-start | bytes 829448 | tf_op jit(solution)/shard_map/ppermute | solution.py:186
  42.0 13.4 %collective-permute-start.5 = (bf16[144,960]{1,0:T(8,128)(2,1)}, bf16[144,960]{1,0:T(8,128)(2,1)S(1)}, u32[]{:S(2)}, u32[]{:S(2)}) collective-permute-start(bf16[144,960]{1,0:T(8,128)(2,1)} %get-tuple-element.35), channel_id=1, source_target_pairs={{0,12},{4,0},{8,4},{12,8},{1,13},{5,1},{9,5},{13,9},{2,14},{6,2},{... | collective-permute-start | bytes 829448 | tf_op jit(solution)/shard_map/ppermute | solution.py:186
  45.8 14.5 %collective-permute-start.2 = (bf16[144,960]{1,0:T(8,128)(2,1)S(1)}, bf16[144,960]{1,0:T(8,128)(2,1)}, u32[]{:S(2)}, u32[]{:S(2)}) collective-permute-start(bf16[144,960]{1,0:T(8,128)(2,1)S(1)} %collective-permute-done.refs_1_), channel_id=1, source_target_pairs={{0,4},{4,8},{8,12},{12,0},{1,5},{5,9},{9,13},{13,1},{2,6},{6,10},{... | collective-permute-start | bytes 829448 | tf_op jit(solution)/shard_map/ppermute | solution.py:186
  49.1 11.9 %collective-permute-start.3 = (bf16[144,960]{1,0:T(8,128)(2,1)S(1)}, bf16[144,960]{1,0:T(8,128)(2,1)}, u32[]{:S(2)}, u32[]{:S(2)}) collective-permute-start(bf16[144,960]{1,0:T(8,128)(2,1)S(1)} %collective-permute-done.1.refs_4_), channel_id=1, source_target_pairs={{0,12},{4,0},{8,4},{12,8},{1,13},{5,1},{9,5},{13,9},{2,14},{6,2},{... | collective-permute-start | bytes 829448 | tf_op jit(solution)/shard_map/ppermute | solution.py:186
  52.6 6.8 %copy-start.5 = (bf16[288,256]{1,0:T(8,128)(2,1)}, bf16[288,256]{1,0:T(8,128)(2,1)S(1)}, u32[]{:S(2)}) copy-start(bf16[288,256]{1,0:T(8,128)(2,1)S(1)} %get-tuple-element.22) | copy-start | bytes 442372
  63.7 0.9 copy-start.6
  78.3 1.6 %copy-start.3 = (bf16[1,960,1024]{2,1,0:T(8,128)(2,1)S(1)}, bf16[1,960,1024]{2,1,0:T(8,128)(2,1)}, u32[]{:S(2)}) copy-start(bf16[1,960,1024]{2,1,0:T(8,128)(2,1)} %param.15) | copy-start | bytes 5898244
  79.9 1.5 copy-start.4
  81.4 14.1 %copy-start.7 = (s32[128,2]{0,1:T(2,128)S(1)}, s32[128,2]{0,1:T(2,128)}, u32[]{:S(2)}) copy-start(s32[128,2]{0,1:T(2,128)} %param.10) | copy-start | bytes 3076
  81.4 14.1 %copy-start.8 = (bf16[128,2]{0,1:T(2,128)(2,1)S(1)}, bf16[128,2]{0,1:T(2,128)(2,1)}, u32[]{:S(2)}) copy-start(bf16[128,2]{0,1:T(2,128)(2,1)} %param.11) | copy-start | bytes 1540
  85.3 7.6 %collective-permute-start.8 = (bf16[72,1024]{1,0:T(8,128)(2,1)S(1)}, bf16[72,1024]{1,0:T(8,128)(2,1)S(1)}, u32[]{:S(2)}, u32[]{:S(2)}) collective-permute-start(bf16[72,1024]{1,0:T(8,128)(2,1)S(1)} %get-tuple-element.30), channel_id=1, source_target_pairs={{0,3},{1,2},{2,1},{3,0},{4,7},{5,6},{6,5},{7,4},{8,11},{9,10},{10,... | collective-permute-start | bytes 442376 | tf_op jit(solution)/shard_map/ppermute | solution.py:306
  87.2 8.3 %collective-permute-start.7 = (bf16[72,1024]{1,0:T(8,128)(2,1)S(1)}, bf16[72,1024]{1,0:T(8,128)(2,1)S(1)}, u32[]{:S(2)}, u32[]{:S(2)}) collective-permute-start(bf16[72,1024]{1,0:T(8,128)(2,1)S(1)} %get-tuple-element.31), channel_id=1, source_target_pairs={{0,2},{1,3},{2,0},{3,1},{4,6},{5,7},{6,4},{7,5},{8,10},{9,11},{10,... | collective-permute-start | bytes 442376 | tf_op jit(solution)/shard_map/ppermute | solution.py:306
  89.6 5.9 %collective-permute-start.6 = (bf16[72,1024]{1,0:T(8,128)(2,1)S(1)}, bf16[72,1024]{1,0:T(8,128)(2,1)S(1)}, u32[]{:S(2)}, u32[]{:S(2)}) collective-permute-start(bf16[72,1024]{1,0:T(8,128)(2,1)S(1)} %get-tuple-element.32), channel_id=1, source_target_pairs={{0,1},{1,0},{2,3},{3,2},{4,5},{5,4},{6,7},{7,6},{8,9},{9,8},{10,11... | collective-permute-start | bytes 442376 | tf_op jit(solution)/shard_map/ppermute | solution.py:306
Sparse Core Ops, SparseCore 0:
  63.9 64.9 reduce-scatter.1

commit v9 on v8

--- a/solution.py
+++ b/solution.py
@@ -57,8 +57,20 @@
         out_ref[e] = out[e * capacity : (e + 1) * capacity]
 
 
-def raw_kernel(rows_ref, down_ref, out_ref):
-    out_ref[0] = jnp.dot(rows_ref[...], down_ref[...], preferred_element_type=F32).astype(BF)
+def raw_kernel(rows_ref, down_in, out_ref, down_ref, sems):
+    count, _, quarter = down_ref.shape
+    copies = [
+        pltpu.make_async_copy(
+            down_in.at[:, i * quarter : (i + 1) * quarter], down_ref.at[i], sems.at[i]
+        )
+        for i in range(count)
+    ]
+    for copy in copies:
+        copy.start()
+    rows = rows_ref[...]
+    for i, copy in enumerate(copies):
+        copy.wait()
+        out_ref[i] = jnp.dot(rows, down_ref[i], preferred_element_type=F32).astype(BF)
 
 
 def factors(g, u):
@@ -232,12 +244,11 @@
 
     raw_parts = pl.pallas_call(
         raw_kernel,
-        grid=(n_node,),
-        in_specs=[
-            pl.BlockSpec((slots, feat), lambda i: (0, 0)),
-            pl.BlockSpec((feat, quarter), lambda i: (0, i)),
-        ],
-        out_specs=pl.BlockSpec((1, slots, quarter), lambda i: (i, 0, 0)),
+        in_specs=[VMEM, HBM],
+        scratch_shapes=[
+            pltpu.VMEM((n_node, feat, quarter), BF),
+            pltpu.SemaphoreType.DMA((n_node,)),
+        ],
         out_shape=jax.ShapeDtypeStruct((n_node, slots, quarter), BF),
         compiler_params=params(),
         name="raw",
@@ -277,7 +288,8 @@
             name="grads",
         )(place, deltas, *pieces, *before)
 
-    grads = products(((x_rows,), x_prev, x_next), (0, n_node - 1, 1), ())
+    grads = products(((x_rows,),), (0,), ())
+    grads = products((x_prev, x_next), (n_node - 1, 1), (grads,))
     grads = products((x_across,), (2,), (grads,))
     z_sum = lax.psum_scatter(
         grads.reshape(n_z * n_y * n_node * tall, 128), "z", scatter_dimension=0, tiled=True

time: 157 us -> 157 us (level)
  waiting for transfers between devices: 38.1 us -> 36.5 us
    reduce_scatter x1, waiting for transfers between devices: 31.1 us -> 28.2 us  [local(): lax.psum_scatter(grads.reshape(n_z * n_y * n_node * tall, 128), 'z', scat...]
    ppermute x3, waiting for transfers between devices: 2.65 us -> 5.43 us  [local(): lax.ppermute(slot_input[k], 'local', [(i, i ^ k) for i in range(n_local)])]
    pallas_call x2 -> x3, Pallas kernels: 6.82 us -> 8.22 us  [products(): pl.pallas_call(functools.partial(grads_kernel, own, [[next(at) for _ in g...]
  transfers between devices with their start and end apart: 12 -> 12, of which waited for: 6 -> 7; matrix products, arithmetic and copies ran while one was open for 1% -> 1% of each run, Pallas kernels for 10% -> 10%
where the time goes in v9:
time: 157 us; the launch traced here: 155 us
  starting transfers between devices  43.2 us (28%)
  waiting for transfers between devices  36.5 us (23%)
  blocking collectives  32.8 us (21%)
  Pallas kernels  22.1 us (14%)
  between operations  14.3 us (9%)
  local copies, waits for them, and re-layouts  6.06 us (4%)
    reduce_scatter x1, waiting for transfers between devices, local(): lax.psum_scatter(grads.reshape(n_z * n_y * n_node * tall, 128), 'z', scat...  28.2 us
    ppermute x6, starting transfers between devices, ring(): return lax.ppermute(x, axis, [(i, (i + step) % n) for i in range(n)])  25 us
    all_to_all x1, blocking collectives, local(): lax.all_to_all(z_sum.reshape(n_y * n_node, tall, 128), ('y', 'node'), spl...  19 us
    all_gather x1, blocking collectives, local(): raw = lax.all_gather(raw_share, 'node', axis=0, tiled=False)  13.8 us
    pallas_call x3, Pallas kernels, products(): pl.pallas_call(functools.partial(grads_kernel, own, [[next(at) for _ in g...  8.22 us
    ppermute x3, starting transfers between devices, local(): lax.ppermute(slot_input[k], 'local', [(i, i ^ k) for i in range(n_local)])  7.59 us
    all_to_all x1, starting transfers between devices, local(): lax.all_to_all(raw_parts, 'node', split_axis=0, concat_axis=0, tiled=True)  7.14 us
    ppermute x3, waiting for transfers between devices, local(): lax.ppermute(slot_input[k], 'local', [(i, i ^ k) for i in range(n_local)])  5.43 us
  transfers between devices with their start and end apart: 12, of which 7 were waited for; matrix products, arithmetic and copies ran while one was open for 1% of the time, Pallas kernels for 10%

profile of v9, /device:TPU:6, one launch (start us, length us, event | category | flops | bytes accessed | tf_op | source)
XLA Modules:
  0.0 155.0 jit_solution(18330792597828919046)
XLA Ops:
  7.2 2.7 %dispatch.1 = bf16[4,72,960]{2,1,0:T(8,128)(2,1)} custom-call(s32[2,128]{1,0:T(2,128)} %bitcast.42, bf16[2,128]{1,0:T(2,128)(2,1)} %bitcast.44, bf16[960,128]{1,0:T(8,128)(2,1)} %bitcast.49), custom_call_target="tpu_custom_call" | custom-call | tf_op jit(solution)/shard_map/dispatch/pallas_call | solution.py:224
  9.9 3.5 %all-to-all-start = ((bf16[4,72,960]{2,1,0:T(8,128)(2,1)}), bf16[4,72,960]{2,1,0:T(8,128)(2,1)S(1)}, u32[]{:S(2)}, u32[]{:S(2)}) async-start(bf16[4,72,960]{2,1,0:T(8,128)(2,1)} %dispatch.1), calls=%async_computation | async-start | bytes 1179648 | tf_op jit(solution)/shard_map/all_to_all | solution.py:237
  13.4 2.0 %fusion = (bf16[144,960]{1,0:T(8,128)(2,1)}, bf16[144,960]{1,0:T(8,128)(2,1)}) fusion(bf16[288,960]{1,0:T(8,128)(2,1)} %bitcast.31), kind=kLoop, calls=%fused_computation.5 | loop fusion | bytes 1105920 | tf_op jit(solution)/shard_map/slice | solution.py:241
  15.4 11.4 %collective-permute-start = (bf16[144,960]{1,0:T(8,128)(2,1)}, bf16[144,960]{1,0:T(8,128)(2,1)S(1)}, u32[]{:S(2)}, u32[]{:S(2)}) collective-permute-start(bf16[144,960]{1,0:T(8,128)(2,1)} %get-tuple-element.35), channel_id=1, source_target_pairs={{0,4},{4,8},{8,12},{12,0},{1,5},{5,9},{9,13},{13,1},{2,6},{6,10},{... | collective-permute-start | bytes 829448 | tf_op jit(solution)/shard_map/ppermute | solution.py:198
  26.8 1.9 %collective-permute-start.1 = (bf16[144,960]{1,0:T(8,128)(2,1)}, bf16[144,960]{1,0:T(8,128)(2,1)S(1)}, u32[]{:S(2)}, u32[]{:S(2)}) collective-permute-start(bf16[144,960]{1,0:T(8,128)(2,1)} %get-tuple-element.34), channel_id=1, source_target_pairs={{0,12},{4,0},{8,4},{12,8},{1,13},{5,1},{9,5},{13,9},{2,14},{6,2},{... | collective-permute-start | bytes 829448 | tf_op jit(solution)/shard_map/ppermute | solution.py:198
  28.7 3.7 %raw.1 = bf16[4,288,256]{2,1,0:T(8,128)(2,1)} custom-call(bf16[288,960]{1,0:T(8,128)(2,1)S(1)} %bitcast.38, bf16[960,1024]{1,0:T(8,128)(2,1)} %bitcast.47), custom_call_target="tpu_custom_call" | custom-call | tf_op jit(solution)/shard_map/raw/pallas_call | solution.py:245
  32.4 7.1 %all-to-all-start.1 = ((bf16[4,288,256]{2,1,0:T(8,128)(2,1)}), bf16[4,288,256]{2,1,0:T(8,128)(2,1)S(1)}, u32[]{:S(2)}, u32[]{:S(2)}) async-start(bf16[4,288,256]{2,1,0:T(8,128)(2,1)} %raw.1), calls=%async_computation.1 | async-start | bytes 1179648 | tf_op jit(solution)/shard_map/all_to_all | solution.py:256
  39.6 2.0 %collective-permute-start.4 = (bf16[144,960]{1,0:T(8,128)(2,1)}, bf16[144,960]{1,0:T(8,128)(2,1)S(1)}, u32[]{:S(2)}, u32[]{:S(2)}) collective-permute-start(bf16[144,960]{1,0:T(8,128)(2,1)} %get-tuple-element.34), channel_id=1, source_target_pairs={{0,4},{4,8},{8,12},{12,0},{1,5},{5,9},{9,13},{13,1},{2,6},{6,10},{... | collective-permute-start | bytes 829448 | tf_op jit(solution)/shard_map/ppermute | solution.py:198
  41.6 3.8 %collective-permute-start.5 = (bf16[144,960]{1,0:T(8,128)(2,1)}, bf16[144,960]{1,0:T(8,128)(2,1)}, u32[]{:S(2)}, u32[]{:S(2)}) collective-permute-start(bf16[144,960]{1,0:T(8,128)(2,1)} %get-tuple-element.35), channel_id=1, source_target_pairs={{0,12},{4,0},{8,4},{12,8},{1,13},{5,1},{9,5},{13,9},{2,14},{6,2},{... | collective-permute-start | bytes 829448 | tf_op jit(solution)/shard_map/ppermute | solution.py:198
  45.5 3.2 %collective-permute-start.2 = (bf16[144,960]{1,0:T(8,128)(2,1)S(1)}, bf16[144,960]{1,0:T(8,128)(2,1)S(1)}, u32[]{:S(2)}, u32[]{:S(2)}) collective-permute-start(bf16[144,960]{1,0:T(8,128)(2,1)S(1)} %collective-permute-done.refs_0_), channel_id=1, source_target_pairs={{0,4},{4,8},{8,12},{12,0},{1,5},{5,9},{9,13},{13,1},{2,6},{6,10},{... | collective-permute-start | bytes 829448 | tf_op jit(solution)/shard_map/ppermute | solution.py:198
  48.7 2.6 %collective-permute-start.3 = (bf16[144,960]{1,0:T(8,128)(2,1)S(1)}, bf16[144,960]{1,0:T(8,128)(2,1)}, u32[]{:S(2)}, u32[]{:S(2)}) collective-permute-start(bf16[144,960]{1,0:T(8,128)(2,1)S(1)} %collective-permute-done.1.refs_3_), channel_id=1, source_target_pairs={{0,12},{4,0},{8,4},{12,8},{1,13},{5,1},{9,5},{13,9},{2,14},{6,2},{... | collective-permute-start | bytes 829448 | tf_op jit(solution)/shard_map/ppermute | solution.py:198
  51.4 0.8 share.1
  52.2 2.3 %grads.3.refs_4_ = bf16[12,4,4,80,128]{4,3,2,1,0:T(8,128)(2,1)} custom-call(s32[3]{0:T(128)S(1)} %pad_add_fusion.place_ref, bf16[288,512]{1,0:T(8,128)(2,1)S(1)} %get-tuple-element.17.delta_ref, bf16[288,960]{1,0:T(8,128)(2,1)S(1)} %bitcast.32), custom_call_target="tpu_custom_call" | custom-call | tf_op jit(solution)/shard_map/grads/pallas_call | solution.py:277
  54.5 0.4 collective-permute-done.4.refs_1_
  55.1 3.2 %grads.4.refs_2_ = bf16[12,4,4,80,128]{4,3,2,1,0:T(8,128)(2,1)} custom-call(s32[3]{0:T(128)S(1)} %pad_add_fusion.place_ref, bf16[288,512]{1,0:T(8,128)(2,1)S(1)} %get-tuple-element.17.delta_ref, bf16[144,960]{1,0:T(8,128)(2,1)S(1)} %collective-permute-done.refs_0_, ...), custom_call_target="tpu_custom_call", output_to_operand_aliasing={{}: (6, {})} | custom-call | tf_op jit(solution)/shard_map/grads/pallas_call | solution.py:277
  58.4 1.5 collective-permute-done.2.refs_0_
  59.8 0.7 collective-permute-done.3.refs_1_
  60.6 2.7 %grads.5 = bf16[12,4,4,80,128]{4,3,2,1,0:T(8,128)(2,1)} custom-call(s32[3]{0:T(128)S(1)} %pad_add_fusion.place_ref, bf16[288,512]{1,0:T(8,128)(2,1)S(1)} %get-tuple-element.17.delta_ref, bf16[144,960]{1,0:T(8,128)(2,1)S(1)} %collective-permute-done.2.refs_0_, bf16[144,960]{1,0:T(8,128)(2,1)} %collective-permute-done.3.refs_1_, ...), custom_call_target="tpu_custom_call", output_to_operand_aliasing={{}: (4, {})} | custom-call | tf_op jit(solution)/shard_map/grads/pallas_call | solution.py:277
  63.3 0.9 copy-done.6
  64.2 13.8 %all-gather = bf16[1152,256]{1,0:T(8,128)(2,1)S(1)} all-gather(bf16[288,256]{1,0:T(8,128)(2,1)S(1)} %copy-done.6), channel_id=2, replica_groups=mesh['y'=4,'z'=12,'node'=4,'local'=4] {'node'}, dimensions={0}, use_global_device_ids=true | all-gather | bytes 737280 | tf_op jit(solution)/shard_map/all_gather | solution.py:299
  78.0 1.6 %copy-done.3 = bf16[1,960,1024]{2,1,0:T(8,128)(2,1)S(1)} copy-done((bf16[1,960,1024]{2,1,0:T(8,128)(2,1)S(1)}, bf16[1,960,1024]{2,1,0:T(8,128)(2,1)}, u32[]{:S(2)}) %copy-start.3) | copy-done | bytes 1966104
  79.6 1.5 copy-done.4
  81.1 3.8 %slot_input.1 = bf16[4,72,1024]{2,1,0:T(8,128)(2,1)S(1)} custom-call(s32[3]{0:T(128)S(1)} %pad_add_fusion.place_ref, bf16[4,288,256]{2,1,0:T(8,128)(2,1)S(1)} %bitcast.33, bf16[288,1024]{1,0:T(8,128)(2,1)S(1)} %bitcast.35, bf16[288,1024]{1,0:T(8,128)(2,1)S(1)} %bitcast.37, bf16[960,1024]{1,0:T(8,128)(2,1)S(1)} %bitcast.39, bf16[960,1024]{1,0:T(8,128)(2,1)S(1)} %bitcast.40), custom_call_target="tpu_custom_call" | custom-call | tf_op jit(solution)/shard_map/slot_input/pallas_call | solution.py:300
  84.9 1.9 %collective-permute-start.6 = (bf16[72,1024]{1,0:T(8,128)(2,1)S(1)}, bf16[72,1024]{1,0:T(8,128)(2,1)S(1)}, u32[]{:S(2)}, u32[]{:S(2)}) collective-permute-start(bf16[72,1024]{1,0:T(8,128)(2,1)S(1)} %get-tuple-element.32), channel_id=1, source_target_pairs={{0,1},{1,0},{2,3},{3,2},{4,5},{5,4},{6,7},{7,6},{8,9},{9,8},{10,11... | collective-permute-start | bytes 442376 | tf_op jit(solution)/shard_map/ppermute | solution.py:318
  86.8 3.4 %collective-permute-start.7 = (bf16[72,1024]{1,0:T(8,128)(2,1)S(1)}, bf16[72,1024]{1,0:T(8,128)(2,1)S(1)}, u32[]{:S(2)}, u32[]{:S(2)}) collective-permute-start(bf16[72,1024]{1,0:T(8,128)(2,1)S(1)} %get-tuple-element.31), channel_id=1, source_target_pairs={{0,2},{1,3},{2,0},{3,1},{4,6},{5,7},{6,4},{7,5},{8,10},{9,11},{10,... | collective-permute-start | bytes 442376 | tf_op jit(solution)/shard_map/ppermute | solution.py:318
  90.2 2.3 %collective-permute-start.8 = (bf16[72,1024]{1,0:T(8,128)(2,1)S(1)}, bf16[72,1024]{1,0:T(8,128)(2,1)S(1)}, u32[]{:S(2)}, u32[]{:S(2)}) collective-permute-start(bf16[72,1024]{1,0:T(8,128)(2,1)S(1)} %get-tuple-element.30), channel_id=1, source_target_pairs={{0,3},{1,2},{2,1},{3,0},{4,7},{5,6},{6,5},{7,4},{8,11},{9,10},{10,... | collective-permute-start | bytes 442376 | tf_op jit(solution)/shard_map/ppermute | solution.py:318
  92.5 2.5 %collective-permute-done.7.rest_2_ = bf16[72,1024]{1,0:T(8,128)(2,1)S(1)} collective-permute-done((bf16[72,1024]{1,0:T(8,128)(2,1)S(1)}, bf16[72,1024]{1,0:T(8,128)(2,1)S(1)}, u32[]{:S(2)}, u32[]{:S(2)}) %collective-permute-start.7) | collective-permute-done | bytes 147488 | tf_op jit(solution)/shard_map/ppermute | solution.py:318
  95.0 3.0 %collective-permute-done.8.rest_3_ = bf16[72,1024]{1,0:T(8,128)(2,1)S(1)} collective-permute-done((bf16[72,1024]{1,0:T(8,128)(2,1)S(1)}, bf16[72,1024]{1,0:T(8,128)(2,1)S(1)}, u32[]{:S(2)}, u32[]{:S(2)}) %collective-permute-start.8) | collective-permute-done | bytes 147488 | tf_op jit(solution)/shard_map/ppermute | solution.py:318
  98.0 2.2 %combine.1 = (bf16[960,128]{1,0:T(8,128)(2,1)}, bf16[2,128]{1,0:T(2,128)(2,1)}) custom-call(s32[3]{0:T(128)S(1)} %pad_add_fusion.place_ref, s32[2,128]{1,0:T(2,128)S(1)} %bitcast.43, bf16[2,128]{1,0:T(2,128)(2,1)S(1)} %bitcast.45, bf16[72,1024]{1,0:T(8,128)(2,1)S(1)} %get-tuple-element.33.rest_0_, bf16[72,1024]{1,0:T(8,128)(2,1)S(1)} %collective-permute-done.6.rest_1_, ...), custom_call_target="tpu_custom_call" | custom-call | tf_op jit(solution)/shard_map/combine/pallas_call | solution.py:321
  100.1 28.2 %reduce-scatter.2.cloned.1.call-done = bf16[1280,128]{1,0:T(8,128)(2,1)} async-done(((bf16[15360,128]{1,0:T(8,128)(2,1)}), bf16[1280,128]{1,0:T(8,128)(2,1)}) %reduce-scatter.2.cloned.1.call-update) | async-done | bytes 327696 | tf_op jit(solution)/shard_map/reduce_scatter | solution.py:294
  128.4 19.0 %all_to_all.15 = bf16[16,80,128]{2,1,0:T(8,128)(2,1)S(1)} all-to-all(bf16[16,80,128]{2,1,0:T(8,128)(2,1)} %bitcast.48), channel_id=1, replica_groups=mesh['y'=4,'z'=12,'node'=4,'local'=4] {'y','node'}, dimensions={0} | all-to-all | bytes 655360 | tf_op jit(solution)/shard_map/all_to_all | solution.py:333
  147.4 0.8 final.1
  (25 shorter events, 0.4 us)
Async XLA Ops:
  7.2 44.2 %copy-start.2 = (bf16[1,1,4,72,1024]{4,3,2,1,0:T(8,128)(2,1)S(1)}, bf16[1,1,4,72,1024]{4,3,2,1,0:T(8,128)(2,1)}, u32[]{:S(2)}) copy-start(bf16[1,1,4,72,1024]{4,3,2,1,0:T(8,128)(2,1)} %param.14) | copy-start | bytes 1769476
  7.2 44.2 %copy-start.1 = (bf16[1,1,4,72,1024]{4,3,2,1,0:T(8,128)(2,1)S(1)}, bf16[1,1,4,72,1024]{4,3,2,1,0:T(8,128)(2,1)}, u32[]{:S(2)}) copy-start(bf16[1,1,4,72,1024]{4,3,2,1,0:T(8,128)(2,1)} %param.13) | copy-start | bytes 1769476
  9.9 18.8 %all-to-all-start = ((bf16[4,72,960]{2,1,0:T(8,128)(2,1)}), bf16[4,72,960]{2,1,0:T(8,128)(2,1)S(1)}, u32[]{:S(2)}, u32[]{:S(2)}) async-start(bf16[4,72,960]{2,1,0:T(8,128)(2,1)} %dispatch.1), calls=%async_computation | async-start | bytes 1179648 | tf_op jit(solution)/shard_map/all_to_all | solution.py:237
  13.4 38.8 %copy-start = (bf16[1,1,4,72,960]{4,3,2,1,0:T(8,128)(2,1)S(1)}, bf16[1,1,4,72,960]{4,3,2,1,0:T(8,128)(2,1)}, u32[]{:S(2)}) copy-start(bf16[1,1,4,72,960]{4,3,2,1,0:T(8,128)(2,1)} %param.12) | copy-start | bytes 1658884
  15.4 30.1 %collective-permute-start = (bf16[144,960]{1,0:T(8,128)(2,1)}, bf16[144,960]{1,0:T(8,128)(2,1)S(1)}, u32[]{:S(2)}, u32[]{:S(2)}) collective-permute-start(bf16[144,960]{1,0:T(8,128)(2,1)} %get-tuple-element.35), channel_id=1, source_target_pairs={{0,4},{4,8},{8,12},{12,0},{1,5},{5,9},{9,13},{13,1},{2,6},{6,10},{... | collective-permute-start | bytes 829448 | tf_op jit(solution)/shard_map/ppermute | solution.py:198
  26.8 18.7 %collective-permute-start.1 = (bf16[144,960]{1,0:T(8,128)(2,1)}, bf16[144,960]{1,0:T(8,128)(2,1)S(1)}, u32[]{:S(2)}, u32[]{:S(2)}) collective-permute-start(bf16[144,960]{1,0:T(8,128)(2,1)} %get-tuple-element.34), channel_id=1, source_target_pairs={{0,12},{4,0},{8,4},{12,8},{1,13},{5,1},{9,5},{13,9},{2,14},{6,2},{... | collective-permute-start | bytes 829448 | tf_op jit(solution)/shard_map/ppermute | solution.py:198
  32.4 19.0 %all-to-all-start.1 = ((bf16[4,288,256]{2,1,0:T(8,128)(2,1)}), bf16[4,288,256]{2,1,0:T(8,128)(2,1)S(1)}, u32[]{:S(2)}, u32[]{:S(2)}) async-start(bf16[4,288,256]{2,1,0:T(8,128)(2,1)} %raw.1), calls=%async_computation.1 | async-start | bytes 1179648 | tf_op jit(solution)/shard_map/all_to_all | solution.py:256
  39.6 88.8 %reduce-scatter.2.cloned.1.call-start = ((), (), s32[]{:S(2)}) async-start(), calls=%async_computation.4 | async-start | bytes 4259840 | tf_op jit(solution)/shard_map/reduce_scatter | solution.py:294
  39.6 15.3 %collective-permute-start.4 = (bf16[144,960]{1,0:T(8,128)(2,1)}, bf16[144,960]{1,0:T(8,128)(2,1)S(1)}, u32[]{:S(2)}, u32[]{:S(2)}) collective-permute-start(bf16[144,960]{1,0:T(8,128)(2,1)} %get-tuple-element.34), channel_id=1, source_target_pairs={{0,4},{4,8},{8,12},{12,0},{1,5},{5,9},{9,13},{13,1},{2,6},{6,10},{... | collective-permute-start | bytes 829448 | tf_op jit(solution)/shard_map/ppermute | solution.py:198
  41.6 13.5 %collective-permute-start.5 = (bf16[144,960]{1,0:T(8,128)(2,1)}, bf16[144,960]{1,0:T(8,128)(2,1)}, u32[]{:S(2)}, u32[]{:S(2)}) collective-permute-start(bf16[144,960]{1,0:T(8,128)(2,1)} %get-tuple-element.35), channel_id=1, source_target_pairs={{0,12},{4,0},{8,4},{12,8},{1,13},{5,1},{9,5},{13,9},{2,14},{6,2},{... | collective-permute-start | bytes 829448 | tf_op jit(solution)/shard_map/ppermute | solution.py:198
  45.5 14.4 %collective-permute-start.2 = (bf16[144,960]{1,0:T(8,128)(2,1)S(1)}, bf16[144,960]{1,0:T(8,128)(2,1)S(1)}, u32[]{:S(2)}, u32[]{:S(2)}) collective-permute-start(bf16[144,960]{1,0:T(8,128)(2,1)S(1)} %collective-permute-done.refs_0_), channel_id=1, source_target_pairs={{0,4},{4,8},{8,12},{12,0},{1,5},{5,9},{9,13},{13,1},{2,6},{6,10},{... | collective-permute-start | bytes 829448 | tf_op jit(solution)/shard_map/ppermute | solution.py:198
  48.7 11.9 %collective-permute-start.3 = (bf16[144,960]{1,0:T(8,128)(2,1)S(1)}, bf16[144,960]{1,0:T(8,128)(2,1)}, u32[]{:S(2)}, u32[]{:S(2)}) collective-permute-start(bf16[144,960]{1,0:T(8,128)(2,1)S(1)} %collective-permute-done.1.refs_3_), channel_id=1, source_target_pairs={{0,12},{4,0},{8,4},{12,8},{1,13},{5,1},{9,5},{13,9},{2,14},{6,2},{... | collective-permute-start | bytes 829448 | tf_op jit(solution)/shard_map/ppermute | solution.py:198
  52.2 6.2 %copy-start.5 = (bf16[288,256]{1,0:T(8,128)(2,1)}, bf16[288,256]{1,0:T(8,128)(2,1)S(1)}, u32[]{:S(2)}) copy-start(bf16[288,256]{1,0:T(8,128)(2,1)S(1)} %get-tuple-element.22) | copy-start | bytes 442372
  63.3 0.9 copy-start.6
  64.2 33.8 %copy-start.7 = (s32[128,2]{0,1:T(2,128)S(1)}, s32[128,2]{0,1:T(2,128)}, u32[]{:S(2)}) copy-start(s32[128,2]{0,1:T(2,128)} %param.10) | copy-start | bytes 3076
  64.2 33.8 %copy-start.8 = (bf16[128,2]{0,1:T(2,128)(2,1)S(1)}, bf16[128,2]{0,1:T(2,128)(2,1)}, u32[]{:S(2)}) copy-start(bf16[128,2]{0,1:T(2,128)(2,1)} %param.11) | copy-start | bytes 1540
  78.0 1.6 %copy-start.3 = (bf16[1,960,1024]{2,1,0:T(8,128)(2,1)S(1)}, bf16[1,960,1024]{2,1,0:T(8,128)(2,1)}, u32[]{:S(2)}) copy-start(bf16[1,960,1024]{2,1,0:T(8,128)(2,1)} %param.15) | copy-start | bytes 5898244
  79.6 1.5 copy-start.4
  84.9 7.6 %collective-permute-start.6 = (bf16[72,1024]{1,0:T(8,128)(2,1)S(1)}, bf16[72,1024]{1,0:T(8,128)(2,1)S(1)}, u32[]{:S(2)}, u32[]{:S(2)}) collective-permute-start(bf16[72,1024]{1,0:T(8,128)(2,1)S(1)} %get-tuple-element.32), channel_id=1, source_target_pairs={{0,1},{1,0},{2,3},{3,2},{4,5},{5,4},{6,7},{7,6},{8,9},{9,8},{10,11... | collective-permute-start | bytes 442376 | tf_op jit(solution)/shard_map/ppermute | solution.py:318
  86.8 8.1 %collective-permute-start.7 = (bf16[72,1024]{1,0:T(8,128)(2,1)S(1)}, bf16[72,1024]{1,0:T(8,128)(2,1)S(1)}, u32[]{:S(2)}, u32[]{:S(2)}) collective-permute-start(bf16[72,1024]{1,0:T(8,128)(2,1)S(1)} %get-tuple-element.31), channel_id=1, source_target_pairs={{0,2},{1,3},{2,0},{3,1},{4,6},{5,7},{6,4},{7,5},{8,10},{9,11},{10,... | collective-permute-start | bytes 442376 | tf_op jit(solution)/shard_map/ppermute | solution.py:318
  90.2 7.7 %collective-permute-start.8 = (bf16[72,1024]{1,0:T(8,128)(2,1)S(1)}, bf16[72,1024]{1,0:T(8,128)(2,1)S(1)}, u32[]{:S(2)}, u32[]{:S(2)}) collective-permute-start(bf16[72,1024]{1,0:T(8,128)(2,1)S(1)} %get-tuple-element.30), channel_id=1, source_target_pairs={{0,3},{1,2},{2,1},{3,0},{4,7},{5,6},{6,5},{7,4},{8,11},{9,10},{10,... | collective-permute-start | bytes 442376 | tf_op jit(solution)/shard_map/ppermute | solution.py:318
Sparse Core Ops, SparseCore 0:
  63.4 64.9 reduce-scatter.1

commit v10 on v9

--- a/solution.py
+++ b/solution.py
@@ -94,7 +94,7 @@
 
 def grads_kernel(own, groups, turns, place_ref, delta_ref, *refs):
     out_ref, held, sems = refs[-3:]
-    n_z, n_y, n_node = out_ref.shape[:3]
+    n_z, n_node, n_y = out_ref.shape[:3]
     copies = []
     for k, (group, turn) in enumerate(zip(groups, turns)):
         slot = k % held.shape[0]
@@ -112,7 +112,7 @@
             held[slot, i % n_z, i // n_z] = tall.astype(BF)
         to = lax.rem(place_ref[1] + turn, n_node)
         copies.append(
-            pltpu.make_async_copy(held.at[slot], out_ref.at[:, :, to], sems.at[slot])
+            pltpu.make_async_copy(held.at[slot], out_ref.at[:, to], sems.at[slot])
         )
         copies[k].start()
     for copy in copies[-held.shape[0] :]:
@@ -173,11 +173,11 @@
 
 
 def final_kernel(n_copies, own, parts_ref, gate_ref, up_ref):
-    copies, n_node = parts_ref.shape[0], parts_ref.shape[1]
+    n_node, copies = parts_ref.shape[0], parts_ref.shape[1]
     for x in range(n_node):
-        total = parts_ref[0, x].astype(F32)
+        total = parts_ref[x, 0].astype(F32)
         for i in range(1, copies):
-            total = total + parts_ref[i, x].astype(F32)
+            total = total + parts_ref[x, i].astype(F32)
         total = total * (1.0 / n_copies)
         per = total.shape[0] // own // 2
         for c in range(2 * per):
@@ -278,7 +278,7 @@
             functools.partial(grads_kernel, own, [[next(at) for _ in g] for g in groups], turns),
             in_specs=[SMEM] + [VMEM] * (1 + len(pieces)) + [HBM] * len(before),
             out_specs=HBM,
-            out_shape=pltpu.HBM((n_z, n_y, n_node, tall, 128), BF),
+            out_shape=pltpu.HBM((n_z, n_node, n_y, tall, 128), BF),
             scratch_shapes=[
                 pltpu.VMEM((count, n_z, n_y, tall, 128), BF),
                 pltpu.SemaphoreType.DMA((count,)),
@@ -331,8 +331,8 @@
 
     z_sum, input_grads, gate_grads = lax.optimization_barrier((z_sum, input_grads, gate_grads))
     parts = lax.all_to_all(
-        z_sum.reshape(n_y * n_node, tall, 128),
-        ("y", "node"),
+        z_sum.reshape(n_node * n_y, tall, 128),
+        ("node", "y"),
         split_axis=0,
         concat_axis=0,
         tiled=True,
@@ -342,7 +342,7 @@
         out_shape=[jax.ShapeDtypeStruct((own, hidden // 128, 128), F32)] * 2,
         compiler_params=params(),
         name="final",
-    )(parts.reshape(n_y, n_node, tall, 128))
+    )(parts.reshape(n_node, n_y, tall, 128))
     rows = own * hidden // 128
     return (
         input_grads.T,

time: 157 us -> 157 us (level)
  no operation moved by 1% of the time
where the time goes in v10:
time: 157 us; the launch traced here: 155 us
  starting transfers between devices  43.2 us (28%)
  waiting for transfers between devices  36.5 us (23%)
  blocking collectives  33.2 us (21%)
  Pallas kernels  22.1 us (14%)
  between operations  14.3 us (9%)
  local copies, waits for them, and re-layouts  6.08 us (4%)
    reduce_scatter x1, waiting for transfers between devices, local(): lax.psum_scatter(grads.reshape(n_z * n_y * n_node * tall, 128), 'z', scat...  28.2 us
    ppermute x6, starting transfers between devices, ring(): return lax.ppermute(x, axis, [(i, (i + step) % n) for i in range(n)])  25 us
    all_to_all x1, blocking collectives, local(): lax.all_to_all(z_sum.reshape(n_node * n_y, tall, 128), ('node', 'y'), spl...  19.5 us
    all_gather x1, blocking collectives, local(): raw = lax.all_gather(raw_share, 'node', axis=0, tiled=False)  13.7 us
    pallas_call x3, Pallas kernels, products(): pl.pallas_call(functools.partial(grads_kernel, own, [[next(at) for _ in g...  8.2 us
    ppermute x3, starting transfers between devices, local(): lax.ppermute(slot_input[k], 'local', [(i, i ^ k) for i in range(n_local)])  7.59 us
    all_to_all x1, starting transfers between devices, local(): lax.all_to_all(raw_parts, 'node', split_axis=0, concat_axis=0, tiled=True)  7.14 us
    ppermute x3, waiting for transfers between devices, local(): lax.ppermute(slot_input[k], 'local', [(i, i ^ k) for i in range(n_local)])  5.44 us
  transfers between devices with their start and end apart: 12, of which 7 were waited for; matrix products, arithmetic and copies ran while one was open for 1% of the time, Pallas kernels for 10%

profile of v10, /device:TPU:6, one launch (start us, length us, event | category | flops | bytes accessed | tf_op | source)
XLA Modules:
  0.0 155.5 jit_solution(8696358704542931427)
XLA Ops:
  7.2 2.7 %dispatch.1 = bf16[4,72,960]{2,1,0:T(8,128)(2,1)} custom-call(s32[2,128]{1,0:T(2,128)} %bitcast.42, bf16[2,128]{1,0:T(2,128)(2,1)} %bitcast.44, bf16[960,128]{1,0:T(8,128)(2,1)} %bitcast.49), custom_call_target="tpu_custom_call" | custom-call | tf_op jit(solution)/shard_map/dispatch/pallas_call | solution.py:224
  9.9 3.5 %all-to-all-start = ((bf16[4,72,960]{2,1,0:T(8,128)(2,1)}), bf16[4,72,960]{2,1,0:T(8,128)(2,1)S(1)}, u32[]{:S(2)}, u32[]{:S(2)}) async-start(bf16[4,72,960]{2,1,0:T(8,128)(2,1)} %dispatch.1), calls=%async_computation | async-start | bytes 1179648 | tf_op jit(solution)/shard_map/all_to_all | solution.py:237
  13.4 2.0 %fusion = (bf16[144,960]{1,0:T(8,128)(2,1)}, bf16[144,960]{1,0:T(8,128)(2,1)}) fusion(bf16[288,960]{1,0:T(8,128)(2,1)} %bitcast.31), kind=kLoop, calls=%fused_computation.5 | loop fusion | bytes 1105920 | tf_op jit(solution)/shard_map/slice | solution.py:241
  15.4 11.4 %collective-permute-start = (bf16[144,960]{1,0:T(8,128)(2,1)}, bf16[144,960]{1,0:T(8,128)(2,1)S(1)}, u32[]{:S(2)}, u32[]{:S(2)}) collective-permute-start(bf16[144,960]{1,0:T(8,128)(2,1)} %get-tuple-element.35), channel_id=1, source_target_pairs={{0,4},{4,8},{8,12},{12,0},{1,5},{5,9},{9,13},{13,1},{2,6},{6,10},{... | collective-permute-start | bytes 829448 | tf_op jit(solution)/shard_map/ppermute | solution.py:198
  26.8 1.9 %collective-permute-start.1 = (bf16[144,960]{1,0:T(8,128)(2,1)}, bf16[144,960]{1,0:T(8,128)(2,1)S(1)}, u32[]{:S(2)}, u32[]{:S(2)}) collective-permute-start(bf16[144,960]{1,0:T(8,128)(2,1)} %get-tuple-element.34), channel_id=1, source_target_pairs={{0,12},{4,0},{8,4},{12,8},{1,13},{5,1},{9,5},{13,9},{2,14},{6,2},{... | collective-permute-start | bytes 829448 | tf_op jit(solution)/shard_map/ppermute | solution.py:198
  28.7 3.7 %raw.1 = bf16[4,288,256]{2,1,0:T(8,128)(2,1)} custom-call(bf16[288,960]{1,0:T(8,128)(2,1)S(1)} %bitcast.38, bf16[960,1024]{1,0:T(8,128)(2,1)} %bitcast.47), custom_call_target="tpu_custom_call" | custom-call | tf_op jit(solution)/shard_map/raw/pallas_call | solution.py:245
  32.4 7.1 %all-to-all-start.1 = ((bf16[4,288,256]{2,1,0:T(8,128)(2,1)}), bf16[4,288,256]{2,1,0:T(8,128)(2,1)S(1)}, u32[]{:S(2)}, u32[]{:S(2)}) async-start(bf16[4,288,256]{2,1,0:T(8,128)(2,1)} %raw.1), calls=%async_computation.1 | async-start | bytes 1179648 | tf_op jit(solution)/shard_map/all_to_all | solution.py:256
  39.6 2.0 %collective-permute-start.4 = (bf16[144,960]{1,0:T(8,128)(2,1)}, bf16[144,960]{1,0:T(8,128)(2,1)S(1)}, u32[]{:S(2)}, u32[]{:S(2)}) collective-permute-start(bf16[144,960]{1,0:T(8,128)(2,1)} %get-tuple-element.34), channel_id=1, source_target_pairs={{0,4},{4,8},{8,12},{12,0},{1,5},{5,9},{9,13},{13,1},{2,6},{6,10},{... | collective-permute-start | bytes 829448 | tf_op jit(solution)/shard_map/ppermute | solution.py:198
  41.6 3.8 %collective-permute-start.5 = (bf16[144,960]{1,0:T(8,128)(2,1)}, bf16[144,960]{1,0:T(8,128)(2,1)}, u32[]{:S(2)}, u32[]{:S(2)}) collective-permute-start(bf16[144,960]{1,0:T(8,128)(2,1)} %get-tuple-element.35), channel_id=1, source_target_pairs={{0,12},{4,0},{8,4},{12,8},{1,13},{5,1},{9,5},{13,9},{2,14},{6,2},{... | collective-permute-start | bytes 829448 | tf_op jit(solution)/shard_map/ppermute | solution.py:198
  45.5 3.2 %collective-permute-start.2 = (bf16[144,960]{1,0:T(8,128)(2,1)S(1)}, bf16[144,960]{1,0:T(8,128)(2,1)S(1)}, u32[]{:S(2)}, u32[]{:S(2)}) collective-permute-start(bf16[144,960]{1,0:T(8,128)(2,1)S(1)} %collective-permute-done.refs_0_), channel_id=1, source_target_pairs={{0,4},{4,8},{8,12},{12,0},{1,5},{5,9},{9,13},{13,1},{2,6},{6,10},{... | collective-permute-start | bytes 829448 | tf_op jit(solution)/shard_map/ppermute | solution.py:198
  48.7 2.6 %collective-permute-start.3 = (bf16[144,960]{1,0:T(8,128)(2,1)S(1)}, bf16[144,960]{1,0:T(8,128)(2,1)}, u32[]{:S(2)}, u32[]{:S(2)}) collective-permute-start(bf16[144,960]{1,0:T(8,128)(2,1)S(1)} %collective-permute-done.1.refs_3_), channel_id=1, source_target_pairs={{0,12},{4,0},{8,4},{12,8},{1,13},{5,1},{9,5},{13,9},{2,14},{6,2},{... | collective-permute-start | bytes 829448 | tf_op jit(solution)/shard_map/ppermute | solution.py:198
  51.4 0.8 share.1
  52.2 2.3 %grads.3.refs_4_ = bf16[12,4,4,80,128]{4,3,2,1,0:T(8,128)(2,1)} custom-call(s32[3]{0:T(128)S(1)} %pad_add_fusion.place_ref, bf16[288,512]{1,0:T(8,128)(2,1)S(1)} %get-tuple-element.17.delta_ref, bf16[288,960]{1,0:T(8,128)(2,1)S(1)} %bitcast.32), custom_call_target="tpu_custom_call" | custom-call | tf_op jit(solution)/shard_map/grads/pallas_call | solution.py:277
  54.5 0.4 collective-permute-done.4.refs_1_
  55.1 3.2 %grads.4.refs_2_ = bf16[12,4,4,80,128]{4,3,2,1,0:T(8,128)(2,1)} custom-call(s32[3]{0:T(128)S(1)} %pad_add_fusion.place_ref, bf16[288,512]{1,0:T(8,128)(2,1)S(1)} %get-tuple-element.17.delta_ref, bf16[144,960]{1,0:T(8,128)(2,1)S(1)} %collective-permute-done.refs_0_, ...), custom_call_target="tpu_custom_call", output_to_operand_aliasing={{}: (6, {})} | custom-call | tf_op jit(solution)/shard_map/grads/pallas_call | solution.py:277
  58.3 1.5 collective-permute-done.2.refs_0_
  59.8 0.7 collective-permute-done.3.refs_1_
  60.6 2.7 %grads.5 = bf16[12,4,4,80,128]{4,3,2,1,0:T(8,128)(2,1)} custom-call(s32[3]{0:T(128)S(1)} %pad_add_fusion.place_ref, bf16[288,512]{1,0:T(8,128)(2,1)S(1)} %get-tuple-element.17.delta_ref, bf16[144,960]{1,0:T(8,128)(2,1)S(1)} %collective-permute-done.2.refs_0_, bf16[144,960]{1,0:T(8,128)(2,1)} %collective-permute-done.3.refs_1_, ...), custom_call_target="tpu_custom_call", output_to_operand_aliasing={{}: (4, {})} | custom-call | tf_op jit(solution)/shard_map/grads/pallas_call | solution.py:277
  63.3 0.9 copy-done.6
  64.2 13.7 %all-gather = bf16[1152,256]{1,0:T(8,128)(2,1)S(1)} all-gather(bf16[288,256]{1,0:T(8,128)(2,1)S(1)} %copy-done.6), channel_id=2, replica_groups=mesh['y'=4,'z'=12,'node'=4,'local'=4] {'node'}, dimensions={0}, use_global_device_ids=true | all-gather | bytes 737280 | tf_op jit(solution)/shard_map/all_gather | solution.py:299
  77.9 1.6 %copy-done.3 = bf16[1,960,1024]{2,1,0:T(8,128)(2,1)S(1)} copy-done((bf16[1,960,1024]{2,1,0:T(8,128)(2,1)S(1)}, bf16[1,960,1024]{2,1,0:T(8,128)(2,1)}, u32[]{:S(2)}) %copy-start.3) | copy-done | bytes 1966104
  79.5 1.5 copy-done.4
  81.1 3.8 %slot_input.1 = bf16[4,72,1024]{2,1,0:T(8,128)(2,1)S(1)} custom-call(s32[3]{0:T(128)S(1)} %pad_add_fusion.place_ref, bf16[4,288,256]{2,1,0:T(8,128)(2,1)S(1)} %bitcast.33, bf16[288,1024]{1,0:T(8,128)(2,1)S(1)} %bitcast.35, bf16[288,1024]{1,0:T(8,128)(2,1)S(1)} %bitcast.37, bf16[960,1024]{1,0:T(8,128)(2,1)S(1)} %bitcast.39, bf16[960,1024]{1,0:T(8,128)(2,1)S(1)} %bitcast.40), custom_call_target="tpu_custom_call" | custom-call | tf_op jit(solution)/shard_map/slot_input/pallas_call | solution.py:300
  84.9 1.9 %collective-permute-start.6 = (bf16[72,1024]{1,0:T(8,128)(2,1)S(1)}, bf16[72,1024]{1,0:T(8,128)(2,1)S(1)}, u32[]{:S(2)}, u32[]{:S(2)}) collective-permute-start(bf16[72,1024]{1,0:T(8,128)(2,1)S(1)} %get-tuple-element.32), channel_id=1, source_target_pairs={{0,1},{1,0},{2,3},{3,2},{4,5},{5,4},{6,7},{7,6},{8,9},{9,8},{10,11... | collective-permute-start | bytes 442376 | tf_op jit(solution)/shard_map/ppermute | solution.py:318
  86.8 3.4 %collective-permute-start.7 = (bf16[72,1024]{1,0:T(8,128)(2,1)S(1)}, bf16[72,1024]{1,0:T(8,128)(2,1)S(1)}, u32[]{:S(2)}, u32[]{:S(2)}) collective-permute-start(bf16[72,1024]{1,0:T(8,128)(2,1)S(1)} %get-tuple-element.31), channel_id=1, source_target_pairs={{0,2},{1,3},{2,0},{3,1},{4,6},{5,7},{6,4},{7,5},{8,10},{9,11},{10,... | collective-permute-start | bytes 442376 | tf_op jit(solution)/shard_map/ppermute | solution.py:318
  90.2 2.3 %collective-permute-start.8 = (bf16[72,1024]{1,0:T(8,128)(2,1)S(1)}, bf16[72,1024]{1,0:T(8,128)(2,1)S(1)}, u32[]{:S(2)}, u32[]{:S(2)}) collective-permute-start(bf16[72,1024]{1,0:T(8,128)(2,1)S(1)} %get-tuple-element.30), channel_id=1, source_target_pairs={{0,3},{1,2},{2,1},{3,0},{4,7},{5,6},{6,5},{7,4},{8,11},{9,10},{10,... | collective-permute-start | bytes 442376 | tf_op jit(solution)/shard_map/ppermute | solution.py:318
  92.5 2.5 %collective-permute-done.7.rest_2_ = bf16[72,1024]{1,0:T(8,128)(2,1)S(1)} collective-permute-done((bf16[72,1024]{1,0:T(8,128)(2,1)S(1)}, bf16[72,1024]{1,0:T(8,128)(2,1)S(1)}, u32[]{:S(2)}, u32[]{:S(2)}) %collective-permute-start.7) | collective-permute-done | bytes 147488 | tf_op jit(solution)/shard_map/ppermute | solution.py:318
  94.9 3.0 %collective-permute-done.8.rest_3_ = bf16[72,1024]{1,0:T(8,128)(2,1)S(1)} collective-permute-done((bf16[72,1024]{1,0:T(8,128)(2,1)S(1)}, bf16[72,1024]{1,0:T(8,128)(2,1)S(1)}, u32[]{:S(2)}, u32[]{:S(2)}) %collective-permute-start.8) | collective-permute-done | bytes 147488 | tf_op jit(solution)/shard_map/ppermute | solution.py:318
  97.9 2.2 %combine.1 = (bf16[960,128]{1,0:T(8,128)(2,1)}, bf16[2,128]{1,0:T(2,128)(2,1)}) custom-call(s32[3]{0:T(128)S(1)} %pad_add_fusion.place_ref, s32[2,128]{1,0:T(2,128)S(1)} %bitcast.43, bf16[2,128]{1,0:T(2,128)(2,1)S(1)} %bitcast.45, bf16[72,1024]{1,0:T(8,128)(2,1)S(1)} %get-tuple-element.33.rest_0_, bf16[72,1024]{1,0:T(8,128)(2,1)S(1)} %collective-permute-done.6.rest_1_, ...), custom_call_target="tpu_custom_call" | custom-call | tf_op jit(solution)/shard_map/combine/pallas_call | solution.py:321
  100.1 28.2 %reduce-scatter.2.cloned.1.call-done = bf16[1280,128]{1,0:T(8,128)(2,1)} async-done(((bf16[15360,128]{1,0:T(8,128)(2,1)}), bf16[1280,128]{1,0:T(8,128)(2,1)}) %reduce-scatter.2.cloned.1.call-update) | async-done | bytes 327696 | tf_op jit(solution)/shard_map/reduce_scatter | solution.py:294
  128.3 19.5 %all_to_all.15 = bf16[16,80,128]{2,1,0:T(8,128)(2,1)S(1)} all-to-all(bf16[16,80,128]{2,1,0:T(8,128)(2,1)} %bitcast.48), channel_id=1, replica_groups=mesh['y'=4,'z'=12,'node'=4,'local'=4] {'node','y'}, dimensions={0} | all-to-all | bytes 655360 | tf_op jit(solution)/shard_map/all_to_all | solution.py:333
  147.9 0.8 final.1
  (25 shorter events, 0.4 us)
Async XLA Ops:
  7.2 44.2 %copy-start.2 = (bf16[1,1,4,72,1024]{4,3,2,1,0:T(8,128)(2,1)S(1)}, bf16[1,1,4,72,1024]{4,3,2,1,0:T(8,128)(2,1)}, u32[]{:S(2)}) copy-start(bf16[1,1,4,72,1024]{4,3,2,1,0:T(8,128)(2,1)} %param.14) | copy-start | bytes 1769476
  7.2 44.2 %copy-start.1 = (bf16[1,1,4,72,1024]{4,3,2,1,0:T(8,128)(2,1)S(1)}, bf16[1,1,4,72,1024]{4,3,2,1,0:T(8,128)(2,1)}, u32[]{:S(2)}) copy-start(bf16[1,1,4,72,1024]{4,3,2,1,0:T(8,128)(2,1)} %param.13) | copy-start | bytes 1769476
  9.9 18.8 %all-to-all-start = ((bf16[4,72,960]{2,1,0:T(8,128)(2,1)}), bf16[4,72,960]{2,1,0:T(8,128)(2,1)S(1)}, u32[]{:S(2)}, u32[]{:S(2)}) async-start(bf16[4,72,960]{2,1,0:T(8,128)(2,1)} %dispatch.1), calls=%async_computation | async-start | bytes 1179648 | tf_op jit(solution)/shard_map/all_to_all | solution.py:237
  13.4 38.8 %copy-start = (bf16[1,1,4,72,960]{4,3,2,1,0:T(8,128)(2,1)S(1)}, bf16[1,1,4,72,960]{4,3,2,1,0:T(8,128)(2,1)}, u32[]{:S(2)}) copy-start(bf16[1,1,4,72,960]{4,3,2,1,0:T(8,128)(2,1)} %param.12) | copy-start | bytes 1658884
  15.4 30.1 %collective-permute-start = (bf16[144,960]{1,0:T(8,128)(2,1)}, bf16[144,960]{1,0:T(8,128)(2,1)S(1)}, u32[]{:S(2)}, u32[]{:S(2)}) collective-permute-start(bf16[144,960]{1,0:T(8,128)(2,1)} %get-tuple-element.35), channel_id=1, source_target_pairs={{0,4},{4,8},{8,12},{12,0},{1,5},{5,9},{9,13},{13,1},{2,6},{6,10},{... | collective-permute-start | bytes 829448 | tf_op jit(solution)/shard_map/ppermute | solution.py:198
  26.8 18.7 %collective-permute-start.1 = (bf16[144,960]{1,0:T(8,128)(2,1)}, bf16[144,960]{1,0:T(8,128)(2,1)S(1)}, u32[]{:S(2)}, u32[]{:S(2)}) collective-permute-start(bf16[144,960]{1,0:T(8,128)(2,1)} %get-tuple-element.34), channel_id=1, source_target_pairs={{0,12},{4,0},{8,4},{12,8},{1,13},{5,1},{9,5},{13,9},{2,14},{6,2},{... | collective-permute-start | bytes 829448 | tf_op jit(solution)/shard_map/ppermute | solution.py:198
  32.4 19.0 %all-to-all-start.1 = ((bf16[4,288,256]{2,1,0:T(8,128)(2,1)}), bf16[4,288,256]{2,1,0:T(8,128)(2,1)S(1)}, u32[]{:S(2)}, u32[]{:S(2)}) async-start(bf16[4,288,256]{2,1,0:T(8,128)(2,1)} %raw.1), calls=%async_computation.1 | async-start | bytes 1179648 | tf_op jit(solution)/shard_map/all_to_all | solution.py:256
  39.6 88.8 %reduce-scatter.2.cloned.1.call-start = ((), (), s32[]{:S(2)}) async-start(), calls=%async_computation.4 | async-start | bytes 4259840 | tf_op jit(solution)/shard_map/reduce_scatter | solution.py:294
  39.6 15.3 %collective-permute-start.4 = (bf16[144,960]{1,0:T(8,128)(2,1)}, bf16[144,960]{1,0:T(8,128)(2,1)S(1)}, u32[]{:S(2)}, u32[]{:S(2)}) collective-permute-start(bf16[144,960]{1,0:T(8,128)(2,1)} %get-tuple-element.34), channel_id=1, source_target_pairs={{0,4},{4,8},{8,12},{12,0},{1,5},{5,9},{9,13},{13,1},{2,6},{6,10},{... | collective-permute-start | bytes 829448 | tf_op jit(solution)/shard_map/ppermute | solution.py:198
  41.6 13.5 %collective-permute-start.5 = (bf16[144,960]{1,0:T(8,128)(2,1)}, bf16[144,960]{1,0:T(8,128)(2,1)}, u32[]{:S(2)}, u32[]{:S(2)}) collective-permute-start(bf16[144,960]{1,0:T(8,128)(2,1)} %get-tuple-element.35), channel_id=1, source_target_pairs={{0,12},{4,0},{8,4},{12,8},{1,13},{5,1},{9,5},{13,9},{2,14},{6,2},{... | collective-permute-start | bytes 829448 | tf_op jit(solution)/shard_map/ppermute | solution.py:198
  45.5 14.4 %collective-permute-start.2 = (bf16[144,960]{1,0:T(8,128)(2,1)S(1)}, bf16[144,960]{1,0:T(8,128)(2,1)S(1)}, u32[]{:S(2)}, u32[]{:S(2)}) collective-permute-start(bf16[144,960]{1,0:T(8,128)(2,1)S(1)} %collective-permute-done.refs_0_), channel_id=1, source_target_pairs={{0,4},{4,8},{8,12},{12,0},{1,5},{5,9},{9,13},{13,1},{2,6},{6,10},{... | collective-permute-start | bytes 829448 | tf_op jit(solution)/shard_map/ppermute | solution.py:198
  48.7 11.9 %collective-permute-start.3 = (bf16[144,960]{1,0:T(8,128)(2,1)S(1)}, bf16[144,960]{1,0:T(8,128)(2,1)}, u32[]{:S(2)}, u32[]{:S(2)}) collective-permute-start(bf16[144,960]{1,0:T(8,128)(2,1)S(1)} %collective-permute-done.1.refs_3_), channel_id=1, source_target_pairs={{0,12},{4,0},{8,4},{12,8},{1,13},{5,1},{9,5},{13,9},{2,14},{6,2},{... | collective-permute-start | bytes 829448 | tf_op jit(solution)/shard_map/ppermute | solution.py:198
  52.2 6.1 %copy-start.5 = (bf16[288,256]{1,0:T(8,128)(2,1)}, bf16[288,256]{1,0:T(8,128)(2,1)S(1)}, u32[]{:S(2)}) copy-start(bf16[288,256]{1,0:T(8,128)(2,1)S(1)} %get-tuple-element.22) | copy-start | bytes 442372
  63.3 0.9 copy-start.6
  64.2 33.7 %copy-start.7 = (s32[128,2]{0,1:T(2,128)S(1)}, s32[128,2]{0,1:T(2,128)}, u32[]{:S(2)}) copy-start(s32[128,2]{0,1:T(2,128)} %param.10) | copy-start | bytes 3076
  64.2 33.7 %copy-start.8 = (bf16[128,2]{0,1:T(2,128)(2,1)S(1)}, bf16[128,2]{0,1:T(2,128)(2,1)}, u32[]{:S(2)}) copy-start(bf16[128,2]{0,1:T(2,128)(2,1)} %param.11) | copy-start | bytes 1540
  77.9 1.6 %copy-start.3 = (bf16[1,960,1024]{2,1,0:T(8,128)(2,1)S(1)}, bf16[1,960,1024]{2,1,0:T(8,128)(2,1)}, u32[]{:S(2)}) copy-start(bf16[1,960,1024]{2,1,0:T(8,128)(2,1)} %param.15) | copy-start | bytes 5898244
  79.5 1.5 copy-start.4
  84.9 7.6 %collective-permute-start.6 = (bf16[72,1024]{1,0:T(8,128)(2,1)S(1)}, bf16[72,1024]{1,0:T(8,128)(2,1)S(1)}, u32[]{:S(2)}, u32[]{:S(2)}) collective-permute-start(bf16[72,1024]{1,0:T(8,128)(2,1)S(1)} %get-tuple-element.32), channel_id=1, source_target_pairs={{0,1},{1,0},{2,3},{3,2},{4,5},{5,4},{6,7},{7,6},{8,9},{9,8},{10,11... | collective-permute-start | bytes 442376 | tf_op jit(solution)/shard_map/ppermute | solution.py:318
  86.8 8.1 %collective-permute-start.7 = (bf16[72,1024]{1,0:T(8,128)(2,1)S(1)}, bf16[72,1024]{1,0:T(8,128)(2,1)S(1)}, u32[]{:S(2)}, u32[]{:S(2)}) collective-permute-start(bf16[72,1024]{1,0:T(8,128)(2,1)S(1)} %get-tuple-element.31), channel_id=1, source_target_pairs={{0,2},{1,3},{2,0},{3,1},{4,6},{5,7},{6,4},{7,5},{8,10},{9,11},{10,... | collective-permute-start | bytes 442376 | tf_op jit(solution)/shard_map/ppermute | solution.py:318
  90.2 7.7 %collective-permute-start.8 = (bf16[72,1024]{1,0:T(8,128)(2,1)S(1)}, bf16[72,1024]{1,0:T(8,128)(2,1)S(1)}, u32[]{:S(2)}, u32[]{:S(2)}) collective-permute-start(bf16[72,1024]{1,0:T(8,128)(2,1)S(1)} %get-tuple-element.30), channel_id=1, source_target_pairs={{0,3},{1,2},{2,1},{3,0},{4,7},{5,6},{6,5},{7,4},{8,11},{9,10},{10,... | collective-permute-start | bytes 442376 | tf_op jit(solution)/shard_map/ppermute | solution.py:318
Sparse Core Ops, SparseCore 0:
  63.4 64.8 reduce-scatter.1
